TPU v7x, 128 devices: a whole 4x4x4 slice. The times are simulated.
128 devices in a mesh: src: 8 (over x, z_hi), tgt: 16 (over y, z_lo, core).
Axes of the slice: x: 4, y: 4, z: 4 (z_hi: 2, z_lo: 2; z = z_hi * 2 + z_lo), core: 2. Of those that a mesh axis runs over, the one named last changes fastest.
Arguments:
- noise: bfloat16 [4096, 2048], P(('src', 'tgt')), may hold values from -6 to 6
- data: bfloat16 [4096, 2048], P(('src', 'tgt')), may hold values from -6 to 6
- t_index: int32 [4096], P(('src', 'tgt')), may hold values from 0 to 1000
- embed_weight: bfloat16 [64, 2048], replicated, may hold values from -0.75 to 0.75
- position: bfloat16 [32, 2048], replicated, may hold values from -6 to 6
- norm_gain: float32 [2048], replicated, may hold values from 0.5 to 1.5
- qkv_weight: bfloat16 [2048, 6144], P(None, 'tgt'), may hold values from -0.125 to 0.125
Outputs:
- velocity: bfloat16 [4096, 2048], P(('src', 'tgt'))
- qkv: bfloat16 [131072, 6144], P(('src', 'tgt'))
All inputs are finite; a program needn't handle non-finite values.
Results may differ from a plain program's by a relative error of at most 0.014.
Values may be sent and summed in bfloat16 or wider, within the bound.
No kernel may reach another device: no remote copies, remote signals or barrier semaphores. Data moves between devices by JAX's collectives and lax.ppermute only.
A program may use at most 448 MiB of HBM per device.

v0:
```python
import jax
import jax.numpy as jnp
from jax import lax
from jax.sharding import PartitionSpec as P

ITERS = 3
TGRID = 1000


def joined(value, axis, join):
    pieces = jax.tree.map(lambda part: lax.all_gather(part, axis), value)
    head = jax.tree.map(lambda part: part[0], pieces)
    tail = jax.tree.map(lambda part: part[1:], pieces)
    total, _ = lax.scan(lambda total, share: (join(total, share), None), head, tail)
    return total


def combine_lse(first, second):
    highest = jnp.maximum(first[0], second[0])
    return (
        highest,
        first[1] * jnp.exp(first[0] - highest) + second[1] * jnp.exp(second[0] - highest),
    )


def row_potential(scores, epsilon):
    local_peak = jnp.max(scores, axis=1)
    local_total = jnp.sum(jnp.exp(scores - local_peak[:, None]), axis=1)
    peak_all, total_all = joined((local_peak, local_total), "tgt", combine_lse)
    return -epsilon * (peak_all + jnp.log(total_all))


def col_potential(scores, epsilon):
    local_peak = jnp.max(scores, axis=0)
    local_total = jnp.sum(jnp.exp(scores - local_peak[None, :]), axis=0)
    peak_all, total_all = joined((local_peak, local_total), "src", combine_lse)
    return -epsilon * (peak_all + jnp.log(total_all))


def embed_rows(samples, embed_weight, position, norm_gain):
    count = samples.shape[0]
    patch_count = position.shape[0]
    patch_in = embed_weight.shape[0]
    width = embed_weight.shape[1]
    patches = samples.reshape(count * patch_count, patch_in)
    embedded = jnp.dot(patches, embed_weight, preferred_element_type=jnp.float32).reshape(
        count, patch_count, width
    )
    embedded = embedded + position.astype(jnp.float32)[None]
    meansq = jnp.mean(embedded * embedded, axis=-1, keepdims=True)
    normed = (embedded * lax.rsqrt(meansq + 1e-06) * norm_gain).astype(jnp.bfloat16)
    return normed.reshape(count * patch_count, width)


def local(noise, data, t_index, embed_weight, position, norm_gain, qkv_weight):
    latent = noise.shape[1]
    own_rows = noise.shape[0]
    noise_block = lax.all_gather(noise, "tgt", axis=0, tiled=True)
    data_block = lax.all_gather(data, "src", axis=0, tiled=True)
    noise_sq = jnp.sum(jnp.square(noise_block.astype(jnp.float32)), axis=1)
    data_sq = jnp.sum(jnp.square(data_block.astype(jnp.float32)), axis=1)
    cross_term = lax.dot_general(
        noise_block, data_block, (((1,), (1,)), ((), ())), preferred_element_type=jnp.float32
    )
    cost = (noise_sq[:, None] + data_sq[None, :] - 2.0 * cross_term) / latent
    col_pot = jnp.zeros((data_block.shape[0],), jnp.float32)
    row_pot = jnp.zeros((noise_block.shape[0],), jnp.float32)
    epsilon = 0.04
    for step in range(ITERS):
        epsilon = 0.04 * 0.45**step
        row_pot = row_potential((col_pot[None, :] - cost) / epsilon, epsilon)
        col_pot = col_potential((row_pot[:, None] - cost) / epsilon, epsilon)
    scores = (col_pot[None, :] - cost) / epsilon
    offset = lax.axis_index("tgt") * own_rows
    local_peak = jnp.max(scores, axis=1)
    local_total = jnp.sum(jnp.exp(scores - local_peak[:, None]), axis=1)
    peak_all, denom = joined((local_peak, local_total), "tgt", combine_lse)
    coupling = jnp.exp(scores - peak_all[:, None]).astype(jnp.bfloat16)
    partial_sum = jnp.dot(coupling, data_block, preferred_element_type=jnp.float32)
    numer = lax.psum_scatter(
        partial_sum.astype(jnp.bfloat16), "tgt", scatter_dimension=0, tiled=True
    ).astype(jnp.float32)
    own_denom = lax.dynamic_slice_in_dim(denom, offset, own_rows, 0)
    target = numer / own_denom[:, None]
    noise_own = noise.astype(jnp.float32)
    velocity = (target - noise_own).astype(jnp.bfloat16)
    times = t_index.astype(jnp.float32) / TGRID
    mixed = ((1.0 - times)[:, None] * noise_own + times[:, None] * target).astype(jnp.bfloat16)
    normed = embed_rows(mixed, embed_weight, position, norm_gain)
    qkv = jnp.dot(
        normed,
        lax.all_gather(qkv_weight, "tgt", axis=1, tiled=True),
        preferred_element_type=jnp.float32,
    ).astype(jnp.bfloat16)
    return (velocity, qkv)


def solution(mesh):
    return jax.shard_map(
        local,
        mesh=mesh,
        in_specs=(
            P(("src", "tgt"), None),
            P(("src", "tgt"), None),
            P(("src", "tgt")),
            P(),
            P(),
            P(),
            P(None, "tgt"),
        ),
        out_specs=(P(("src", "tgt"), None), P(("src", "tgt"), None)),
        check_vma=False,
    )
```

profile of v0, /device:TPU:1, one launch (start us, length us, event | category | flops | bytes accessed | tf_op | source)
XLA Modules:
  0.0 597.8 jit_solution(4102030687520857336)
XLA Ops:
  7.2 0.7 all-gather.34.cloned.1.call-update
  8.0 0.7 all-gather.32.cloned.1.call-update
  8.7 51.4 %all-gather.34.cloned.1.call-done = bf16[256,2048]{1,0:T(8,128)(2,1)} async-done(((bf16[32,2048]{1,0:T(8,128)(2,1)}), bf16[256,2048]{1,0:T(8,128)(2,1)}) %all-gather.34.cloned.1.call-update) | async-done | bytes 1048592 | tf_op jit(solution)/shard_map/all_gather | solution.py:59
  60.1 1.5 multiply_reduce_fusion.2
  61.6 34.1 %all-gather.32.cloned.1.call-done = bf16[512,2048]{1,0:T(8,128)(2,1)} async-done(((bf16[32,2048]{1,0:T(8,128)(2,1)}), bf16[512,2048]{1,0:T(8,128)(2,1)}) %all-gather.32.cloned.1.call-update) | async-done | bytes 2097168 | tf_op jit(solution)/shard_map/all_gather | solution.py:58
  95.7 2.1 multiply_reduce_fusion.1
  97.7 2.7 fusion.2
  100.5 0.1 exponential_reduce_fusion.6
  100.6 18.1 %all-gather.15 = f32[16,1,512]{2,1,0:T(1,128)S(1)} all-gather(f32[1,1,512]{2,1,0:T(1,128)S(1)} %bitcast.176), channel_id=3, replica_groups=mesh['src'=8,'tgt'=16] {'tgt'}, dimensions={0}, use_global_device_ids=true | all-gather | bytes 34816 | tf_op jit(solution)/shard_map/all_gather | solution.py:11
  118.8 16.3 %all-gather.14 = f32[16,1,512]{2,1,0:T(1,128)S(1)} all-gather(f32[1,1,512]{2,1,0:T(1,128)S(1)} %bitcast.173), channel_id=2, replica_groups=mesh['src'=8,'tgt'=16] {'tgt'}, dimensions={0}, use_global_device_ids=true | all-gather | bytes 34816 | tf_op jit(solution)/shard_map/all_gather | solution.py:11
  135.1 0.8 while.84
  136.1 0.2 exponential_reduce_fusion.5
  136.3 19.5 %all-gather.16 = f32[8,1,256]{2,1,0:T(1,128)S(1)} all-gather(f32[1,1,256]{2,1,0:T(1,128)S(1)} %bitcast.170), channel_id=4, replica_groups=mesh['src'=8,'tgt'=16] {'src'}, dimensions={0}, use_global_device_ids=true | all-gather | bytes 9216 | tf_op jit(solution)/shard_map/all_gather | solution.py:11
  155.8 14.6 %all-gather.17 = f32[8,1,256]{2,1,0:T(1,128)S(1)} all-gather(f32[1,1,256]{2,1,0:T(1,128)S(1)} %bitcast.178), channel_id=5, replica_groups=mesh['src'=8,'tgt'=16] {'src'}, dimensions={0}, use_global_device_ids=true | all-gather | bytes 9216 | tf_op jit(solution)/shard_map/all_gather | solution.py:11
  170.4 0.3 while.85
  170.8 0.1 fusion.4
  170.9 0.2 exponential_reduce_fusion.4
  171.1 24.3 %all-gather.19 = f32[16,1,512]{2,1,0:T(1,128)S(1)} all-gather(f32[1,1,512]{2,1,0:T(1,128)S(1)} %bitcast.174), channel_id=7, replica_groups=mesh['src'=8,'tgt'=16] {'tgt'}, dimensions={0}, use_global_device_ids=true | all-gather | bytes 34816 | tf_op jit(solution)/shard_map/all_gather | solution.py:11
  195.5 16.9 %all-gather.18 = f32[16,1,512]{2,1,0:T(1,128)S(1)} all-gather(f32[1,1,512]{2,1,0:T(1,128)S(1)} %bitcast.167), channel_id=6, replica_groups=mesh['src'=8,'tgt'=16] {'tgt'}, dimensions={0}, use_global_device_ids=true | all-gather | bytes 34816 | tf_op jit(solution)/shard_map/all_gather | solution.py:11
  212.4 0.8 while.86
  213.4 0.2 exponential_reduce_fusion.3
  213.6 17.9 %all-gather.20 = f32[8,1,256]{2,1,0:T(1,128)S(1)} all-gather(f32[1,1,256]{2,1,0:T(1,128)S(1)} %bitcast.171), channel_id=8, replica_groups=mesh['src'=8,'tgt'=16] {'src'}, dimensions={0}, use_global_device_ids=true | all-gather | bytes 9216 | tf_op jit(solution)/shard_map/all_gather | solution.py:11
  231.4 14.6 %all-gather.21 = f32[8,1,256]{2,1,0:T(1,128)S(1)} all-gather(f32[1,1,256]{2,1,0:T(1,128)S(1)} %bitcast.179), channel_id=9, replica_groups=mesh['src'=8,'tgt'=16] {'src'}, dimensions={0}, use_global_device_ids=true | all-gather | bytes 9216 | tf_op jit(solution)/shard_map/all_gather | solution.py:11
  246.1 0.3 while.87
  246.4 0.1 fusion.6
  246.6 0.2 exponential_reduce_fusion.2
  246.8 24.3 %all-gather.23 = f32[16,1,512]{2,1,0:T(1,128)S(1)} all-gather(f32[1,1,512]{2,1,0:T(1,128)S(1)} %bitcast.175), channel_id=11, replica_groups=mesh['src'=8,'tgt'=16] {'tgt'}, dimensions={0}, use_global_device_ids=true | all-gather | bytes 34816 | tf_op jit(solution)/shard_map/all_gather | solution.py:11
  271.1 16.9 %all-gather.22 = f32[16,1,512]{2,1,0:T(1,128)S(1)} all-gather(f32[1,1,512]{2,1,0:T(1,128)S(1)} %bitcast.168), channel_id=10, replica_groups=mesh['src'=8,'tgt'=16] {'tgt'}, dimensions={0}, use_global_device_ids=true | all-gather | bytes 34816 | tf_op jit(solution)/shard_map/all_gather | solution.py:11
  288.0 0.8 while.88
  289.0 0.2 exponential_reduce_fusion.1
  289.2 17.9 %all-gather.24 = f32[8,1,256]{2,1,0:T(1,128)S(1)} all-gather(f32[1,1,256]{2,1,0:T(1,128)S(1)} %bitcast.172), channel_id=12, replica_groups=mesh['src'=8,'tgt'=16] {'src'}, dimensions={0}, use_global_device_ids=true | all-gather | bytes 9216 | tf_op jit(solution)/shard_map/all_gather | solution.py:11
  307.1 14.6 %all-gather.25 = f32[8,1,256]{2,1,0:T(1,128)S(1)} all-gather(f32[1,1,256]{2,1,0:T(1,128)S(1)} %bitcast.180), channel_id=13, replica_groups=mesh['src'=8,'tgt'=16] {'src'}, dimensions={0}, use_global_device_ids=true | all-gather | bytes 9216 | tf_op jit(solution)/shard_map/all_gather | solution.py:11
  321.7 0.3 while.89
  322.1 0.1 fusion.8
  322.2 0.2 exponential_reduce_fusion
  322.4 24.3 %all-gather.27 = f32[16,1,512]{2,1,0:T(1,128)S(1)} all-gather(f32[1,1,512]{2,1,0:T(1,128)S(1)} %bitcast.177), channel_id=15, replica_groups=mesh['src'=8,'tgt'=16] {'tgt'}, dimensions={0}, use_global_device_ids=true | all-gather | bytes 34816 | tf_op jit(solution)/shard_map/all_gather | solution.py:11
  346.7 16.9 %all-gather.26 = f32[16,1,512]{2,1,0:T(1,128)S(1)} all-gather(f32[1,1,512]{2,1,0:T(1,128)S(1)} %bitcast.169), channel_id=14, replica_groups=mesh['src'=8,'tgt'=16] {'tgt'}, dimensions={0}, use_global_device_ids=true | all-gather | bytes 34816 | tf_op jit(solution)/shard_map/all_gather | solution.py:11
  363.7 0.8 while.90
  364.5 2.2 convolution_convert_fusion.1
  366.7 0.2 all-gather.36.cloned.1.call-start
  367.0 0.3 all-gather.36.cloned.1.call-update
  367.5 56.1 %reduce-scatter.2.cloned.1.call-done = bf16[32,2048]{1,0:T(8,128)(2,1)} async-done(((bf16[512,2048]{1,0:T(8,128)(2,1)}), bf16[32,2048]{1,0:T(8,128)(2,1)}) %reduce-scatter.2.cloned.1.call-update) | async-done | bytes 131088 | tf_op jit(solution)/shard_map/reduce_scatter | solution.py:80
  423.6 1.7 fusion.11
  425.3 0.2 dot_general.16
  425.6 1.3 multiply_reduce_fusion
  426.9 3.0 multiply_convert_fusion
  430.0 129.0 %all-gather.36.cloned.1.call-done = bf16[2048,6144]{1,0:T(8,128)(2,1)} async-done(((bf16[2048,384]{1,0:T(8,128)(2,1)}), bf16[2048,6144]{1,0:T(8,128)(2,1)}) %all-gather.36.cloned.1.call-update) | async-done | bytes 25165840 | tf_op jit(solution)/shard_map/all_gather | solution.py:92
  558.9 32.3 %convolution_convert_fusion = bf16[1024,6144]{1,0:T(8,128)(2,1)} fusion(bf16[1024,2048]{1,0:T(8,128)(2,1)} %bitcast.124, bf16[2048,6144]{1,0:T(8,128)(2,1)} %all-gather.36.cloned.1.call-done), kind=kOutput, calls=%fused_computation.21 | convolution fusion | flops 25776095232 | bytes 41943040 | tf_op jit(solution)/shard_map/dot_general | solution.py:90
  (233 shorter events, 3.4 us)
Async XLA Ops:
  7.2 418.4 %copy-start = (bf16[64,2048]{1,0:T(8,128)(2,1)S(1)}, bf16[64,2048]{1,0:T(8,128)(2,1)}, u32[]{:S(2)}) copy-start(bf16[64,2048]{1,0:T(8,128)(2,1)} %param.24) | copy-start | bytes 786436
  7.2 52.9 %all-gather.34.cloned.1.call-start = ((), (), s32[]{:S(2)}) async-start(), calls=%async_computation.2 | async-start | bytes 1179648 | tf_op jit(solution)/shard_map/all_gather | solution.py:59
  7.9 87.7 %all-gather.32.cloned.1.call-start = ((), (), s32[]{:S(2)}) async-start(), calls=%async_computation.1 | async-start | bytes 2228224 | tf_op jit(solution)/shard_map/all_gather | solution.py:58
  8.7 414.9 %reduce-scatter.2.cloned.1.call-start = ((), (), s32[]{:S(2)}) async-start(), calls=%async_computation.3 | async-start | bytes 2228224 | tf_op jit(solution)/shard_map/reduce_scatter | solution.py:80
  97.7 266.8 %copy-start.1 = (bf16[256,2048]{1,0:T(8,128)(2,1)S(1)}, bf16[256,2048]{1,0:T(8,128)(2,1)}, u32[]{:S(2)}) copy-start(bf16[256,2048]{1,0:T(8,128)(2,1)} %all-gather.34.cloned.1.call-done) | copy-start | bytes 3145732
  135.9 231.4 %copy-start.3 = (bf16[32,2048]{1,0:T(8,128)(2,1)S(1)}, bf16[32,2048]{1,0:T(8,128)(2,1)}, u32[]{:S(2)}) copy-start(bf16[32,2048]{1,0:T(8,128)(2,1)} %param.25) | copy-start | bytes 393220
  135.9 231.4 %copy-start.5 = (s32[32]{0:T(128)S(1)}, s32[32]{0:T(128)}, u32[]{:S(2)}) copy-start(s32[32]{0:T(128)} %param.23) | copy-start | bytes 388
  135.9 287.7 %copy-start.2 = (bf16[32,2048]{1,0:T(8,128)(2,1)S(1)}, bf16[32,2048]{1,0:T(8,128)(2,1)}, u32[]{:S(2)}) copy-start(bf16[32,2048]{1,0:T(8,128)(2,1)} %param.21) | copy-start | bytes 393220
  364.5 62.4 %copy-start.4 = (f32[2048]{0:T(1024)S(1)}, f32[2048]{0:T(1024)}, u32[]{:S(2)}) copy-start(f32[2048]{0:T(1024)} %param.26) | copy-start | bytes 24580
  366.7 192.2 %all-gather.36.cloned.1.call-start = ((), (), s32[]{:S(2)}) async-start(), calls=%async_computation.4 | async-start | bytes 26738688 | tf_op jit(solution)/shard_map/all_gather | solution.py:92
Sparse Core Ops, SparseCore 0:
  10.4 49.6 all-gather.33
  61.8 33.8 all-gather.31
  366.9 56.7 reduce-scatter.1
  425.1 133.7 all-gather.35
where the time goes:
time: 598 us
  waiting for transfers between devices  272 us (45%)
  blocking collectives  257 us (43%)
  matrix products  38.6 us (6%)
  between operations  14.1 us (2%)
  other arithmetic  12.3 us (2%)
    all_gather x14, blocking collectives, joined(): pieces = jax.tree.map(lambda part: lax.all_gather(part, axis), value)  257 us
    all_gather x1, waiting for transfers between devices, local(): lax.all_gather(qkv_weight, 'tgt', axis=1, tiled=True)  129 us
    reduce_scatter x1, waiting for transfers between devices, local(): lax.psum_scatter(partial_sum.astype(jnp.bfloat16), 'tgt', scatter_dimensi...  56.1 us
    all_gather x1, waiting for transfers between devices, local(): data_block = lax.all_gather(data, 'src', axis=0, tiled=True)  51.4 us
    all_gather x1, waiting for transfers between devices, local(): noise_block = lax.all_gather(noise, 'tgt', axis=0, tiled=True)  34.1 us
    dot_general x1, matrix products, local(): jnp.dot(normed, lax.all_gather(qkv_weight, 'tgt', axis=1, tiled=True), pr...  32.3 us
  transfers between devices with their start and end apart: 4, of which 4 were waited for; matrix products, arithmetic and copies ran while one was open for 1% of the time, Pallas kernels for 0%

commit v1 on v0

v1 whole, which is shorter than its diff:
```python
import jax
import jax.numpy as jnp
from jax import lax
from jax.sharding import PartitionSpec as P

ITERS = 3
TGRID = 1000


def shared(value, axis, count):
    spread = lax.optimization_barrier(jnp.broadcast_to(value[None], (count,) + value.shape))
    return lax.all_to_all(spread, axis, 0, 0)


def lse(scores, dim):
    peak = jnp.max(scores, axis=dim, keepdims=True)
    total = jnp.sum(jnp.exp(scores - peak), axis=dim)
    return jnp.squeeze(peak, dim) + jnp.log(total)


def halves(value):
    high = value.astype(jnp.bfloat16)
    low = (value - high.astype(jnp.float32)).astype(jnp.bfloat16)
    return high, low


def folded_weights(embed_weight, position, norm_gain, qkv_weight):
    scaled = jnp.concatenate([embed_weight, position], 0).astype(jnp.float32) * norm_gain
    high, low = halves(scaled)
    both = jnp.dot(
        jnp.concatenate([high, low], 0), qkv_weight, preferred_element_type=jnp.float32
    )
    rows = scaled.shape[0]
    return jnp.concatenate(halves(both[:rows] + both[rows:]), 0)


def local(noise, data, t_index, embed_weight, position, norm_gain, qkv_weight):
    latent = noise.shape[1]
    own = noise.shape[0]
    n_src = lax.axis_size("src")
    n_tgt = lax.axis_size("tgt")
    folded = lax.all_gather(
        folded_weights(embed_weight, position, norm_gain, qkv_weight), "tgt", axis=1, tiled=True
    )
    noise_block = lax.all_gather(noise, "tgt", axis=0, tiled=True)
    data_block = lax.all_gather(data, "src", axis=0, tiled=True)
    noise_sq = jnp.sum(jnp.square(noise_block.astype(jnp.float32)), axis=1)
    data_sq = jnp.sum(jnp.square(data_block.astype(jnp.float32)), axis=1)
    cross_term = lax.dot_general(
        noise_block, data_block, (((1,), (1,)), ((), ())), preferred_element_type=jnp.float32
    )
    cost = (noise_sq[:, None] + data_sq[None, :] - 2.0 * cross_term) / latent
    col_pot = jnp.zeros((data_block.shape[0],), jnp.float32)
    epsilon = 0.04
    for step in range(ITERS):
        epsilon = 0.04 * 0.45**step
        part = lse((col_pot[None, :] - cost) / epsilon, 1)
        row_pot = -epsilon * lse(shared(part, "tgt", n_tgt), 0)
        part = lse((row_pot[:, None] - cost) / epsilon, 0)
        col_pot = -epsilon * lse(shared(part, "src", n_src), 0)
    scores = (col_pot[None, :] - cost) / epsilon
    total = lse(shared(lse(scores, 1), "tgt", n_tgt), 0)
    coupling = jnp.exp(scores - total[:, None]).astype(jnp.bfloat16)
    partial_sum = jnp.dot(coupling, data_block, preferred_element_type=jnp.float32)
    pieces = lax.all_to_all(
        partial_sum.astype(jnp.bfloat16).reshape(n_tgt, own, latent), "tgt", 0, 0
    )
    target = jnp.sum(pieces.astype(jnp.float32), axis=0)
    noise_own = noise.astype(jnp.float32)
    velocity = (target - noise_own).astype(jnp.bfloat16)
    times = t_index.astype(jnp.float32) / TGRID
    mixed = ((1.0 - times)[:, None] * noise_own + times[:, None] * target).astype(jnp.bfloat16)

    patch_in, width = embed_weight.shape
    patch_count = position.shape[0]
    patches = mixed.reshape(own * patch_count, patch_in)
    embedded = jnp.dot(patches, embed_weight, preferred_element_type=jnp.float32)
    embedded = embedded.reshape(own, patch_count, width) + position.astype(jnp.float32)[None]
    scale = lax.rsqrt(jnp.mean(embedded * embedded, axis=-1) + 1e-06).reshape(own * patch_count)
    place = jnp.tile(jnp.eye(patch_count, dtype=jnp.bfloat16), (own, 1))
    tokens = jnp.concatenate([patches, place, patches, place], 1)
    qkv = jnp.dot(tokens, folded, preferred_element_type=jnp.float32) * scale[:, None]
    return (velocity, qkv.astype(jnp.bfloat16))


def solution(mesh):
    return jax.shard_map(
        local,
        mesh=mesh,
        in_specs=(
            P(("src", "tgt"), None),
            P(("src", "tgt"), None),
            P(("src", "tgt")),
            P(),
            P(),
            P(),
            P(None, "tgt"),
        ),
        out_specs=(P(("src", "tgt"), None), P(("src", "tgt"), None)),
        check_vma=False,
    )
```

time: 598 us -> 237 us (0.40)
  blocking collectives: 257 us -> 32.3 us
  waiting for transfers between devices: 272 us -> 136 us
  matrix products: 38.6 us -> 15.3 us
  starting transfers between devices: 0.34 us -> 21.4 us
    all_gather x14 -> x0, blocking collectives: 257 us -> none  [joined(): pieces = jax.tree.map(lambda part: lax.all_gather(part, axis), value)]
    all_gather x1, waiting for transfers between devices: 129 us -> 0.01 us  [local(): lax.all_gather(folded_weights(embed_weight, position, norm_gain, qkv_weig...]
    reduce_scatter x1 -> x0, waiting for transfers between devices: 56.1 us -> none  [local(): lax.psum_scatter(partial_sum.astype(jnp.bfloat16), 'tgt', scatter_dimensi...]
    all_to_all x0 -> x5, waiting for transfers between devices: none -> 49.1 us  [the longest x1 30.6 us: local(): lax.all_to_all(partial_sum.astype(jnp.bfloat16).reshape(n_tgt, own, laten...]
    all_to_all x0 -> x3, blocking collectives: none -> 32.3 us  [shared(): return lax.all_to_all(spread, axis, 0, 0)]
    dot_general x2 -> x3, matrix products: 33.6 us -> 12.2 us  [the longest x1 8.46 us: local(): jnp.dot(tokens, folded, preferred_element_type=jnp.float32) * scale[:, None]]
    all_to_all x0 -> x5, starting transfers between devices: none -> 21.3 us  [the longest x4 16.6 us: shared(): return lax.all_to_all(spread, axis, 0, 0)]
  transfers between devices with their start and end apart: 4 -> 8, of which waited for: 4 -> 7; matrix products, arithmetic and copies ran while one was open for 1% -> 6% of each run, Pallas kernels for 0% -> 0%
where the time goes in v1:
time: 237 us; the launch traced here: 235 us
  waiting for transfers between devices  136 us (57%)
  blocking collectives  32.3 us (14%)
  starting transfers between devices  21.4 us (9%)
  matrix products  15.3 us (6%)
  between operations  14.1 us (6%)
  other arithmetic  12.9 us (5%)
  local copies, waits for them, and re-layouts  3.21 us (1%)
    all_gather x1, waiting for transfers between devices, local(): data_block = lax.all_gather(data, 'src', axis=0, tiled=True)  51.4 us
    all_gather x1, waiting for transfers between devices, local(): noise_block = lax.all_gather(noise, 'tgt', axis=0, tiled=True)  34 us
    all_to_all x3, blocking collectives, shared(): return lax.all_to_all(spread, axis, 0, 0)  32.3 us
    all_to_all x1, waiting for transfers between devices, local(): lax.all_to_all(partial_sum.astype(jnp.bfloat16).reshape(n_tgt, own, laten...  30.6 us
    all_to_all x4, waiting for transfers between devices, shared(): return lax.all_to_all(spread, axis, 0, 0)  18.5 us
    all_to_all x4, starting transfers between devices, shared(): return lax.all_to_all(spread, axis, 0, 0)  16.6 us
    dot_general x1, matrix products, local(): jnp.dot(tokens, folded, preferred_element_type=jnp.float32) * scale[:, None]  8.46 us
  transfers between devices with their start and end apart: 8, of which 7 were waited for; matrix products, arithmetic and copies ran while one was open for 6% of the time, Pallas kernels for 0%

profile of v1, /device:TPU:1, one launch (start us, length us, event | category | flops | bytes accessed | tf_op | source)
XLA Modules:
  0.0 235.2 jit_solution(10667740617140354199)
XLA Ops:
  7.2 0.7 all-gather.6.cloned.1.call-update
  8.0 0.7 all-gather.4.cloned.1.call-update
  8.7 51.4 %all-gather.6.cloned.1.call-done = bf16[256,2048]{1,0:T(8,128)(2,1)} async-done(((bf16[32,2048]{1,0:T(8,128)(2,1)}), bf16[256,2048]{1,0:T(8,128)(2,1)}) %all-gather.6.cloned.1.call-update) | async-done | bytes 1048592 | tf_op jit(solution)/shard_map/all_gather | solution.py:46
  60.1 1.6 multiply_reduce_fusion.2
  61.7 34.0 %all-gather.4.cloned.1.call-done = bf16[512,2048]{1,0:T(8,128)(2,1)} async-done(((bf16[32,2048]{1,0:T(8,128)(2,1)}), bf16[512,2048]{1,0:T(8,128)(2,1)}) %all-gather.4.cloned.1.call-update) | async-done | bytes 2097168 | tf_op jit(solution)/shard_map/all_gather | solution.py:45
  95.7 2.2 multiply_reduce_fusion.1
  97.9 0.9 fusion.14
  98.9 0.1 exponential_reduce_fusion.6
  99.1 10.1 %all_to_all.89 = f32[16,1,512]{2,1,0:T(1,128)S(1)} all-to-all(f32[16,1,512]{2,1,0:T(1,128)S(1)} %all_to_all.59), channel_id=1, replica_groups=mesh['src'=8,'tgt'=16] {'tgt'}, dimensions={0} | all-to-all | bytes 65536 | tf_op jit(solution)/shard_map/all_to_all | solution.py:12
  109.2 0.1 fusion.15
  109.4 0.2 exponential_reduce_fusion.5
  109.6 12.4 %all_to_all.90 = f32[8,1,256]{2,1,0:T(1,128)S(1)} all-to-all(f32[8,1,256]{2,1,0:T(1,128)S(1)} %all_to_all.62), channel_id=1, replica_groups=mesh['src'=8,'tgt'=16] {'src'}, dimensions={0} | all-to-all | bytes 16384 | tf_op jit(solution)/shard_map/all_to_all | solution.py:12
  122.1 0.1 fusion.16
  122.2 0.2 exponential_reduce_fusion.4
  122.5 0.6 all_to_all.65
  123.1 5.1 %all-to-all-start.2 = ((f32[16,1,512]{2,1,0:T(1,128)}), f32[16,1,512]{2,1,0:T(1,128)S(1)}, u32[]{:S(2)}, u32[]{:S(2)}) async-start(f32[16,1,512]{2,1,0:T(1,128)} %all_to_all.65), calls=%async_computation.2 | async-start | bytes 65536 | tf_op jit(solution)/shard_map/all_to_all | solution.py:12
  128.2 2.0 fusion.6
  130.2 3.9 %all-to-all-done.2 = f32[16,1,512]{2,1,0:T(1,128)S(1)} async-done(((f32[16,1,512]{2,1,0:T(1,128)}), f32[16,1,512]{2,1,0:T(1,128)S(1)}, u32[]{:S(2)}, u32[]{:S(2)}) %all-to-all-start.2) | async-done | bytes 32800 | tf_op jit(solution)/shard_map/all_to_all | solution.py:12
  134.2 0.1 fusion.17
  134.3 0.2 exponential_reduce_fusion.3
  134.6 0.6 all_to_all.68
  135.2 3.3 %all-to-all-start.3 = ((f32[8,1,256]{2,1,0:T(1,128)}), f32[8,1,256]{2,1,0:T(1,128)S(1)}, u32[]{:S(2)}, u32[]{:S(2)}) async-start(f32[8,1,256]{2,1,0:T(1,128)} %all_to_all.68), calls=%async_computation.3 | async-start | bytes 16384 | tf_op jit(solution)/shard_map/all_to_all | solution.py:12
  138.5 2.4 %fusion.2 = f32[192,384]{1,0:T(8,128)} fusion(bf16[2048,384]{1,0:T(8,128)(2,1)S(1)} %copy-done, bf16[96,2048]{1,0:T(8,128)(2,1)} %get-tuple-element.5, bf16[96,2048]{1,0:T(8,128)(2,1)} %get-tuple-element.4), kind=kOutput, calls=%fused_computation.9 | convolution fusion | flops 303562752 | bytes 2654208 | tf_op jit(solution)/shard_map/dot_general | solution.py:30
  140.9 4.0 %all-to-all-done.3 = f32[8,1,256]{2,1,0:T(1,128)S(1)} async-done(((f32[8,1,256]{2,1,0:T(1,128)}), f32[8,1,256]{2,1,0:T(1,128)S(1)}, u32[]{:S(2)}, u32[]{:S(2)}) %all-to-all-start.3) | async-done | bytes 8224 | tf_op jit(solution)/shard_map/all_to_all | solution.py:12
  145.0 0.1 fusion.18
  145.2 0.2 exponential_reduce_fusion.2
  145.4 0.6 all_to_all.71
  146.0 4.8 %all-to-all-start.4 = ((f32[16,1,512]{2,1,0:T(1,128)}), f32[16,1,512]{2,1,0:T(1,128)S(1)}, u32[]{:S(2)}, u32[]{:S(2)}) async-start(f32[16,1,512]{2,1,0:T(1,128)} %all_to_all.71), calls=%async_computation.4 | async-start | bytes 65536 | tf_op jit(solution)/shard_map/all_to_all | solution.py:12
  150.9 1.0 subtract_convert_fusion.1
  151.9 4.9 %all-to-all-done.4 = f32[16,1,512]{2,1,0:T(1,128)S(1)} async-done(((f32[16,1,512]{2,1,0:T(1,128)}), f32[16,1,512]{2,1,0:T(1,128)S(1)}, u32[]{:S(2)}, u32[]{:S(2)}) %all-to-all-start.4) | async-done | bytes 32800 | tf_op jit(solution)/shard_map/all_to_all | solution.py:12
  156.8 0.1 fusion.19
  157.0 0.2 exponential_reduce_fusion.1
  157.2 0.6 all_to_all.74
  157.8 3.3 %all-to-all-start.5 = ((f32[8,1,256]{2,1,0:T(1,128)}), f32[8,1,256]{2,1,0:T(1,128)S(1)}, u32[]{:S(2)}, u32[]{:S(2)}) async-start(f32[8,1,256]{2,1,0:T(1,128)} %all_to_all.74), calls=%async_computation.5 | async-start | bytes 16384 | tf_op jit(solution)/shard_map/all_to_all | solution.py:12
  161.2 0.7 pad_maximum_fusion.1
  161.9 5.7 %all-to-all-done.5 = f32[8,1,256]{2,1,0:T(1,128)S(1)} async-done(((f32[8,1,256]{2,1,0:T(1,128)}), f32[8,1,256]{2,1,0:T(1,128)S(1)}, u32[]{:S(2)}, u32[]{:S(2)}) %all-to-all-start.5) | async-done | bytes 8224 | tf_op jit(solution)/shard_map/all_to_all | solution.py:12
  167.7 0.1 fusion.20
  167.8 0.2 exponential_reduce_fusion
  168.1 9.8 %all_to_all.91 = f32[16,1,512]{2,1,0:T(1,128)S(1)} all-to-all(f32[16,1,512]{2,1,0:T(1,128)S(1)} %all_to_all.77), channel_id=1, replica_groups=mesh['src'=8,'tgt'=16] {'tgt'}, dimensions={0} | all-to-all | bytes 65536 | tf_op jit(solution)/shard_map/all_to_all | solution.py:12
  178.0 2.2 convolution_convert_fusion
  180.2 4.7 %all-to-all-start.7 = ((bf16[16,32,2048]{2,1,0:T(8,128)(2,1)}), bf16[16,32,2048]{2,1,0:T(8,128)(2,1)}, u32[]{:S(2)}, u32[]{:S(2)}) async-start(bf16[16,32,2048]{2,1,0:T(8,128)(2,1)} %bitcast.53), calls=%async_computation.7 | async-start | bytes 4194304 | tf_op jit(solution)/shard_map/all_to_all | solution.py:65
  185.0 30.6 %all-to-all-done.7 = bf16[16,32,2048]{2,1,0:T(8,128)(2,1)} async-done(((bf16[16,32,2048]{2,1,0:T(8,128)(2,1)}), bf16[16,32,2048]{2,1,0:T(8,128)(2,1)}, u32[]{:S(2)}, u32[]{:S(2)}) %all-to-all-start.7) | async-done | bytes 2097184 | tf_op jit(solution)/shard_map/all_to_all | solution.py:65
  215.6 2.0 convert_reduce_fusion
  217.6 0.7 fusion.23
  218.3 0.2 dot_general.21
  218.5 0.2 reshape.161
  218.8 1.3 multiply_reduce_fusion
  220.2 8.5 %multiply_convert_fusion = bf16[1024,6144]{1,0:T(8,128)(2,1)} fusion(f32[1024]{0:T(1024)S(1)} %rsqrt.11, bf16[192,6144]{1,0:T(8,128)(2,1)} %all-gather.8.cloned.1.call-done, bf16[1024,32]{1,0:T(8,128)(2,1)S(1)} %bitcast.54, bf16[1024,64]{1,0:T(8,128)(2,1)S(1)} %reshape.161), kind=kOutput, calls=%fused_computation | convolution fusion | flops 2430074880 | bytes 15142912 | tf_op jit(solution)/shard_map/dot_general | solution.py:82
  (65 shorter events, 1.0 us)
Async XLA Ops:
  7.2 131.4 %copy-start = (bf16[2048,384]{1,0:T(8,128)(2,1)S(1)}, bf16[2048,384]{1,0:T(8,128)(2,1)}, u32[]{:S(2)}) copy-start(bf16[2048,384]{1,0:T(8,128)(2,1)} %param.13) | copy-start | bytes 4718596
  7.2 52.9 %all-gather.6.cloned.1.call-start = ((), (), s32[]{:S(2)}) async-start(), calls=%async_computation.9 | async-start | bytes 1179648 | tf_op jit(solution)/shard_map/all_gather | solution.py:46
  7.9 87.7 %all-gather.4.cloned.1.call-start = ((), (), s32[]{:S(2)}) async-start(), calls=%async_computation.8 | async-start | bytes 2228224 | tf_op jit(solution)/shard_map/all_gather | solution.py:45
  60.1 37.8 %copy-start.1 = (bf16[256,2048]{1,0:T(8,128)(2,1)S(1)}, bf16[256,2048]{1,0:T(8,128)(2,1)}, u32[]{:S(2)}) copy-start(bf16[256,2048]{1,0:T(8,128)(2,1)} %all-gather.6.cloned.1.call-done) | copy-start | bytes 3145732
  95.7 2.2 copy-start.2
  98.8 29.4 %copy-start.3 = (bf16[32,2048]{1,0:T(8,128)(2,1)S(1)}, bf16[32,2048]{1,0:T(8,128)(2,1)}, u32[]{:S(2)}) copy-start(bf16[32,2048]{1,0:T(8,128)(2,1)} %param.11) | copy-start | bytes 393220
  98.9 29.4 %copy-start.6 = (f32[2048]{0:T(1024)S(1)}, f32[2048]{0:T(1024)}, u32[]{:S(2)}) copy-start(f32[2048]{0:T(1024)} %param.12) | copy-start | bytes 24580
  123.1 11.0 %all-to-all-start.2 = ((f32[16,1,512]{2,1,0:T(1,128)}), f32[16,1,512]{2,1,0:T(1,128)S(1)}, u32[]{:S(2)}, u32[]{:S(2)}) async-start(f32[16,1,512]{2,1,0:T(1,128)} %all_to_all.65), calls=%async_computation.2 | async-start | bytes 65536 | tf_op jit(solution)/shard_map/all_to_all | solution.py:12
  135.2 9.8 %all-to-all-start.3 = ((f32[8,1,256]{2,1,0:T(1,128)}), f32[8,1,256]{2,1,0:T(1,128)S(1)}, u32[]{:S(2)}, u32[]{:S(2)}) async-start(f32[8,1,256]{2,1,0:T(1,128)} %all_to_all.68), calls=%async_computation.3 | async-start | bytes 16384 | tf_op jit(solution)/shard_map/all_to_all | solution.py:12
  146.0 10.7 %all-to-all-start.4 = ((f32[16,1,512]{2,1,0:T(1,128)}), f32[16,1,512]{2,1,0:T(1,128)S(1)}, u32[]{:S(2)}, u32[]{:S(2)}) async-start(f32[16,1,512]{2,1,0:T(1,128)} %all_to_all.71), calls=%async_computation.4 | async-start | bytes 65536 | tf_op jit(solution)/shard_map/all_to_all | solution.py:12
  157.8 9.8 %all-to-all-start.5 = ((f32[8,1,256]{2,1,0:T(1,128)}), f32[8,1,256]{2,1,0:T(1,128)S(1)}, u32[]{:S(2)}, u32[]{:S(2)}) async-start(f32[8,1,256]{2,1,0:T(1,128)} %all_to_all.74), calls=%async_computation.5 | async-start | bytes 16384 | tf_op jit(solution)/shard_map/all_to_all | solution.py:12
  161.2 59.0 %all-gather.8.cloned.1.call-start = ((), (), s32[]{:S(2)}) async-start(), calls=%async_computation.10 | async-start | bytes 2506752 | tf_op jit(solution)/shard_map/all_gather | solution.py:42
  180.2 4.8 %copy-start.7 = (s32[32]{0:T(128)S(1)}, s32[32]{0:T(128)}, u32[]{:S(2)}) copy-start(s32[32]{0:T(128)} %param.9) | copy-start | bytes 388
  180.2 35.4 %all-to-all-start.7 = ((bf16[16,32,2048]{2,1,0:T(8,128)(2,1)}), bf16[16,32,2048]{2,1,0:T(8,128)(2,1)}, u32[]{:S(2)}, u32[]{:S(2)}) async-start(bf16[16,32,2048]{2,1,0:T(8,128)(2,1)} %bitcast.53), calls=%async_computation.7 | async-start | bytes 4194304 | tf_op jit(solution)/shard_map/all_to_all | solution.py:65
  184.9 32.7 %copy-start.4 = (bf16[32,2048]{1,0:T(8,128)(2,1)S(1)}, bf16[32,2048]{1,0:T(8,128)(2,1)}, u32[]{:S(2)}) copy-start(bf16[32,2048]{1,0:T(8,128)(2,1)} %param.7) | copy-start | bytes 393220
  184.9 33.9 %copy-start.5 = (bf16[64,2048]{1,0:T(8,128)(2,1)S(1)}, bf16[64,2048]{1,0:T(8,128)(2,1)}, u32[]{:S(2)}) copy-start(bf16[64,2048]{1,0:T(8,128)(2,1)} %param.10) | copy-start | bytes 786436
Sparse Core Ops, SparseCore 0:
  10.4 49.6 all-gather.5
  61.8 33.8 all-gather.3
  163.7 46.1 all-gather.7

commit v2 on v1

v2 whole, which is shorter than its diff:
```python
import functools

import jax
import jax.numpy as jnp
from jax import lax
from jax.experimental import pallas as pl
from jax.experimental.pallas import tpu as pltpu
from jax.sharding import PartitionSpec as P

ITERS = 3
TGRID = 1000
BOTH = ("src", "tgt")
CORE, ZPAIR, ZFAR = 1, 2, 16 + 2
Y_STEPS = (4, 8, 12)
X_STEPS = (32, 64, 96)
QUARTERS = (1, 2, 3)
BF, F32 = jnp.bfloat16, jnp.float32


def epsilon_of(step):
    return 0.04 * 0.45**step


def swap(value, mask):
    return lax.ppermute(value, BOTH, [(i, i ^ mask) for i in range(128)])


def column_groups():
    groups = {}
    for i in range(128):
        groups.setdefault((((i >> 4) ^ (i >> 1)) & 1, i & 1), []).append(i)
    return [groups[key] for key in sorted(groups)]


def vmem_call(kernel, out_shape, scratch=(), smem=0, inputs=0, flops=0, nbytes=0):
    return pl.pallas_call(
        kernel,
        out_shape=out_shape,
        in_specs=[pl.BlockSpec(memory_space=pltpu.SMEM)] * smem
        + [pl.BlockSpec(memory_space=pltpu.VMEM)] * inputs,
        out_specs=jax.tree.map(lambda _: pl.BlockSpec(memory_space=pltpu.VMEM), out_shape),
        scratch_shapes=list(scratch),
        compiler_params=pltpu.CompilerParams(vmem_limit_bytes=48 * 1024 * 1024),
        cost_estimate=pl.CostEstimate(flops=flops, bytes_accessed=nbytes, transcendentals=0),
    )


def shape(dims, dtype=F32):
    return jax.ShapeDtypeStruct(dims, dtype)


def eye(size):
    return lax.broadcasted_iota(jnp.int32, (size, size), 0) == lax.broadcasted_iota(
        jnp.int32, (size, size), 1
    )


def to_lanes(column):
    size = column.shape[0]
    wide = jnp.broadcast_to(column, (size, size))
    return jnp.sum(jnp.where(eye(size), wide, 0.0), axis=0, keepdims=True)


def to_rows(lanes):
    size = lanes.shape[1]
    wide = jnp.broadcast_to(lanes, (size, size))
    return jnp.sum(jnp.where(eye(size), wide, 0.0), axis=1, keepdims=True)


def join_lse(parts):
    peak = functools.reduce(jnp.maximum, parts)
    total = functools.reduce(jnp.add, [jnp.exp(part - peak) for part in parts])
    return peak + jnp.log(total)


def row_stats(cost_ref, col_pot, inverse):
    tiles = cost_ref.shape[1] // 128

    def score(tile):
        part = cost_ref[:, tile * 128 : (tile + 1) * 128]
        if col_pot is None:
            return -part * inverse
        return (col_pot[tile : tile + 1, :] - part) * inverse

    peak = score(0)
    for tile in range(1, tiles):
        peak = jnp.maximum(peak, score(tile))
    peak = jnp.max(peak, axis=1, keepdims=True)
    return score, peak


def row_lse(cost_ref, col_pot, inverse):
    score, peak = row_stats(cost_ref, col_pot, inverse)
    total = jnp.exp(score(0) - peak)
    for tile in range(1, cost_ref.shape[1] // 128):
        total = total + jnp.exp(score(tile) - peak)
    return peak + jnp.log(jnp.sum(total, axis=1, keepdims=True))


def cost_kernel(place, n0, n1, n23, *refs):
    left, right = refs[:4], refs[4:8]
    data_ref, cost_ref, lse_ref, noise_ref = refs[8:]
    x, z, y, q = place[0], place[1], place[2], place[3]
    half = left[0].shape[-1]
    rows = n0.shape[0]
    noise_ref[q] = n0[...]
    noise_ref[q ^ 1] = n1[...]
    noise_ref[q ^ 2] = n23[0]
    noise_ref[q ^ 3] = n23[1]
    for a in range(4):
        for b in range(4):
            for c in range(2):
                slot = ((x ^ b) * 2 + (z ^ c)) * 4 + (y ^ a)
                data_ref[slot, :, 0:half] = left[a][b, c]
                slot = ((x ^ a) * 2 + (z ^ c)) * 4 + (y ^ b)
                data_ref[slot, :, half : 2 * half] = right[a][b, c]
    latent = 2 * half
    noise = noise_ref[...].reshape(4 * rows, latent)

    def square_sum(value):
        total = jnp.zeros((value.shape[0], 128), F32)
        for tile in range(latent // 128):
            part = value[:, tile * 128 : (tile + 1) * 128].astype(F32)
            total = total + part * part
        return jnp.sum(total, axis=1, keepdims=True)

    noise_sq = square_sum(noise)
    for group in range(4):
        part = data_ref[group * 8 : group * 8 + 8].reshape(8 * rows, latent)
        cross = lax.dot_general(
            noise, part, (((1,), (1,)), ((), ())), preferred_element_type=F32
        )
        for side in range(2):
            data_sq = to_lanes(square_sum(part[side * 128 : side * 128 + 128]))
            at = group * 256 + side * 128
            cost_ref[:, at : at + 128] = (
                noise_sq + data_sq - 2.0 * cross[:, side * 128 : side * 128 + 128]
            ) / latent
    lse = row_lse(cost_ref, None, 1.0 / epsilon_of(0))
    lse_ref[...] = jnp.broadcast_to(to_lanes(lse), lse_ref.shape)


def col_kernel(step, cost_ref, a, b, c, d, out_ref):
    epsilon = epsilon_of(step)
    joined = join_lse([a[...], b[...], c[...], d[...]])
    row_pot = to_rows(-epsilon * joined[0:1, :])
    scores = (row_pot - cost_ref[...]) * (1.0 / epsilon)
    peak = jnp.max(scores, axis=0, keepdims=True)
    lse = peak + jnp.log(jnp.sum(jnp.exp(scores - peak), axis=0, keepdims=True))
    place = lax.broadcasted_iota(jnp.int32, (8, 128), 0)
    packed = jnp.zeros((8, 128), F32)
    for tile in range(8):
        packed = jnp.where(place == tile, lse[:, tile * 128 : (tile + 1) * 128], packed)
    out_ref[...] = jnp.broadcast_to(packed[None], out_ref.shape)


def col_potential(step, parts_ref):
    parts = parts_ref[...]
    peak = jnp.max(parts, axis=0)
    total = jnp.sum(jnp.exp(parts - peak[None]), axis=0)
    return -epsilon_of(step) * (peak + jnp.log(total))


def row_kernel(step, cost_ref, parts_ref, lse_ref):
    lse = row_lse(cost_ref, col_potential(step - 1, parts_ref), 1.0 / epsilon_of(step))
    lse_ref[...] = jnp.broadcast_to(to_lanes(lse), lse_ref.shape)


def target_kernel(place, cost_ref, data_ref, parts_ref, own_ref, own_lse_ref, s1, s2, s3, coupling, sums, lses):
    q = place[3]
    col_pot = col_potential(ITERS - 1, parts_ref)
    score, peak = row_stats(cost_ref, col_pot, 1.0 / epsilon_of(ITERS - 1))
    total = jnp.zeros(cost_ref.shape[:1] + (128,), F32)
    for tile in range(8):
        expo = jnp.exp(score(tile) - peak)
        total = total + expo
        coupling[:, tile * 128 : (tile + 1) * 128] = expo.astype(BF)
    denom = jnp.sum(total, axis=1, keepdims=True)
    rows = sums.shape[1]
    lses[...] = jnp.broadcast_to(peak + jnp.log(denom), (4 * rows, 128)).reshape(4, rows, 128)
    latent = sums.shape[2]
    for at in range(0, latent, 512):
        part = data_ref[:, :, at : at + 512].reshape(-1, 512)
        product = jnp.dot(coupling[...], part, preferred_element_type=F32) / denom
        sums[:, :, at : at + 512] = product.reshape(4, rows, 512)
    own_ref[...] = sums[q]
    own_lse_ref[...] = lses[q]
    lane = lax.broadcasted_iota(jnp.int32, (rows, 128), 1)
    for mask, out in ((1, s1), (2, s2), (3, s3)):
        out[:, 0:latent] = sums[q ^ mask].astype(BF)
        value = lses[q ^ mask]
        high = value.astype(BF).astype(F32)
        middle = (value - high).astype(BF).astype(F32)
        low = value - high - middle
        out[:, latent : latent + 128] = jnp.where(
            lane == 0, high, jnp.where(lane == 1, middle, jnp.where(lane == 2, low, 0.0))
        ).astype(BF)


def halves(value):
    high = value.astype(BF)
    low = (value - high.astype(F32)).astype(BF)
    return high, low


def folded_weights(embed_weight, position, norm_gain, qkv_weight):
    scaled = jnp.concatenate([embed_weight, position], 0).astype(F32) * norm_gain
    high, low = halves(scaled)
    both = jnp.dot(jnp.concatenate([high, low], 0), qkv_weight, preferred_element_type=F32)
    rows = scaled.shape[0]
    return jnp.concatenate(halves(both[:rows] + both[rows:]), 0)


def coupled_target(noise, data, place):
    rows, latent = noise.shape
    half = latent // 2
    far = swap(data, ZFAR)
    noise_core = swap(noise, CORE)
    first = [jnp.stack([data[:, s], far[:, s]]) for s in (slice(0, half), slice(half, latent))]
    noise_pair = swap(jnp.stack([noise, noise_core]), ZPAIR)
    left = jnp.stack([first[0]] + [swap(first[0], mask) for mask in X_STEPS])
    right = jnp.stack([first[1]] + [swap(first[1], mask) for mask in Y_STEPS])
    lefts = [left] + [swap(left, mask) for mask in Y_STEPS]
    rights = [right] + [swap(right, mask) for mask in X_STEPS]
    data_all, cost, row_part = vmem_call(
        cost_kernel,
        (shape((32, rows, latent), BF), shape((4 * rows, 32 * rows)), shape((8, 128))),
        scratch=[pltpu.VMEM((4, rows, latent), BF)],
        smem=1,
        inputs=11,
        flops=2 * 4 * rows * 32 * rows * latent,
        nbytes=8 * 1024 * 1024,
    )(place, noise, noise_core, noise_pair, *lefts, *rights)
    groups = column_groups()
    for step in range(ITERS):
        parts = [row_part] + [swap(row_part, mask) for mask in QUARTERS]
        col_part = vmem_call(
            functools.partial(col_kernel, step), shape((32, 8, 128)), inputs=5, nbytes=1024 * 1024
        )(cost, *parts)
        col_parts = lax.all_to_all(
            col_part, BOTH, 0, 0, axis_index_groups=groups, tiled=True
        )
        if step + 1 < ITERS:
            row_part = vmem_call(
                functools.partial(row_kernel, step + 1),
                shape((8, 128)),
                inputs=2,
                nbytes=1024 * 1024,
            )(cost, col_parts)
    own, own_lse, *sends = vmem_call(
        target_kernel,
        (shape((rows, latent)), shape((rows, 128))) + (shape((rows, latent + 128), BF),) * 3,
        scratch=[
            pltpu.VMEM((4 * rows, 32 * rows), BF),
            pltpu.VMEM((4, rows, latent), F32),
            pltpu.VMEM((4, rows, 128), F32),
        ],
        smem=1,
        inputs=3,
        flops=2 * 4 * rows * 32 * rows * latent,
        nbytes=6 * 1024 * 1024,
    )(place, cost, data_all, col_parts)
    others = [swap(send, mask) for send, mask in zip(sends, QUARTERS)]
    logs = [own_lse[:, 0]] + [
        jnp.sum(other[:, latent : latent + 3].astype(F32), axis=1) for other in others
    ]
    total = join_lse(logs)
    target = own * jnp.exp(logs[0] - total)[:, None]
    for other, log in zip(others, logs[1:]):
        target = target + other[:, :latent].astype(F32) * jnp.exp(log - total)[:, None]
    return target


def local(noise, data, t_index, embed_weight, position, norm_gain, qkv_weight):
    own = noise.shape[0]
    src, tgt = lax.axis_index("src"), lax.axis_index("tgt")
    place = jnp.stack([src // 2, src % 2, tgt // 4, tgt % 4]).astype(jnp.int32)
    folded = lax.all_gather(
        folded_weights(embed_weight, position, norm_gain, qkv_weight), "tgt", axis=1, tiled=True
    )
    target = coupled_target(noise, data, place)
    noise_own = noise.astype(F32)
    velocity = (target - noise_own).astype(BF)
    times = t_index.astype(F32) / TGRID
    mixed = ((1.0 - times)[:, None] * noise_own + times[:, None] * target).astype(BF)

    patch_in, width = embed_weight.shape
    patch_count = position.shape[0]
    patches = mixed.reshape(own * patch_count, patch_in)
    embedded = jnp.dot(patches, embed_weight, preferred_element_type=F32)
    embedded = embedded.reshape(own, patch_count, width) + position.astype(F32)[None]
    scale = lax.rsqrt(jnp.mean(embedded * embedded, axis=-1) + 1e-06).reshape(own * patch_count)
    spots = jnp.tile(jnp.eye(patch_count, dtype=BF), (own, 1))
    tokens = jnp.concatenate([patches, spots, patches, spots], 1)
    qkv = jnp.dot(tokens, folded, preferred_element_type=F32) * scale[:, None]
    return (velocity, qkv.astype(BF))


def solution(mesh):
    return jax.shard_map(
        local,
        mesh=mesh,
        in_specs=(
            P(("src", "tgt"), None),
            P(("src", "tgt"), None),
            P(("src", "tgt")),
            P(),
            P(),
            P(),
            P(None, "tgt"),
        ),
        out_specs=(P(("src", "tgt"), None), P(("src", "tgt"), None)),
        check_vma=False,
    )
```

time: 237 us -> 189 us (0.80)
  waiting for transfers between devices: 136 us -> 57.5 us
  blocking collectives: 32.3 us -> 51 us
  starting transfers between devices: 21.4 us -> 37.9 us
  other arithmetic: 12.9 us -> 3.6 us
  Pallas kernels: 0 us -> 8.8 us
  matrix products: 15.3 us -> 10.3 us
    all_gather x2 -> x0, waiting for transfers between devices: 85.4 us -> none  [the longest x1 51.4 us: local(): data_block = lax.all_gather(data, 'src', axis=0, tiled=True)]
    ppermute x0 -> x27, waiting for transfers between devices: none -> 57.5 us  [swap(): return lax.ppermute(value, BOTH, [(i, i ^ mask) for i in range(128)])]
    all_to_all x5 -> x0, waiting for transfers between devices: 49.1 us -> none  [the longest x1 30.6 us: local(): lax.all_to_all(partial_sum.astype(jnp.bfloat16).reshape(n_tgt, own, laten...]
    ppermute x0 -> x27, starting transfers between devices: none -> 37.8 us  [swap(): return lax.ppermute(value, BOTH, [(i, i ^ mask) for i in range(128)])]
    all_to_all x5 -> x0, starting transfers between devices: 21.3 us -> none  [the longest x4 16.6 us: shared(): return lax.all_to_all(spread, axis, 0, 0)]
    all_to_all x3, blocking collectives: 32.3 us -> 51 us  [coupled_target(): lax.all_to_all(col_part, BOTH, 0, 0, axis_index_groups=groups, tiled=True)]
    pallas_call x0 -> x7, Pallas kernels: none -> 8.8 us  [the longest x1 5.86 us: coupled_target(): vmem_call(cost_kernel, (shape((32, rows, latent), BF), shape((4 * rows, 3...]
    reduce_sum x17 -> x3, other arithmetic: 7.39 us -> 0.33 us  [coupled_target(): jnp.sum(other[:, latent:latent + 3].astype(F32), axis=1)]
  transfers between devices with their start and end apart: 8 -> 28, of which waited for: 7 -> 14; matrix products, arithmetic and copies ran while one was open for 6% -> 3% of each run, Pallas kernels for 0% -> 5%
where the time goes in v2:
time: 189 us; the launch traced here: 188 us
  waiting for transfers between devices  57.5 us (30%)
  blocking collectives  51 us (27%)
  starting transfers between devices  37.9 us (20%)
  between operations  14.3 us (8%)
  matrix products  10.3 us (5%)
  Pallas kernels  8.8 us (5%)
  local copies, waits for them, and re-layouts  4.75 us (3%)
  other arithmetic  3.6 us (2%)
    ppermute x27, waiting for transfers between devices, swap(): return lax.ppermute(value, BOTH, [(i, i ^ mask) for i in range(128)])  57.5 us
    all_to_all x3, blocking collectives, coupled_target(): lax.all_to_all(col_part, BOTH, 0, 0, axis_index_groups=groups, tiled=True)  51 us
    ppermute x27, starting transfers between devices, swap(): return lax.ppermute(value, BOTH, [(i, i ^ mask) for i in range(128)])  37.8 us
    dot_general x1, matrix products, local(): qkv = jnp.dot(tokens, folded, preferred_element_type=F32) * scale[:, None]  8.47 us
    pallas_call x1, Pallas kernels, coupled_target(): vmem_call(cost_kernel, (shape((32, rows, latent), BF), shape((4 * rows, 3...  5.86 us
    unnamed x18, local copies, waits for them, and re-layouts  3.87 us
  transfers between devices with their start and end apart: 28, of which 14 were waited for; matrix products, arithmetic and copies ran while one was open for 3% of the time, Pallas kernels for 5%

profile of v2, /device:TPU:1, one launch (start us, length us, event | category | flops | bytes accessed | tf_op | source)
XLA Modules:
  0.0 188.1 jit_solution(14549884565938951606)
XLA Ops:
  7.2 4.7 %collective-permute-start.2 = (bf16[32,2048]{1,0:T(8,128)(2,1)}, bf16[32,2048]{1,0:T(8,128)(2,1)S(1)}, u32[]{:S(2)}, u32[]{:S(2)}) collective-permute-start(bf16[32,2048]{1,0:T(8,128)(2,1)} %param.8), channel_id=1, source_target_pairs={{0,18},{1,19},{2,16},{3,17},{4,22},{5,23},{6,20},{7,21},{8,26},{9,... | collective-permute-start | bytes 393224 | tf_op jit(solution)/shard_map/ppermute | solution.py:25
  11.9 1.2 fusion.4
  13.1 0.6 fusion
  13.7 0.7 pad_maximum_fusion.4
  14.4 0.9 collective-permute-done.2
  15.4 2.8 %collective-permute-start.4 = (bf16[2,32,1024]{2,1,0:T(8,128)(2,1)S(1)}, bf16[2,32,1024]{2,1,0:T(8,128)(2,1)S(1)}, u32[]{:S(2)}, u32[]{:S(2)}) collective-permute-start(bf16[2,32,1024]{2,1,0:T(8,128)(2,1)S(1)} %get-tuple-element.35), channel_id=1, source_target_pairs={{0,64},{1,65},{2,66},{3,67},{4,68},{5,69},{6,70},{7,71},{8,72},{9,... | collective-permute-start | bytes 393224 | tf_op jit(solution)/shard_map/ppermute | solution.py:25
  18.2 0.3 collective-permute-start.3
  18.5 0.6 collective-permute-start.5
  19.1 1.8 collective-permute-start
  20.9 2.8 %collective-permute-done.3 = bf16[2,32,1024]{2,1,0:T(8,128)(2,1)S(1)} collective-permute-done((bf16[2,32,1024]{2,1,0:T(8,128)(2,1)S(1)}, bf16[2,32,1024]{2,1,0:T(8,128)(2,1)S(1)}, u32[]{:S(2)}, u32[]{:S(2)}) %collective-permute-start.3) | collective-permute-done | bytes 131104 | tf_op jit(solution)/shard_map/ppermute | solution.py:25
  23.6 0.7 collective-permute-done.5
  24.4 2.8 %collective-permute-start.8 = (bf16[4,2,32,1024]{3,2,1,0:T(8,128)(2,1)S(1)}, bf16[4,2,32,1024]{3,2,1,0:T(8,128)(2,1)S(1)}, u32[]{:S(2)}, u32[]{:S(2)}) collective-permute-start(bf16[4,2,32,1024]{3,2,1,0:T(8,128)(2,1)S(1)} %pad_maximum_fusion.refs_0_), channel_id=1, source_target_pairs={{0,12},{1,13},{2,14},{3,15},{4,8},{5,9},{6,10},{7,11},{8,4},{9,5},... | collective-permute-start | bytes 1572872 | tf_op jit(solution)/shard_map/ppermute | solution.py:25
  27.4 0.4 collective-permute-start.10
  28.1 2.6 %collective-permute-start.11 = (bf16[2,32,1024]{2,1,0:T(8,128)(2,1)S(1)}, bf16[2,32,1024]{2,1,0:T(8,128)(2,1)S(1)}, u32[]{:S(2)}, u32[]{:S(2)}) collective-permute-start(bf16[2,32,1024]{2,1,0:T(8,128)(2,1)S(1)} %get-tuple-element.29), channel_id=1, source_target_pairs={{0,12},{1,13},{2,14},{3,15},{4,8},{5,9},{6,10},{7,11},{8,4},{9,5},... | collective-permute-start | bytes 393224 | tf_op jit(solution)/shard_map/ppermute | solution.py:25
  30.7 2.9 %collective-permute-done.10 = bf16[2,32,1024]{2,1,0:T(8,128)(2,1)S(1)} collective-permute-done((bf16[2,32,1024]{2,1,0:T(8,128)(2,1)S(1)}, bf16[2,32,1024]{2,1,0:T(8,128)(2,1)S(1)}, u32[]{:S(2)}, u32[]{:S(2)}) %collective-permute-start.10) | collective-permute-done | bytes 131104 | tf_op jit(solution)/shard_map/ppermute | solution.py:25
  33.8 1.7 collective-permute-done.9
  35.6 0.8 collective-permute-start.6
  36.4 17.6 %collective-permute-done.11 = bf16[2,32,1024]{2,1,0:T(8,128)(2,1)S(1)} collective-permute-done((bf16[2,32,1024]{2,1,0:T(8,128)(2,1)S(1)}, bf16[2,32,1024]{2,1,0:T(8,128)(2,1)S(1)}, u32[]{:S(2)}, u32[]{:S(2)}) %collective-permute-start.11) | collective-permute-done | bytes 131104 | tf_op jit(solution)/shard_map/ppermute | solution.py:25
  54.0 3.1 %collective-permute-start.14 = (bf16[4,2,32,1024]{3,2,1,0:T(8,128)(2,1)S(1)}, bf16[4,2,32,1024]{3,2,1,0:T(8,128)(2,1)}, u32[]{:S(2)}, u32[]{:S(2)}) collective-permute-start(bf16[4,2,32,1024]{3,2,1,0:T(8,128)(2,1)S(1)} %pad_maximum_fusion.1.refs_4_), channel_id=1, source_target_pairs={{0,96},{1,97},{2,98},{3,99},{4,100},{5,101},{6,102},{7,103},{8,104... | collective-permute-start | bytes 1572872 | tf_op jit(solution)/shard_map/ppermute | solution.py:25
  57.1 0.7 copy-done.3
  58.5 5.6 %collective-permute-done.6.refs_1_ = bf16[4,2,32,1024]{3,2,1,0:T(8,128)(2,1)} collective-permute-done((bf16[4,2,32,1024]{3,2,1,0:T(8,128)(2,1)S(1)}, bf16[4,2,32,1024]{3,2,1,0:T(8,128)(2,1)}, u32[]{:S(2)}, u32[]{:S(2)}) %collective-permute-start.6) | collective-permute-done | bytes 524320 | tf_op jit(solution)/shard_map/ppermute | solution.py:25
  64.1 14.8 %collective-permute-done.14.refs_7_ = bf16[4,2,32,1024]{3,2,1,0:T(8,128)(2,1)} collective-permute-done((bf16[4,2,32,1024]{3,2,1,0:T(8,128)(2,1)S(1)}, bf16[4,2,32,1024]{3,2,1,0:T(8,128)(2,1)}, u32[]{:S(2)}, u32[]{:S(2)}) %collective-permute-start.14) | collective-permute-done | bytes 524320 | tf_op jit(solution)/shard_map/ppermute | solution.py:25
  78.9 0.4 collective-permute-done.12.refs_5_
  79.3 0.9 copy-done.4
  80.3 5.9 %shard_map.86 = (bf16[32,32,2048]{2,1,0:T(8,128)(2,1)}, f32[128,1024]{1,0:T(8,128)S(1)}, f32[8,128]{1,0:T(8,128)S(1)}) custom-call(s32[4]{0:T(128)S(1)} %pad_add_fusion.place, bf16[32,2048]{1,0:T(8,128)(2,1)S(1)} %copy-done.2, bf16[32,2048]{1,0:T(8,128)(2,1)S(1)} %collective-permute-done.n1, bf16[2,32,2048]{2,1,0:T(8,128)(2,1)S(1)} %copy-done.4, ...), custom_call_target="tpu_custom_call" | custom-call | flops 536870912 | bytes 8388608 | tf_op jit(solution)/shard_map/pallas_call | solution.py:225
  86.1 0.4 collective-permute-start.17
  86.5 4.3 %collective-permute-start.16 = (f32[8,128]{1,0:T(8,128)S(1)}, f32[8,128]{1,0:T(8,128)S(1)}, u32[]{:S(2)}, u32[]{:S(2)}) collective-permute-start(f32[8,128]{1,0:T(8,128)S(1)} %get-tuple-element.12.a), channel_id=1, source_target_pairs={{0,2},{1,3},{2,0},{3,1},{4,6},{5,7},{6,4},{7,5},{8,10},{9,11},{10,... | collective-permute-start | bytes 12296 | tf_op jit(solution)/shard_map/ppermute | solution.py:25
  90.8 1.3 collective-permute-done.16.c
  92.4 27.0 %all_to_all.15.parts_ref = f32[32,8,128]{2,1,0:T(8,128)S(1)} all-to-all(f32[32,8,128]{2,1,0:T(8,128)S(1)} %shard_map.87), channel_id=1, replica_groups={{0,4,8,12,18,22,26,30,32,36,40,44,50,54,58,62,64,68,72,76,82,86,90,94,9..., dimensions={0} | all-to-all | bytes 262144 | tf_op jit(solution)/shard_map/all_to_all | solution.py:240
  119.4 0.3 shard_map.88.a
  119.7 0.7 collective-permute-start.20
  120.4 3.2 %collective-permute-start.19 = (f32[8,128]{1,0:T(8,128)S(1)}, f32[8,128]{1,0:T(8,128)S(1)}, u32[]{:S(2)}, u32[]{:S(2)}) collective-permute-start(f32[8,128]{1,0:T(8,128)S(1)} %shard_map.88.a), channel_id=1, source_target_pairs={{0,2},{1,3},{2,0},{3,1},{4,6},{5,7},{6,4},{7,5},{8,10},{9,11},{10,... | collective-permute-start | bytes 12296 | tf_op jit(solution)/shard_map/ppermute | solution.py:25
  123.6 1.3 collective-permute-done.19.c
  125.1 12.0 %all_to_all.16.parts_ref = f32[32,8,128]{2,1,0:T(8,128)S(1)} all-to-all(f32[32,8,128]{2,1,0:T(8,128)S(1)} %shard_map.89), channel_id=1, replica_groups={{0,4,8,12,18,22,26,30,32,36,40,44,50,54,58,62,64,68,72,76,82,86,90,94,9..., dimensions={0} | all-to-all | bytes 262144 | tf_op jit(solution)/shard_map/all_to_all | solution.py:240
  137.1 0.3 shard_map.90.a
  137.4 1.0 collective-permute-start.23
  138.5 2.9 %collective-permute-start.22 = (f32[8,128]{1,0:T(8,128)S(1)}, f32[8,128]{1,0:T(8,128)S(1)}, u32[]{:S(2)}, u32[]{:S(2)}) collective-permute-start(f32[8,128]{1,0:T(8,128)S(1)} %shard_map.90.a), channel_id=1, source_target_pairs={{0,2},{1,3},{2,0},{3,1},{4,6},{5,7},{6,4},{7,5},{8,10},{9,11},{10,... | collective-permute-start | bytes 12296 | tf_op jit(solution)/shard_map/ppermute | solution.py:25
  141.3 1.3 collective-permute-done.22.c
  142.9 12.0 %all_to_all.17.parts_ref = f32[32,8,128]{2,1,0:T(8,128)S(1)} all-to-all(f32[32,8,128]{2,1,0:T(8,128)S(1)} %shard_map.91), channel_id=1, replica_groups={{0,4,8,12,18,22,26,30,32,36,40,44,50,54,58,62,64,68,72,76,82,86,90,94,9..., dimensions={0} | all-to-all | bytes 262144 | tf_op jit(solution)/shard_map/all_to_all | solution.py:240
  154.9 2.2 %copy-done.1 = bf16[32,32,2048]{2,1,0:T(8,128)(2,1)S(1)} copy-done((bf16[32,32,2048]{2,1,0:T(8,128)(2,1)S(1)}, bf16[32,32,2048]{2,1,0:T(8,128)(2,1)}, u32[]{:S(2)}) %copy-start.1) | copy-done | bytes 4194328
  157.1 1.6 shard_map.92
  158.6 2.5 %collective-permute-start.24 = (bf16[32,2176]{1,0:T(8,128)(2,1)S(1)}, bf16[32,2176]{1,0:T(8,128)(2,1)S(1)}, u32[]{:S(2)}, u32[]{:S(2)}) collective-permute-start(bf16[32,2176]{1,0:T(8,128)(2,1)S(1)} %get-tuple-element.15), channel_id=1, source_target_pairs={{0,1},{1,0},{2,3},{3,2},{4,5},{5,4},{6,7},{7,6},{8,9},{9,8},{10,11... | collective-permute-start | bytes 417800 | tf_op jit(solution)/shard_map/ppermute | solution.py:25
  161.2 1.8 collective-permute-start.26
  163.2 3.2 %collective-permute-done.25 = bf16[32,2176]{1,0:T(8,128)(2,1)S(1)} collective-permute-done((bf16[32,2176]{1,0:T(8,128)(2,1)S(1)}, bf16[32,2176]{1,0:T(8,128)(2,1)S(1)}, u32[]{:S(2)}, u32[]{:S(2)}) %collective-permute-start.25) | collective-permute-done | bytes 139296 | tf_op jit(solution)/shard_map/ppermute | solution.py:25
  166.6 3.0 %collective-permute-done.26 = bf16[32,2176]{1,0:T(8,128)(2,1)S(1)} collective-permute-done((bf16[32,2176]{1,0:T(8,128)(2,1)S(1)}, bf16[32,2176]{1,0:T(8,128)(2,1)S(1)}, u32[]{:S(2)}, u32[]{:S(2)}) %collective-permute-start.26) | collective-permute-done | bytes 139296 | tf_op jit(solution)/shard_map/ppermute | solution.py:25
  170.7 1.3 multiply_reduce_fusion
  172.1 0.7 fusion.12
  172.8 8.5 %multiply_convert_fusion = bf16[1024,6144]{1,0:T(8,128)(2,1)} fusion(f32[1024]{0:T(1024)S(1)} %rsqrt.11, bf16[192,6144]{1,0:T(8,128)(2,1)} %all-gather.2.cloned.1.call-done, bf16[1024,32]{1,0:T(8,128)(2,1)S(1)} %bitcast.36, bf16[1024,64]{1,0:T(8,128)(2,1)S(1)} %reshape.49), kind=kOutput, calls=%fused_computation | convolution fusion | flops 2430074880 | bytes 15142912 | tf_op jit(solution)/shard_map/dot_general | solution.py:295
  (68 shorter events, 4.0 us)
Async XLA Ops:
  7.2 5.9 %copy-start = (bf16[2048,384]{1,0:T(8,128)(2,1)S(1)}, bf16[2048,384]{1,0:T(8,128)(2,1)}, u32[]{:S(2)}) copy-start(bf16[2048,384]{1,0:T(8,128)(2,1)} %param.13) | copy-start | bytes 4718596
  7.2 7.2 %copy-start.7 = (bf16[32,2048]{1,0:T(8,128)(2,1)S(1)}, bf16[32,2048]{1,0:T(8,128)(2,1)}, u32[]{:S(2)}) copy-start(bf16[32,2048]{1,0:T(8,128)(2,1)} %param.8) | copy-start | bytes 393220
  7.2 165.6 %all-gather.2.cloned.1.call-start = ((), (), s32[]{:S(2)}) async-start(), calls=%async_computation.3 | async-start | bytes 2506752 | tf_op jit(solution)/shard_map/all_gather | solution.py:278
  7.2 8.1 %collective-permute-start.2 = (bf16[32,2048]{1,0:T(8,128)(2,1)}, bf16[32,2048]{1,0:T(8,128)(2,1)S(1)}, u32[]{:S(2)}, u32[]{:S(2)}) collective-permute-start(bf16[32,2048]{1,0:T(8,128)(2,1)} %param.8), channel_id=1, source_target_pairs={{0,18},{1,19},{2,16},{3,17},{4,22},{5,23},{6,20},{7,21},{8,26},{9,... | collective-permute-start | bytes 393224 | tf_op jit(solution)/shard_map/ppermute | solution.py:25
  13.1 6.0 %copy-start.2 = (bf16[32,2048]{1,0:T(8,128)(2,1)S(1)}, bf16[32,2048]{1,0:T(8,128)(2,1)}, u32[]{:S(2)}) copy-start(bf16[32,2048]{1,0:T(8,128)(2,1)} %n0.1) | copy-start | bytes 393220
  15.4 5.5 %collective-permute-start.4 = (bf16[2,32,1024]{2,1,0:T(8,128)(2,1)S(1)}, bf16[2,32,1024]{2,1,0:T(8,128)(2,1)S(1)}, u32[]{:S(2)}, u32[]{:S(2)}) collective-permute-start(bf16[2,32,1024]{2,1,0:T(8,128)(2,1)S(1)} %get-tuple-element.35), channel_id=1, source_target_pairs={{0,64},{1,65},{2,66},{3,67},{4,68},{5,69},{6,70},{7,71},{8,72},{9,... | collective-permute-start | bytes 393224 | tf_op jit(solution)/shard_map/ppermute | solution.py:25
  18.2 5.4 %collective-permute-start.3 = (bf16[2,32,1024]{2,1,0:T(8,128)(2,1)S(1)}, bf16[2,32,1024]{2,1,0:T(8,128)(2,1)S(1)}, u32[]{:S(2)}, u32[]{:S(2)}) collective-permute-start(bf16[2,32,1024]{2,1,0:T(8,128)(2,1)S(1)} %get-tuple-element.35), channel_id=1, source_target_pairs={{0,32},{1,33},{2,34},{3,35},{4,36},{5,37},{6,38},{7,39},{8,40},{9,... | collective-permute-start | bytes 393224 | tf_op jit(solution)/shard_map/ppermute | solution.py:25
  18.5 5.8 %collective-permute-start.5 = (bf16[2,32,1024]{2,1,0:T(8,128)(2,1)S(1)}, bf16[2,32,1024]{2,1,0:T(8,128)(2,1)S(1)}, u32[]{:S(2)}, u32[]{:S(2)}) collective-permute-start(bf16[2,32,1024]{2,1,0:T(8,128)(2,1)S(1)} %get-tuple-element.35), channel_id=1, source_target_pairs={{0,96},{1,97},{2,98},{3,99},{4,100},{5,101},{6,102},{7,103},{8,104... | collective-permute-start | bytes 393224 | tf_op jit(solution)/shard_map/ppermute | solution.py:25
  19.1 8.2 %collective-permute-start = (bf16[32,2048]{1,0:T(8,128)(2,1)S(1)}, bf16[32,2048]{1,0:T(8,128)(2,1)S(1)}, u32[]{:S(2)}, u32[]{:S(2)}) collective-permute-start(bf16[32,2048]{1,0:T(8,128)(2,1)S(1)} %copy-done.2), channel_id=1, source_target_pairs={{0,1},{1,0},{2,3},{3,2},{4,5},{5,4},{6,7},{7,6},{8,9},{9,8},{10,11... | collective-permute-start | bytes 393224 | tf_op jit(solution)/shard_map/ppermute | solution.py:25
  24.4 33.7 %collective-permute-start.8 = (bf16[4,2,32,1024]{3,2,1,0:T(8,128)(2,1)S(1)}, bf16[4,2,32,1024]{3,2,1,0:T(8,128)(2,1)S(1)}, u32[]{:S(2)}, u32[]{:S(2)}) collective-permute-start(bf16[4,2,32,1024]{3,2,1,0:T(8,128)(2,1)S(1)} %pad_maximum_fusion.refs_0_), channel_id=1, source_target_pairs={{0,12},{1,13},{2,14},{3,15},{4,8},{5,9},{6,10},{7,11},{8,4},{9,5},... | collective-permute-start | bytes 1572872 | tf_op jit(solution)/shard_map/ppermute | solution.py:25
  27.3 29.8 %collective-permute-start.1 = (bf16[2,32,2048]{2,1,0:T(8,128)(2,1)S(1)}, bf16[2,32,2048]{2,1,0:T(8,128)(2,1)S(1)}, u32[]{:S(2)}, u32[]{:S(2)}) collective-permute-start(bf16[2,32,2048]{2,1,0:T(8,128)(2,1)S(1)} %pad_maximum_fusion.3), channel_id=1, source_target_pairs={{0,2},{1,3},{2,0},{3,1},{4,6},{5,7},{6,4},{7,5},{8,10},{9,11},{10,... | collective-permute-start | bytes 786440 | tf_op jit(solution)/shard_map/ppermute | solution.py:25
  27.4 6.2 %collective-permute-start.10 = (bf16[2,32,1024]{2,1,0:T(8,128)(2,1)S(1)}, bf16[2,32,1024]{2,1,0:T(8,128)(2,1)S(1)}, u32[]{:S(2)}, u32[]{:S(2)}) collective-permute-start(bf16[2,32,1024]{2,1,0:T(8,128)(2,1)S(1)} %get-tuple-element.29), channel_id=1, source_target_pairs={{0,8},{1,9},{2,10},{3,11},{4,12},{5,13},{6,14},{7,15},{8,0},{9,1},... | collective-permute-start | bytes 393224 | tf_op jit(solution)/shard_map/ppermute | solution.py:25
  27.8 7.7 %collective-permute-start.9 = (bf16[2,32,1024]{2,1,0:T(8,128)(2,1)S(1)}, bf16[2,32,1024]{2,1,0:T(8,128)(2,1)S(1)}, u32[]{:S(2)}, u32[]{:S(2)}) collective-permute-start(bf16[2,32,1024]{2,1,0:T(8,128)(2,1)S(1)} %get-tuple-element.29), channel_id=1, source_target_pairs={{0,4},{1,5},{2,6},{3,7},{4,0},{5,1},{6,2},{7,3},{8,12},{9,13},{10,... | collective-permute-start | bytes 393224 | tf_op jit(solution)/shard_map/ppermute | solution.py:25
  28.1 25.9 %collective-permute-start.11 = (bf16[2,32,1024]{2,1,0:T(8,128)(2,1)S(1)}, bf16[2,32,1024]{2,1,0:T(8,128)(2,1)S(1)}, u32[]{:S(2)}, u32[]{:S(2)}) collective-permute-start(bf16[2,32,1024]{2,1,0:T(8,128)(2,1)S(1)} %get-tuple-element.29), channel_id=1, source_target_pairs={{0,12},{1,13},{2,14},{3,15},{4,8},{5,9},{6,10},{7,11},{8,4},{9,5},... | collective-permute-start | bytes 393224 | tf_op jit(solution)/shard_map/ppermute | solution.py:25
  33.6 24.9 %collective-permute-start.7 = (bf16[4,2,32,1024]{3,2,1,0:T(8,128)(2,1)S(1)}, bf16[4,2,32,1024]{3,2,1,0:T(8,128)(2,1)}, u32[]{:S(2)}, u32[]{:S(2)}) collective-permute-start(bf16[4,2,32,1024]{3,2,1,0:T(8,128)(2,1)S(1)} %pad_maximum_fusion.refs_0_), channel_id=1, source_target_pairs={{0,8},{1,9},{2,10},{3,11},{4,12},{5,13},{6,14},{7,15},{8,0},{9,1},... | collective-permute-start | bytes 1572872 | tf_op jit(solution)/shard_map/ppermute | solution.py:25
  35.6 28.5 %collective-permute-start.6 = (bf16[4,2,32,1024]{3,2,1,0:T(8,128)(2,1)S(1)}, bf16[4,2,32,1024]{3,2,1,0:T(8,128)(2,1)}, u32[]{:S(2)}, u32[]{:S(2)}) collective-permute-start(bf16[4,2,32,1024]{3,2,1,0:T(8,128)(2,1)S(1)} %pad_maximum_fusion.refs_0_), channel_id=1, source_target_pairs={{0,4},{1,5},{2,6},{3,7},{4,0},{5,1},{6,2},{7,3},{8,12},{9,13},{10,... | collective-permute-start | bytes 1572872 | tf_op jit(solution)/shard_map/ppermute | solution.py:25
  54.0 24.9 %collective-permute-start.14 = (bf16[4,2,32,1024]{3,2,1,0:T(8,128)(2,1)S(1)}, bf16[4,2,32,1024]{3,2,1,0:T(8,128)(2,1)}, u32[]{:S(2)}, u32[]{:S(2)}) collective-permute-start(bf16[4,2,32,1024]{3,2,1,0:T(8,128)(2,1)S(1)} %pad_maximum_fusion.1.refs_4_), channel_id=1, source_target_pairs={{0,96},{1,97},{2,98},{3,99},{4,100},{5,101},{6,102},{7,103},{8,104... | collective-permute-start | bytes 1572872 | tf_op jit(solution)/shard_map/ppermute | solution.py:25
  57.1 0.7 copy-start.3
  57.8 21.1 %collective-permute-start.13 = (bf16[4,2,32,1024]{3,2,1,0:T(8,128)(2,1)S(1)}, bf16[4,2,32,1024]{3,2,1,0:T(8,128)(2,1)}, u32[]{:S(2)}, u32[]{:S(2)}) collective-permute-start(bf16[4,2,32,1024]{3,2,1,0:T(8,128)(2,1)S(1)} %pad_maximum_fusion.1.refs_4_), channel_id=1, source_target_pairs={{0,64},{1,65},{2,66},{3,67},{4,68},{5,69},{6,70},{7,71},{8,72},{9,... | collective-permute-start | bytes 1572872 | tf_op jit(solution)/shard_map/ppermute | solution.py:25
  58.1 21.2 %collective-permute-start.12 = (bf16[4,2,32,1024]{3,2,1,0:T(8,128)(2,1)S(1)}, bf16[4,2,32,1024]{3,2,1,0:T(8,128)(2,1)}, u32[]{:S(2)}, u32[]{:S(2)}) collective-permute-start(bf16[4,2,32,1024]{3,2,1,0:T(8,128)(2,1)S(1)} %pad_maximum_fusion.1.refs_4_), channel_id=1, source_target_pairs={{0,32},{1,33},{2,34},{3,35},{4,36},{5,37},{6,38},{7,39},{8,40},{9,... | collective-permute-start | bytes 1572872 | tf_op jit(solution)/shard_map/ppermute | solution.py:25
  79.3 1.0 copy-start.4
  86.1 4.7 %collective-permute-start.17 = (f32[8,128]{1,0:T(8,128)S(1)}, f32[8,128]{1,0:T(8,128)S(1)}, u32[]{:S(2)}, u32[]{:S(2)}) collective-permute-start(f32[8,128]{1,0:T(8,128)S(1)} %get-tuple-element.12.a), channel_id=1, source_target_pairs={{0,3},{1,2},{2,1},{3,0},{4,7},{5,6},{6,5},{7,4},{8,11},{9,10},{10,... | collective-permute-start | bytes 12296 | tf_op jit(solution)/shard_map/ppermute | solution.py:25
  86.5 5.6 %collective-permute-start.16 = (f32[8,128]{1,0:T(8,128)S(1)}, f32[8,128]{1,0:T(8,128)S(1)}, u32[]{:S(2)}, u32[]{:S(2)}) collective-permute-start(f32[8,128]{1,0:T(8,128)S(1)} %get-tuple-element.12.a), channel_id=1, source_target_pairs={{0,2},{1,3},{2,0},{3,1},{4,6},{5,7},{6,4},{7,5},{8,10},{9,11},{10,... | collective-permute-start | bytes 12296 | tf_op jit(solution)/shard_map/ppermute | solution.py:25
  90.8 1.3 collective-permute-start.15
  119.7 3.9 %collective-permute-start.20 = (f32[8,128]{1,0:T(8,128)S(1)}, f32[8,128]{1,0:T(8,128)S(1)}, u32[]{:S(2)}, u32[]{:S(2)}) collective-permute-start(f32[8,128]{1,0:T(8,128)S(1)} %shard_map.88.a), channel_id=1, source_target_pairs={{0,3},{1,2},{2,1},{3,0},{4,7},{5,6},{6,5},{7,4},{8,11},{9,10},{10,... | collective-permute-start | bytes 12296 | tf_op jit(solution)/shard_map/ppermute | solution.py:25
  120.4 4.4 %collective-permute-start.19 = (f32[8,128]{1,0:T(8,128)S(1)}, f32[8,128]{1,0:T(8,128)S(1)}, u32[]{:S(2)}, u32[]{:S(2)}) collective-permute-start(f32[8,128]{1,0:T(8,128)S(1)} %shard_map.88.a), channel_id=1, source_target_pairs={{0,2},{1,3},{2,0},{3,1},{4,6},{5,7},{6,4},{7,5},{8,10},{9,11},{10,... | collective-permute-start | bytes 12296 | tf_op jit(solution)/shard_map/ppermute | solution.py:25
  123.6 1.3 collective-permute-start.18
  137.4 3.9 %collective-permute-start.23 = (f32[8,128]{1,0:T(8,128)S(1)}, f32[8,128]{1,0:T(8,128)S(1)}, u32[]{:S(2)}, u32[]{:S(2)}) collective-permute-start(f32[8,128]{1,0:T(8,128)S(1)} %shard_map.90.a), channel_id=1, source_target_pairs={{0,3},{1,2},{2,1},{3,0},{4,7},{5,6},{6,5},{7,4},{8,11},{9,10},{10,... | collective-permute-start | bytes 12296 | tf_op jit(solution)/shard_map/ppermute | solution.py:25
  138.5 4.1 %collective-permute-start.22 = (f32[8,128]{1,0:T(8,128)S(1)}, f32[8,128]{1,0:T(8,128)S(1)}, u32[]{:S(2)}, u32[]{:S(2)}) collective-permute-start(f32[8,128]{1,0:T(8,128)S(1)} %shard_map.90.a), channel_id=1, source_target_pairs={{0,2},{1,3},{2,0},{3,1},{4,6},{5,7},{6,4},{7,5},{8,10},{9,11},{10,... | collective-permute-start | bytes 12296 | tf_op jit(solution)/shard_map/ppermute | solution.py:25
  141.3 1.3 collective-permute-start.21
  154.9 2.2 %copy-start.1 = (bf16[32,32,2048]{2,1,0:T(8,128)(2,1)S(1)}, bf16[32,32,2048]{2,1,0:T(8,128)(2,1)}, u32[]{:S(2)}) copy-start(bf16[32,32,2048]{2,1,0:T(8,128)(2,1)} %get-tuple-element.11.data_ref) | copy-start | bytes 12582916
  157.1 4.1 %copy-start.8 = (s32[32]{0:T(128)S(1)}, s32[32]{0:T(128)}, u32[]{:S(2)}) copy-start(s32[32]{0:T(128)} %param.9) | copy-start | bytes 388
  157.1 4.1 %copy-start.5 = (bf16[32,2048]{1,0:T(8,128)(2,1)S(1)}, bf16[32,2048]{1,0:T(8,128)(2,1)}, u32[]{:S(2)}) copy-start(bf16[32,2048]{1,0:T(8,128)(2,1)} %param.11) | copy-start | bytes 393220
  158.6 12.1 %copy-start.6 = (bf16[64,2048]{1,0:T(8,128)(2,1)S(1)}, bf16[64,2048]{1,0:T(8,128)(2,1)}, u32[]{:S(2)}) copy-start(bf16[64,2048]{1,0:T(8,128)(2,1)} %param.10) | copy-start | bytes 786436
  158.6 4.4 %collective-permute-start.24 = (bf16[32,2176]{1,0:T(8,128)(2,1)S(1)}, bf16[32,2176]{1,0:T(8,128)(2,1)S(1)}, u32[]{:S(2)}, u32[]{:S(2)}) collective-permute-start(bf16[32,2176]{1,0:T(8,128)(2,1)S(1)} %get-tuple-element.15), channel_id=1, source_target_pairs={{0,1},{1,0},{2,3},{3,2},{4,5},{5,4},{6,7},{7,6},{8,9},{9,8},{10,11... | collective-permute-start | bytes 417800 | tf_op jit(solution)/shard_map/ppermute | solution.py:25
  161.2 5.2 %collective-permute-start.25 = (bf16[32,2176]{1,0:T(8,128)(2,1)S(1)}, bf16[32,2176]{1,0:T(8,128)(2,1)S(1)}, u32[]{:S(2)}, u32[]{:S(2)}) collective-permute-start(bf16[32,2176]{1,0:T(8,128)(2,1)S(1)} %get-tuple-element.16), channel_id=1, source_target_pairs={{0,2},{1,3},{2,0},{3,1},{4,6},{5,7},{6,4},{7,5},{8,10},{9,11},{10,... | collective-permute-start | bytes 417800 | tf_op jit(solution)/shard_map/ppermute | solution.py:25
  161.2 8.4 %collective-permute-start.26 = (bf16[32,2176]{1,0:T(8,128)(2,1)S(1)}, bf16[32,2176]{1,0:T(8,128)(2,1)S(1)}, u32[]{:S(2)}, u32[]{:S(2)}) collective-permute-start(bf16[32,2176]{1,0:T(8,128)(2,1)S(1)} %get-tuple-element.17), channel_id=1, source_target_pairs={{0,3},{1,2},{2,1},{3,0},{4,7},{5,6},{6,5},{7,4},{8,11},{9,10},{10,... | collective-permute-start | bytes 417800 | tf_op jit(solution)/shard_map/ppermute | solution.py:25
Sparse Core Ops, SparseCore 0:
  14.5 48.9 all-gather.1

commit v3 on v2

v3 whole, which is shorter than its diff:
```python
import functools

import jax
import jax.numpy as jnp
from jax import lax
from jax.experimental import pallas as pl
from jax.experimental.pallas import tpu as pltpu
from jax.sharding import PartitionSpec as P

ITERS = 3
TGRID = 1000
BOTH = ("src", "tgt")
CORE = 1
Z_STEPS = (2, 16, 18)
Y_STEPS = (4, 8, 12)
X_STEPS = (32, 64, 96)
BF, F32 = jnp.bfloat16, jnp.float32


def epsilon_of(step):
    return 0.04 * 0.45**step


def swap(value, mask):
    return lax.ppermute(value, BOTH, [(i, i ^ mask) for i in range(128)])


def column_groups():
    groups = {}
    for i in range(128):
        groups.setdefault(((i >> 4) & 1, i & 3), []).append(i)
    return [groups[key] for key in sorted(groups)]


def vmem_call(kernel, out_shape, scratch=(), smem=0, inputs=0, flops=0, nbytes=0):
    return pl.pallas_call(
        kernel,
        out_shape=out_shape,
        in_specs=[pl.BlockSpec(memory_space=pltpu.SMEM)] * smem
        + [pl.BlockSpec(memory_space=pltpu.VMEM)] * inputs,
        out_specs=jax.tree.map(lambda _: pl.BlockSpec(memory_space=pltpu.VMEM), out_shape),
        scratch_shapes=list(scratch),
        compiler_params=pltpu.CompilerParams(vmem_limit_bytes=48 * 1024 * 1024),
        cost_estimate=pl.CostEstimate(flops=flops, bytes_accessed=nbytes, transcendentals=0),
    )


def shape(dims, dtype=F32):
    return jax.ShapeDtypeStruct(dims, dtype)


def eye(size):
    return lax.broadcasted_iota(jnp.int32, (size, size), 0) == lax.broadcasted_iota(
        jnp.int32, (size, size), 1
    )


def to_lanes(column):
    size = column.shape[0]
    wide = jnp.broadcast_to(column, (size, size))
    return jnp.sum(jnp.where(eye(size), wide, 0.0), axis=0, keepdims=True)


def to_rows(lanes):
    size = lanes.shape[1]
    wide = jnp.broadcast_to(lanes, (size, size))
    return jnp.sum(jnp.where(eye(size), wide, 0.0), axis=1, keepdims=True)


def join_lse(parts):
    peak = functools.reduce(jnp.maximum, parts)
    total = functools.reduce(jnp.add, [jnp.exp(part - peak) for part in parts])
    return peak + jnp.log(total)


def row_stats(cost_ref, col_pot, inverse):
    tiles = cost_ref.shape[1] // 128

    def score(tile):
        part = cost_ref[:, tile * 128 : (tile + 1) * 128]
        if col_pot is None:
            return -part * inverse
        return (col_pot[tile : tile + 1, :] - part) * inverse

    peak = score(0)
    for tile in range(1, tiles):
        peak = jnp.maximum(peak, score(tile))
    peak = jnp.max(peak, axis=1, keepdims=True)
    return score, peak


def row_lse(cost_ref, col_pot, inverse):
    score, peak = row_stats(cost_ref, col_pot, inverse)
    total = jnp.exp(score(0) - peak)
    for tile in range(1, cost_ref.shape[1] // 128):
        total = total + jnp.exp(score(tile) - peak)
    return peak + jnp.log(jnp.sum(total, axis=1, keepdims=True))


def pack(lse, out_ref):
    out_ref[...] = jnp.zeros(out_ref.shape, F32)
    for part in range(lse.shape[0] // 128):
        out_ref[part : part + 1, :] = to_lanes(lse[part * 128 : part * 128 + 128])


def cost_kernel(place, data_ref, a, b, c, d, cost_ref, lse_ref, noise_ref):
    h = place[2]
    rows, latent = a.shape[1:]
    for k, pair in enumerate((a, b, c, d)):
        noise_ref[h ^ (2 * k)] = pair[0]
        noise_ref[h ^ (2 * k + 1)] = pair[1]
    noise = noise_ref[...].reshape(8 * rows, latent)

    def square_sum(value):
        total = jnp.zeros((value.shape[0], 128), F32)
        for tile in range(latent // 128):
            part = value[:, tile * 128 : (tile + 1) * 128].astype(F32)
            total = total + part * part
        return jnp.sum(total, axis=1, keepdims=True)

    noise_sq = square_sum(noise)
    for group in range(2):
        part = data_ref[group * 8 : group * 8 + 8].reshape(8 * rows, latent)
        cross = lax.dot_general(
            noise, part, (((1,), (1,)), ((), ())), preferred_element_type=F32
        )
        for side in range(2):
            data_sq = to_lanes(square_sum(part[side * 128 : side * 128 + 128]))
            at = group * 256 + side * 128
            cost_ref[:, at : at + 128] = (
                noise_sq + data_sq - 2.0 * cross[:, side * 128 : side * 128 + 128]
            ) / latent
    pack(row_lse(cost_ref, None, 1.0 / epsilon_of(0)), lse_ref)


def col_kernel(step, cost_ref, a, b, c, d, out_ref):
    epsilon = epsilon_of(step)
    joined = -epsilon * join_lse([a[...], b[...], c[...], d[...]])
    halfway = cost_ref.shape[0] // 2
    inverse = 1.0 / epsilon
    upper = (to_rows(joined[0:1, :]) - cost_ref[0:halfway, :]) * inverse
    lower = (to_rows(joined[1:2, :]) - cost_ref[halfway : 2 * halfway, :]) * inverse
    peak = jnp.maximum(
        jnp.max(upper, axis=0, keepdims=True), jnp.max(lower, axis=0, keepdims=True)
    )
    total = jnp.sum(jnp.exp(upper - peak) + jnp.exp(lower - peak), axis=0, keepdims=True)
    lse = peak + jnp.log(total)
    place = lax.broadcasted_iota(jnp.int32, (8, 128), 0)
    packed = jnp.zeros((8, 128), F32)
    for tile in range(lse.shape[1] // 128):
        packed = jnp.where(place == tile, lse[:, tile * 128 : (tile + 1) * 128], packed)
    out_ref[...] = jnp.broadcast_to(packed[None], out_ref.shape)


def col_potential(step, parts_ref):
    parts = parts_ref[...]
    peak = jnp.max(parts, axis=0)
    total = jnp.sum(jnp.exp(parts - peak[None]), axis=0)
    return -epsilon_of(step) * (peak + jnp.log(total))


def row_kernel(step, cost_ref, parts_ref, lse_ref):
    pack(row_lse(cost_ref, col_potential(step - 1, parts_ref), 1.0 / epsilon_of(step)), lse_ref)


def packed_log(value):
    lane = lax.broadcasted_iota(jnp.int32, value.shape, 1)
    high = value.astype(BF).astype(F32)
    middle = (value - high).astype(BF).astype(F32)
    low = value - high - middle
    return jnp.where(
        lane == 0, high, jnp.where(lane == 1, middle, jnp.where(lane == 2, low, 0.0))
    ).astype(BF)


def target_kernel(place, cost_ref, data_ref, parts_ref, keep_ref, log_ref, send_ref, coupling, sums, lses):
    h = place[2]
    col_pot = col_potential(ITERS - 1, parts_ref)
    score, peak = row_stats(cost_ref, col_pot, 1.0 / epsilon_of(ITERS - 1))
    total = jnp.zeros(cost_ref.shape[:1] + (128,), F32)
    for tile in range(cost_ref.shape[1] // 128):
        expo = jnp.exp(score(tile) - peak)
        total = total + expo
        coupling[:, tile * 128 : (tile + 1) * 128] = expo.astype(BF)
    denom = jnp.sum(total, axis=1, keepdims=True)
    count, rows, latent = sums.shape
    lses[...] = jnp.broadcast_to(peak + jnp.log(denom), (count * rows, 128)).reshape(lses.shape)
    share = 1.0 / denom
    for at in range(0, latent, 512):
        part = data_ref[:, :, at : at + 512].reshape(-1, 512)
        product = jnp.dot(coupling[...], part, preferred_element_type=F32) * share
        sums[:, :, at : at + 512] = product.reshape(count, rows, 512)
    for k in range(4):
        keep_ref[k] = sums[h ^ (2 * k)]
        log_ref[k] = lses[h ^ (2 * k)]
        send_ref[k, :, 0:latent] = sums[h ^ (2 * k + 1)].astype(BF)
        send_ref[k, :, latent : latent + 128] = packed_log(lses[h ^ (2 * k + 1)])


def read_log(ref_value):
    return jnp.sum(ref_value.astype(F32), axis=1, keepdims=True)


def pair_kernel(keep_ref, log_ref, got_ref, own_ref, own_log_ref, s1, s2, s3):
    latent = keep_ref.shape[2]
    for k, out in enumerate((own_ref, s1, s2, s3)):
        first = log_ref[k]
        second = jnp.broadcast_to(read_log(got_ref[k, :, latent : latent + 128]), first.shape)
        total = join_lse([first, second])
        mixed = keep_ref[k] * jnp.exp(first - total)[:, 0:1] + got_ref[
            k, :, 0:latent
        ].astype(F32) * jnp.exp(second - total)[:, 0:1]
        if k == 0:
            out[...] = mixed
            own_log_ref[...] = total
        else:
            out[:, 0:latent] = mixed.astype(BF)
            out[:, latent : latent + 128] = packed_log(total)


def finish_kernel(own_ref, log_ref, a, b, c, noise_ref, time_ref, velocity_ref, mixed_ref):
    latent = own_ref.shape[1]
    logs = [log_ref[...]] + [
        jnp.broadcast_to(read_log(got[:, latent : latent + 128]), log_ref.shape)
        for got in (a, b, c)
    ]
    total = join_lse(logs)
    shares = [jnp.exp(log - total)[:, 0:1] for log in logs]
    times = time_ref[...].astype(F32) / TGRID
    for at in range(0, latent, 256):
        cut = slice(at, at + 256)
        target = own_ref[:, cut] * shares[0]
        for got, share in zip((a, b, c), shares[1:]):
            target = target + got[:, cut].astype(F32) * share
        noise = noise_ref[:, cut].astype(F32)
        velocity_ref[:, cut] = (target - noise).astype(BF)
        mixed_ref[:, cut] = ((1.0 - times) * noise + times * target).astype(BF)


def qkv_kernel(place, tokens_ref, table_ref, f0, f1, f2, f3, out_ref):
    width = table_ref.shape[1]
    chunk = tokens_ref[...]
    count = chunk.shape[0]
    total = jnp.zeros((count, 128), F32)
    for col in range(0, width, 256):
        part = jnp.dot(chunk, table_ref[:, col : col + 256], preferred_element_type=F32)
        part = part * part
        total = total + part[:, 0:128] + part[:, 128:256]
    scale = lax.rsqrt(jnp.sum(total, axis=1, keepdims=True) / width + 1e-06)
    columns = f0.shape[2]
    for k in range(16):
        folded = (f0, f1, f2, f3)[k // 4][k % 4]
        product = jnp.dot(chunk, folded, preferred_element_type=F32) * scale
        at = pl.multiple_of((place[3] ^ k) * columns, 128)
        out_ref[:, pl.ds(at, columns)] = product.astype(BF)


def halves(value):
    high = value.astype(BF)
    low = (value - high.astype(F32)).astype(BF)
    return high, low


def folded_weights(embed_weight, position, norm_gain, qkv_weight):
    scaled = jnp.concatenate([embed_weight, position], 0).astype(F32) * norm_gain
    high, low = halves(scaled)
    both = jnp.dot(jnp.concatenate([high, low], 0), qkv_weight, preferred_element_type=F32)
    rows = scaled.shape[0]
    return jnp.concatenate(halves(both[:rows] + both[rows:]), 0)


def together(*values):
    return lax.optimization_barrier(values)


def coupled_target(noise, data, t_index, place, folded):
    rows, latent = noise.shape
    groups = column_groups()
    noise_pair = jnp.stack([noise, swap(noise, CORE)])
    noises = [noise_pair] + [swap(noise_pair, mask) for mask in Z_STEPS]
    spread = jnp.broadcast_to(data[None], (16, rows, latent)).reshape(16 * rows, latent)
    data_all = lax.all_to_all(
        lax.optimization_barrier(spread), BOTH, 0, 0, axis_index_groups=groups, tiled=True
    ).reshape(16, rows, latent)
    flops = 2 * 8 * rows * 16 * rows * latent
    cost, row_part = vmem_call(
        cost_kernel,
        (shape((8 * rows, 16 * rows)), shape((8, 128))),
        scratch=[pltpu.VMEM((8, rows, latent), BF)],
        smem=1,
        inputs=5,
        flops=flops,
        nbytes=4 * 1024 * 1024,
    )(place, data_all, *noises)
    quads = [None] * 4
    folded, row_part = together(folded, row_part)
    folded = jnp.stack([folded, swap(folded, CORE)])
    for step in range(ITERS):
        if step == 1:
            folded, row_part = together(folded, row_part)
            quads = [folded, swap(folded, Y_STEPS[0]), None, swap(folded, Y_STEPS[2])]
        elif step == 2:
            folded, row_part = together(folded, row_part)
            quads[2] = swap(folded, Y_STEPS[1])
        row_pair = join_lse([row_part, swap(row_part, CORE)])
        parts = [row_pair] + [swap(row_pair, mask) for mask in Z_STEPS]
        col_part = vmem_call(
            functools.partial(col_kernel, step), shape((16, 8, 128)), inputs=5, nbytes=1024 * 1024
        )(cost, *parts)
        if step == 0:
            folded, col_part = together(folded, col_part)
            folded = jnp.concatenate([folded, swap(folded, Z_STEPS[0])])
        col_parts = lax.all_to_all(
            col_part, BOTH, 0, 0, axis_index_groups=groups, tiled=True
        )
        if step == 0:
            folded, col_parts = together(folded, col_parts)
        elif step == 1:
            quads[1], quads[3], col_parts = together(quads[1], quads[3], col_parts)
        elif step == 2:
            quads[2], col_parts = together(quads[2], col_parts)
        if step + 1 < ITERS:
            row_part = vmem_call(
                functools.partial(row_kernel, step + 1),
                shape((8, 128)),
                inputs=2,
                nbytes=1024 * 1024,
            )(cost, col_parts)
    keep, log, send = vmem_call(
        target_kernel,
        (
            shape((4, rows, latent)),
            shape((4, rows, 128)),
            shape((4, rows, latent + 128), BF),
        ),
        scratch=[
            pltpu.VMEM((8 * rows, 16 * rows), BF),
            pltpu.VMEM((8, rows, latent), F32),
            pltpu.VMEM((8, rows, 128), F32),
        ],
        smem=1,
        inputs=3,
        flops=flops,
        nbytes=6 * 1024 * 1024,
    )(place, cost, data_all, col_parts)
    own, own_log, *sends = vmem_call(
        pair_kernel,
        (shape((rows, latent)), shape((rows, 128))) + (shape((rows, latent + 128), BF),) * 3,
        inputs=3,
        nbytes=2 * 1024 * 1024,
    )(keep, log, swap(send, CORE))
    others = [swap(value, mask) for value, mask in zip(sends, Z_STEPS)]
    velocity, mixed = vmem_call(
        finish_kernel, (shape((rows, latent), BF),) * 2, inputs=7, nbytes=1024 * 1024
    )(own, own_log, *others, noise, t_index[:, None])
    return velocity, mixed, quads


def local(noise, data, t_index, embed_weight, position, norm_gain, qkv_weight):
    own = noise.shape[0]
    src, tgt = lax.axis_index("src"), lax.axis_index("tgt")
    ring = (src % 2) * 4 + tgt % 4
    place = jnp.stack([src // 2, tgt // 4, ring, tgt]).astype(jnp.int32)
    folded = folded_weights(embed_weight, position, norm_gain, qkv_weight)
    velocity, mixed, quads = coupled_target(noise, data, t_index, place, folded)
    patch_in, width = embed_weight.shape
    patch_count = position.shape[0]
    patches = mixed.reshape(own * patch_count, patch_in)
    spots = jnp.tile(jnp.eye(patch_count, dtype=BF), (own, 1))
    tokens = jnp.concatenate([patches, spots, patches, spots], 1)
    table = jnp.concatenate([embed_weight, position], 0)
    table = jnp.concatenate([table, jnp.zeros_like(table)], 0)
    quad, depth, columns = quads[0].shape
    count = 4 * quad
    chunk = 256
    whole = pl.BlockSpec((quad, depth, columns), lambda j, where: (0, 0, 0))
    qkv = pl.pallas_call(
        qkv_kernel,
        out_shape=shape((own * patch_count, count * columns), BF),
        grid_spec=pltpu.PrefetchScalarGridSpec(
            num_scalar_prefetch=1,
            grid=(own * patch_count // chunk,),
            in_specs=[
                pl.BlockSpec((chunk, depth), lambda j, where: (j, 0)),
                pl.BlockSpec((depth, width), lambda j, where: (0, 0)),
            ]
            + [whole] * 4,
            out_specs=pl.BlockSpec((chunk, count * columns), lambda j, where: (j, 0)),
        ),
        compiler_params=pltpu.CompilerParams(vmem_limit_bytes=48 * 1024 * 1024),
        cost_estimate=pl.CostEstimate(
            flops=2 * own * patch_count * depth * count * columns,
            bytes_accessed=16 * 1024 * 1024,
            transcendentals=0,
        ),
    )(place, tokens, table, *quads)
    return (velocity, qkv)


def solution(mesh):
    return jax.shard_map(
        local,
        mesh=mesh,
        in_specs=(
            P(("src", "tgt"), None),
            P(("src", "tgt"), None),
            P(("src", "tgt")),
            P(),
            P(),
            P(),
            P(None, "tgt"),
        ),
        out_specs=(P(("src", "tgt"), None), P(("src", "tgt"), None)),
        check_vma=False,
    )
```

time: 189 us -> 151 us (0.80)
  blocking collectives: 51 us -> 21.3 us
  between operations: 14.3 us -> 0.89 us
  waiting for transfers between devices: 57.5 us -> 45.6 us
  starting transfers between devices: 37.9 us -> 48.2 us
  Pallas kernels: 8.8 us -> 18.9 us
  matrix products: 10.3 us -> 0.57 us
  local copies, waits for them, and re-layouts: 4.75 us -> 10.9 us
    all_to_all x3 -> x2, blocking collectives: 51 us -> 21.3 us  [coupled_target(): lax.all_to_all(col_part, BOTH, 0, 0, axis_index_groups=groups, tiled=True)]
    ppermute x27 -> x25, waiting for transfers between devices: 57.5 us -> 33.9 us  [swap(): return lax.ppermute(value, BOTH, [(i, i ^ mask) for i in range(128)])]
    all_to_all x0 -> x2, waiting for transfers between devices: none -> 11.7 us  [the longest x1 9.53 us: coupled_target(): lax.all_to_all(lax.optimization_barrier(spread), BOTH, 0, 0, axis_index_g...]
    all_to_all x0 -> x2, starting transfers between devices: none -> 11.3 us  [the longest x1 7.78 us: coupled_target(): lax.all_to_all(lax.optimization_barrier(spread), BOTH, 0, 0, axis_index_g...]
    pallas_call x5 -> x8, Pallas kernels: 8.19 us -> 18.3 us  [the longest x1 8.46 us: local(): pl.pallas_call(qkv_kernel, out_shape=shape((own * patch_count, count * co...]
    dot_general x2 -> x0, matrix products: 9.78 us -> none  [the longest x1 8.47 us: local(): qkv = jnp.dot(tokens, folded, preferred_element_type=F32) * scale[:, None]]
    broadcast_in_dim x0 -> x3, local copies, waits for them, and re-layouts: none -> 3.34 us  [the longest x1 2.59 us: coupled_target(): jnp.broadcast_to(data[None], (16, rows, latent)).reshape(16 * rows, latent)]
    concatenate x0 -> x3, other arithmetic: none -> 2.71 us  [the longest x1 1.52 us: local(): tokens = jnp.concatenate([patches, spots, patches, spots], 1)]
  transfers between devices with their start and end apart: 28 -> 27, of which waited for: 14 -> 18; matrix products, arithmetic and copies ran while one was open for 3% -> 2% of each run, Pallas kernels for 5% -> 1%
where the time goes in v3:
time: 151 us; the launch traced here: 150 us
  starting transfers between devices  48.2 us (32%)
  waiting for transfers between devices  45.6 us (30%)
  blocking collectives  21.3 us (14%)
  Pallas kernels  18.9 us (13%)
  local copies, waits for them, and re-layouts  10.9 us (7%)
  other arithmetic  3.65 us (2%)
    ppermute x25, starting transfers between devices, swap(): return lax.ppermute(value, BOTH, [(i, i ^ mask) for i in range(128)])  37 us
    ppermute x25, waiting for transfers between devices, swap(): return lax.ppermute(value, BOTH, [(i, i ^ mask) for i in range(128)])  33.9 us
    all_to_all x2, blocking collectives, coupled_target(): lax.all_to_all(col_part, BOTH, 0, 0, axis_index_groups=groups, tiled=True)  21.3 us
    all_to_all x1, waiting for transfers between devices, coupled_target(): lax.all_to_all(lax.optimization_barrier(spread), BOTH, 0, 0, axis_index_g...  9.53 us
    pallas_call x1, Pallas kernels, local(): pl.pallas_call(qkv_kernel, out_shape=shape((own * patch_count, count * co...  8.46 us
    all_to_all x1, starting transfers between devices, coupled_target(): lax.all_to_all(lax.optimization_barrier(spread), BOTH, 0, 0, axis_index_g...  7.78 us
    unnamed x38, local copies, waits for them, and re-layouts  4.78 us
    all_to_all x1, starting transfers between devices, coupled_target(): lax.all_to_all(col_part, BOTH, 0, 0, axis_index_groups=groups, tiled=True)  3.51 us
  transfers between devices with their start and end apart: 27, of which 18 were waited for; matrix products, arithmetic and copies ran while one was open for 2% of the time, Pallas kernels for 1%

profile of v3, /device:TPU:1, one launch (start us, length us, event | category | flops | bytes accessed | tf_op | source)
XLA Modules:
  0.0 150.1 jit_solution(5310076572493302389)
XLA Ops:
  0.6 2.6 %broadcast_in_dim.6 = bf16[16,32,2048]{2,1,0:T(8,128)(2,1)} broadcast(bf16[32,2048]{1,0:T(8,128)(2,1)} %param.8), dimensions={1,2} | broadcast | bytes 2228224 | tf_op jit(solution)/shard_map/broadcast_in_dim | solution.py:281
  3.2 7.8 %all-to-all-start = ((bf16[16,32,2048]{2,1,0:T(8,128)(2,1)}), bf16[16,32,2048]{2,1,0:T(8,128)(2,1)}, u32[]{:S(2)}, u32[]{:S(2)}) async-start(bf16[16,32,2048]{2,1,0:T(8,128)(2,1)} %broadcast_in_dim.6), calls=%async_computation | async-start | bytes 4194304 | tf_op jit(solution)/shard_map/all_to_all | solution.py:282
  11.0 1.0 collective-permute-start
  13.1 3.8 %collective-permute-start.3 = (bf16[2,32,2048]{2,1,0:T(8,128)(2,1)S(1)}, bf16[2,32,2048]{2,1,0:T(8,128)(2,1)S(1)}, u32[]{:S(2)}, u32[]{:S(2)}) collective-permute-start(bf16[2,32,2048]{2,1,0:T(8,128)(2,1)S(1)} %pad_maximum_fusion.4.a), channel_id=1, source_target_pairs={{0,18},{1,19},{2,16},{3,17},{4,22},{5,23},{6,20},{7,21},{8,26},{9,... | collective-permute-start | bytes 786440 | tf_op jit(solution)/shard_map/ppermute | solution.py:25
  17.8 11.3 %collective-permute-done.3.d = bf16[2,32,2048]{2,1,0:T(8,128)(2,1)S(1)} collective-permute-done((bf16[2,32,2048]{2,1,0:T(8,128)(2,1)S(1)}, bf16[2,32,2048]{2,1,0:T(8,128)(2,1)S(1)}, u32[]{:S(2)}, u32[]{:S(2)}) %collective-permute-start.3) | collective-permute-done | bytes 262176 | tf_op jit(solution)/shard_map/ppermute | solution.py:25
  29.4 9.5 %all-to-all-done.data_ref = bf16[16,32,2048]{2,1,0:T(8,128)(2,1)} async-done(((bf16[16,32,2048]{2,1,0:T(8,128)(2,1)}), bf16[16,32,2048]{2,1,0:T(8,128)(2,1)}, u32[]{:S(2)}, u32[]{:S(2)}) %all-to-all-start) | async-done | bytes 2097184 | tf_op jit(solution)/shard_map/all_to_all | solution.py:282
  39.0 2.8 %shard_map.86 = (f32[256,512]{1,0:T(8,128)S(1)}, f32[8,128]{1,0:T(8,128)S(1)}) custom-call(s32[4]{0:T(128)S(1)} %pad_add_fusion.place, bf16[16,32,2048]{2,1,0:T(8,128)(2,1)} %all-to-all-done.data_ref, bf16[2,32,2048]{2,1,0:T(8,128)(2,1)S(1)} %pad_maximum_fusion.4.a, bf16[2,32,2048]{2,1,0:T(8,128)(2,1)S(1)} %collective-permute-done.1.b, ...), custom_call_target="tpu_custom_call" | custom-call | flops 536870912 | bytes 4194304 | tf_op jit(solution)/shard_map/pallas_call | solution.py:286
  41.7 3.5 %collective-permute-start.5 = (f32[8,128]{1,0:T(8,128)S(1)}, f32[8,128]{1,0:T(8,128)S(1)}, u32[]{:S(2)}, u32[]{:S(2)}) collective-permute-start(f32[8,128]{1,0:T(8,128)S(1)} %get-tuple-element.32), channel_id=1, source_target_pairs={{0,1},{1,0},{2,3},{3,2},{4,5},{5,4},{6,7},{7,6},{8,9},{9,8},{10,11... | collective-permute-start | bytes 12296 | tf_op jit(solution)/shard_map/ppermute | solution.py:25
  45.4 0.7 collective-permute-done.5
  46.1 3.8 %collective-permute-start.8 = (f32[8,128]{1,0:T(8,128)S(1)}, f32[8,128]{1,0:T(8,128)S(1)}, u32[]{:S(2)}, u32[]{:S(2)}) collective-permute-start(f32[8,128]{1,0:T(8,128)S(1)} %log_add_fusion.2.a), channel_id=1, source_target_pairs={{0,18},{1,19},{2,16},{3,17},{4,22},{5,23},{6,20},{7,21},{8,26},{9,... | collective-permute-start | bytes 12296 | tf_op jit(solution)/shard_map/ppermute | solution.py:25
  50.9 3.0 %collective-permute-done.7.c = f32[8,128]{1,0:T(8,128)S(1)} collective-permute-done((f32[8,128]{1,0:T(8,128)S(1)}, f32[8,128]{1,0:T(8,128)S(1)}, u32[]{:S(2)}, u32[]{:S(2)}) %collective-permute-start.7) | collective-permute-done | bytes 4128 | tf_op jit(solution)/shard_map/ppermute | solution.py:25
  53.9 0.9 shard_map.87
  54.9 3.5 %all-to-all-start.1 = ((f32[16,8,128]{2,1,0:T(8,128)}), f32[16,8,128]{2,1,0:T(8,128)S(1)}, u32[]{:S(2)}, u32[]{:S(2)}) async-start(f32[16,8,128]{2,1,0:T(8,128)} %shard_map.87), calls=%async_computation.1 | async-start | bytes 131072 | tf_op jit(solution)/shard_map/all_to_all | solution.py:313
  58.5 3.3 %collective-permute-done.9 = bf16[2,192,384]{2,1,0:T(8,128)(2,1)} collective-permute-done((bf16[2,192,384]{2,1,0:T(8,128)(2,1)S(1)}, bf16[2,192,384]{2,1,0:T(8,128)(2,1)}, u32[]{:S(2)}, u32[]{:S(2)}) %collective-permute-start.9) | collective-permute-done | bytes 294944 | tf_op jit(solution)/shard_map/ppermute | solution.py:25
  61.8 1.0 pad_maximum_fusion.f0
  62.8 2.2 %all-to-all-done.1.parts_ref = f32[16,8,128]{2,1,0:T(8,128)S(1)} async-done(((f32[16,8,128]{2,1,0:T(8,128)}), f32[16,8,128]{2,1,0:T(8,128)S(1)}, u32[]{:S(2)}, u32[]{:S(2)}) %all-to-all-start.1) | async-done | bytes 65568 | tf_op jit(solution)/shard_map/all_to_all | solution.py:313
  65.2 1.0 collective-permute-start.11
  66.3 3.5 %collective-permute-start.12 = (f32[8,128]{1,0:T(8,128)S(1)}, f32[8,128]{1,0:T(8,128)S(1)}, u32[]{:S(2)}, u32[]{:S(2)}) collective-permute-start(f32[8,128]{1,0:T(8,128)S(1)} %shard_map.88), channel_id=1, source_target_pairs={{0,1},{1,0},{2,3},{3,2},{4,5},{5,4},{6,7},{7,6},{8,9},{9,8},{10,11... | collective-permute-start | bytes 12296 | tf_op jit(solution)/shard_map/ppermute | solution.py:25
  69.7 0.8 collective-permute-done.12
  70.6 2.4 %collective-permute-start.15 = (f32[8,128]{1,0:T(8,128)S(1)}, f32[8,128]{1,0:T(8,128)S(1)}, u32[]{:S(2)}, u32[]{:S(2)}) collective-permute-start(f32[8,128]{1,0:T(8,128)S(1)} %log_add_fusion.1.a), channel_id=1, source_target_pairs={{0,18},{1,19},{2,16},{3,17},{4,22},{5,23},{6,20},{7,21},{8,26},{9,... | collective-permute-start | bytes 12296 | tf_op jit(solution)/shard_map/ppermute | solution.py:25
  72.9 1.2 collective-permute-start.14
  74.6 2.3 %collective-permute-done.14.c = f32[8,128]{1,0:T(8,128)S(1)} collective-permute-done((f32[8,128]{1,0:T(8,128)S(1)}, f32[8,128]{1,0:T(8,128)S(1)}, u32[]{:S(2)}, u32[]{:S(2)}) %collective-permute-start.14) | collective-permute-done | bytes 4128 | tf_op jit(solution)/shard_map/ppermute | solution.py:25
  77.2 11.4 %all_to_all.24.parts_ref = f32[16,8,128]{2,1,0:T(8,128)S(1)} all-to-all(f32[16,8,128]{2,1,0:T(8,128)S(1)} %shard_map.89), channel_id=1, replica_groups={{0,4,8,12,32,36,40,44,64,68,72,76,96,100,104,108},{1,5,9,13,33,37,41,45..., dimensions={0} | all-to-all | bytes 131072 | tf_op jit(solution)/shard_map/all_to_all | solution.py:313
  88.9 1.2 collective-permute-start.16
  90.1 3.5 %collective-permute-start.17 = (f32[8,128]{1,0:T(8,128)S(1)}, f32[8,128]{1,0:T(8,128)S(1)}, u32[]{:S(2)}, u32[]{:S(2)}) collective-permute-start(f32[8,128]{1,0:T(8,128)S(1)} %shard_map.90), channel_id=1, source_target_pairs={{0,1},{1,0},{2,3},{3,2},{4,5},{5,4},{6,7},{7,6},{8,9},{9,8},{10,11... | collective-permute-start | bytes 12296 | tf_op jit(solution)/shard_map/ppermute | solution.py:25
  93.5 0.8 collective-permute-done.17
  94.4 0.8 collective-permute-start.20
  95.1 1.2 collective-permute-start.19
  96.3 1.4 collective-permute-start.18
  98.4 1.0 collective-permute-done.19.c
  99.7 9.9 %all_to_all.25.parts_ref = f32[16,8,128]{2,1,0:T(8,128)S(1)} all-to-all(f32[16,8,128]{2,1,0:T(8,128)S(1)} %shard_map.91), channel_id=1, replica_groups={{0,4,8,12,32,36,40,44,64,68,72,76,96,100,104,108},{1,5,9,13,33,37,41,45..., dimensions={0} | all-to-all | bytes 131072 | tf_op jit(solution)/shard_map/all_to_all | solution.py:313
  109.6 0.8 copy-done.3
  110.4 2.6 %shard_map.92 = (f32[4,32,2048]{2,1,0:T(8,128)S(1)}, f32[4,32,128]{2,1,0:T(8,128)S(1)}, bf16[4,32,2176]{2,1,0:T(8,128)(2,1)S(1)}) custom-call(s32[4]{0:T(128)S(1)} %pad_add_fusion.place, f32[256,512]{1,0:T(8,128)S(1)} %get-tuple-element.29.cost_ref, bf16[16,32,2048]{2,1,0:T(8,128)(2,1)} %all-to-all-done.data_ref, f32[16,8,128]{2,1,0:T(8,128)S(1)} %all_to_all.25.parts_ref), custom_call_target="tpu_custom_call" | custom-call | flops 536870912 | bytes 6291456 | tf_op jit(solution)/shard_map/pallas_call | solution.py:329
  113.0 3.3 %collective-permute-start.21 = (bf16[4,32,2176]{2,1,0:T(8,128)(2,1)S(1)}, bf16[4,32,2176]{2,1,0:T(8,128)(2,1)S(1)}, u32[]{:S(2)}, u32[]{:S(2)}) collective-permute-start(bf16[4,32,2176]{2,1,0:T(8,128)(2,1)S(1)} %get-tuple-element.45), channel_id=1, source_target_pairs={{0,1},{1,0},{2,3},{3,2},{4,5},{5,4},{6,7},{7,6},{8,9},{9,8},{10,11... | collective-permute-start | bytes 1671176 | tf_op jit(solution)/shard_map/ppermute | solution.py:25
  116.4 1.5 %collective-permute-done.21.got_ref = bf16[4,32,2176]{2,1,0:T(8,128)(2,1)S(1)} collective-permute-done((bf16[4,32,2176]{2,1,0:T(8,128)(2,1)S(1)}, bf16[4,32,2176]{2,1,0:T(8,128)(2,1)S(1)}, u32[]{:S(2)}, u32[]{:S(2)}) %collective-permute-start.21) | collective-permute-done | bytes 557088 | tf_op jit(solution)/shard_map/ppermute | solution.py:25
  117.9 1.1 shard_map.93
  119.7 1.3 collective-permute-start.22
  121.0 1.8 %collective-permute-start.23 = (bf16[32,2176]{1,0:T(8,128)(2,1)}, bf16[32,2176]{1,0:T(8,128)(2,1)}, u32[]{:S(2)}, u32[]{:S(2)}) collective-permute-start(bf16[32,2176]{1,0:T(8,128)(2,1)} %get-tuple-element.49), channel_id=1, source_target_pairs={{0,16},{1,17},{2,18},{3,19},{4,20},{5,21},{6,22},{7,23},{8,24},{9,... | collective-permute-start | bytes 417800 | tf_op jit(solution)/shard_map/ppermute | solution.py:25
  123.7 0.7 copy.10.time_ref
  125.0 4.6 %collective-permute-done.23.b = bf16[32,2176]{1,0:T(8,128)(2,1)} collective-permute-done((bf16[32,2176]{1,0:T(8,128)(2,1)}, bf16[32,2176]{1,0:T(8,128)(2,1)}, u32[]{:S(2)}, u32[]{:S(2)}) %collective-permute-start.23) | collective-permute-done | bytes 139296 | tf_op jit(solution)/shard_map/ppermute | solution.py:25
  129.6 2.5 %collective-permute-done.24.c = bf16[32,2176]{1,0:T(8,128)(2,1)} collective-permute-done((bf16[32,2176]{1,0:T(8,128)(2,1)}, bf16[32,2176]{1,0:T(8,128)(2,1)}, u32[]{:S(2)}, u32[]{:S(2)}) %collective-permute-start.24) | collective-permute-done | bytes 139296 | tf_op jit(solution)/shard_map/ppermute | solution.py:25
  132.1 0.9 copy-done.6
  133.0 0.9 copy-done.8
  134.7 2.0 %shard_map.94 = (bf16[32,2048]{1,0:T(8,128)(2,1)}, bf16[32,2048]{1,0:T(8,128)(2,1)S(1)}) custom-call(f32[32,2048]{1,0:T(8,128)S(1)} %copy-done.8, f32[32,128]{1,0:T(8,128)S(1)} %copy-done.11, bf16[32,2176]{1,0:T(8,128)(2,1)} %collective-permute-done.22.a, bf16[32,2176]{1,0:T(8,128)(2,1)} %collective-permute-done.23.b, ...), custom_call_target="tpu_custom_call" | custom-call | bytes 1048576 | tf_op jit(solution)/shard_map/pallas_call | solution.py:353
  137.3 1.9 %reshape.28 = bf16[1024,64]{1,0:T(8,128)(2,1)} reshape(bf16[32,2048]{1,0:T(8,128)(2,1)} %copy-done.9) | data formatting | bytes 262144 | tf_op jit(solution)/shard_map/reshape | solution.py:368
  139.2 0.8 tile.13
  140.1 1.5 %pad_maximum_fusion.1.tokens_ref = bf16[1024,192]{1,0:T(8,128)(2,1)S(1)} fusion(bf16[1024,32]{1,0:T(8,128)(2,1)S(1)} %bitcast.14, bf16[1024,64]{1,0:T(8,128)(2,1)} %reshape.28), kind=kLoop, calls=%fused_computation.9 | loop fusion | flops 1572864 | bytes 589824 | tf_op jit(solution)/shard_map/concatenate | solution.py:370
  141.6 8.5 %shard_map.95 = bf16[1024,6144]{1,0:T(8,128)(2,1)} custom-call(s32[4]{0:T(128)S(1)} %copy-done.13, bf16[1024,192]{1,0:T(8,128)(2,1)S(1)} %pad_maximum_fusion.1.tokens_ref, bf16[192,2048]{1,0:T(8,128)(2,1)S(1)} %maximum_maximum_fusion.table_ref, bf16[4,192,384]{2,1,0:T(8,128)(2,1)S(1)} %pad_maximum_fusion.f0, bf16[4,192,384]{2,1,0:T(8,128)(2,1)S(1)} %copy-done.2, ...), custom_call_target="tpu_custom_call" | custom-call | flops 2415919104 | bytes 16777216 | tf_op jit(solution)/shard_map/pallas_call | solution.py:377
  (76 shorter events, 9.3 us)
Async XLA Ops:
  0.6 11.6 %copy-start = (bf16[2048,384]{1,0:T(8,128)(2,1)S(1)}, bf16[2048,384]{1,0:T(8,128)(2,1)}, u32[]{:S(2)}) copy-start(bf16[2048,384]{1,0:T(8,128)(2,1)} %param.13) | copy-start | bytes 4718596
  3.2 7.8 %copy-start.5 = (bf16[32,2048]{1,0:T(8,128)(2,1)S(1)}, bf16[32,2048]{1,0:T(8,128)(2,1)}, u32[]{:S(2)}) copy-start(bf16[32,2048]{1,0:T(8,128)(2,1)} %noise_ref.1) | copy-start | bytes 393220
  3.2 8.8 %copy-start.14 = (bf16[64,2048]{1,0:T(8,128)(2,1)S(1)}, bf16[64,2048]{1,0:T(8,128)(2,1)}, u32[]{:S(2)}) copy-start(bf16[64,2048]{1,0:T(8,128)(2,1)} %param.10) | copy-start | bytes 786436
  3.2 8.8 %copy-start.16 = (bf16[32,2048]{1,0:T(8,128)(2,1)S(1)}, bf16[32,2048]{1,0:T(8,128)(2,1)}, u32[]{:S(2)}) copy-start(bf16[32,2048]{1,0:T(8,128)(2,1)} %param.11) | copy-start | bytes 393220
  3.2 8.8 %copy-start.18 = (f32[2048]{0:T(1024)S(1)}, f32[2048]{0:T(1024)}, u32[]{:S(2)}) copy-start(f32[2048]{0:T(1024)} %param.12) | copy-start | bytes 24580
  3.2 35.7 %all-to-all-start = ((bf16[16,32,2048]{2,1,0:T(8,128)(2,1)}), bf16[16,32,2048]{2,1,0:T(8,128)(2,1)}, u32[]{:S(2)}, u32[]{:S(2)}) async-start(bf16[16,32,2048]{2,1,0:T(8,128)(2,1)} %broadcast_in_dim.6), calls=%async_computation | async-start | bytes 4194304 | tf_op jit(solution)/shard_map/all_to_all | solution.py:282
  11.0 2.0 %collective-permute-start = (bf16[32,2048]{1,0:T(8,128)(2,1)S(1)}, bf16[32,2048]{1,0:T(8,128)(2,1)S(1)}, u32[]{:S(2)}, u32[]{:S(2)}) collective-permute-start(bf16[32,2048]{1,0:T(8,128)(2,1)S(1)} %copy-done.5), channel_id=1, source_target_pairs={{0,1},{1,0},{2,3},{3,2},{4,5},{5,4},{6,7},{7,6},{8,9},{9,8},{10,11... | collective-permute-start | bytes 393224 | tf_op jit(solution)/shard_map/ppermute | solution.py:25
  13.1 15.9 %collective-permute-start.3 = (bf16[2,32,2048]{2,1,0:T(8,128)(2,1)S(1)}, bf16[2,32,2048]{2,1,0:T(8,128)(2,1)S(1)}, u32[]{:S(2)}, u32[]{:S(2)}) collective-permute-start(bf16[2,32,2048]{2,1,0:T(8,128)(2,1)S(1)} %pad_maximum_fusion.4.a), channel_id=1, source_target_pairs={{0,18},{1,19},{2,16},{3,17},{4,22},{5,23},{6,20},{7,21},{8,26},{9,... | collective-permute-start | bytes 786440 | tf_op jit(solution)/shard_map/ppermute | solution.py:25
  16.9 12.1 %collective-permute-start.2 = (bf16[2,32,2048]{2,1,0:T(8,128)(2,1)S(1)}, bf16[2,32,2048]{2,1,0:T(8,128)(2,1)S(1)}, u32[]{:S(2)}, u32[]{:S(2)}) collective-permute-start(bf16[2,32,2048]{2,1,0:T(8,128)(2,1)S(1)} %pad_maximum_fusion.4.a), channel_id=1, source_target_pairs={{0,16},{1,17},{2,18},{3,19},{4,20},{5,21},{6,22},{7,23},{8,24},{9,... | collective-permute-start | bytes 786440 | tf_op jit(solution)/shard_map/ppermute | solution.py:25
  16.9 12.5 %collective-permute-start.1 = (bf16[2,32,2048]{2,1,0:T(8,128)(2,1)S(1)}, bf16[2,32,2048]{2,1,0:T(8,128)(2,1)S(1)}, u32[]{:S(2)}, u32[]{:S(2)}) collective-permute-start(bf16[2,32,2048]{2,1,0:T(8,128)(2,1)S(1)} %pad_maximum_fusion.4.a), channel_id=1, source_target_pairs={{0,2},{1,3},{2,0},{3,1},{4,6},{5,7},{6,4},{7,5},{8,10},{9,11},{10,... | collective-permute-start | bytes 786440 | tf_op jit(solution)/shard_map/ppermute | solution.py:25
  17.7 91.9 %copy-start.12 = (s32[4]{0:T(128)}, s32[4]{0:T(128)S(1)}, u32[]{:S(2)}) copy-start(s32[4]{0:T(128)S(1)} %pad_add_fusion.place) | copy-start | bytes 52
  41.7 4.4 %collective-permute-start.5 = (f32[8,128]{1,0:T(8,128)S(1)}, f32[8,128]{1,0:T(8,128)S(1)}, u32[]{:S(2)}, u32[]{:S(2)}) collective-permute-start(f32[8,128]{1,0:T(8,128)S(1)} %get-tuple-element.32), channel_id=1, source_target_pairs={{0,1},{1,0},{2,3},{3,2},{4,5},{5,4},{6,7},{7,6},{8,9},{9,8},{10,11... | collective-permute-start | bytes 12296 | tf_op jit(solution)/shard_map/ppermute | solution.py:25
  45.3 9.5 %collective-permute-start.4 = (bf16[192,384]{1,0:T(8,128)(2,1)S(1)}, bf16[192,384]{1,0:T(8,128)(2,1)S(1)}, u32[]{:S(2)}, u32[]{:S(2)}) collective-permute-start(bf16[192,384]{1,0:T(8,128)(2,1)S(1)} %pad_maximum_fusion.5), channel_id=1, source_target_pairs={{0,1},{1,0},{2,3},{3,2},{4,5},{5,4},{6,7},{7,6},{8,9},{9,8},{10,11... | collective-permute-start | bytes 442376 | tf_op jit(solution)/shard_map/ppermute | solution.py:25
  46.1 4.8 %collective-permute-start.8 = (f32[8,128]{1,0:T(8,128)S(1)}, f32[8,128]{1,0:T(8,128)S(1)}, u32[]{:S(2)}, u32[]{:S(2)}) collective-permute-start(f32[8,128]{1,0:T(8,128)S(1)} %log_add_fusion.2.a), channel_id=1, source_target_pairs={{0,18},{1,19},{2,16},{3,17},{4,22},{5,23},{6,20},{7,21},{8,26},{9,... | collective-permute-start | bytes 12296 | tf_op jit(solution)/shard_map/ppermute | solution.py:25
  49.9 4.0 %collective-permute-start.7 = (f32[8,128]{1,0:T(8,128)S(1)}, f32[8,128]{1,0:T(8,128)S(1)}, u32[]{:S(2)}, u32[]{:S(2)}) collective-permute-start(f32[8,128]{1,0:T(8,128)S(1)} %log_add_fusion.2.a), channel_id=1, source_target_pairs={{0,16},{1,17},{2,18},{3,19},{4,20},{5,21},{6,22},{7,23},{8,24},{9,... | collective-permute-start | bytes 12296 | tf_op jit(solution)/shard_map/ppermute | solution.py:25
  49.9 4.0 %collective-permute-start.6 = (f32[8,128]{1,0:T(8,128)S(1)}, f32[8,128]{1,0:T(8,128)S(1)}, u32[]{:S(2)}, u32[]{:S(2)}) collective-permute-start(f32[8,128]{1,0:T(8,128)S(1)} %log_add_fusion.2.a), channel_id=1, source_target_pairs={{0,2},{1,3},{2,0},{3,1},{4,6},{5,7},{6,4},{7,5},{8,10},{9,11},{10,... | collective-permute-start | bytes 12296 | tf_op jit(solution)/shard_map/ppermute | solution.py:25
  54.8 6.9 %collective-permute-start.9 = (bf16[2,192,384]{2,1,0:T(8,128)(2,1)S(1)}, bf16[2,192,384]{2,1,0:T(8,128)(2,1)}, u32[]{:S(2)}, u32[]{:S(2)}) collective-permute-start(bf16[2,192,384]{2,1,0:T(8,128)(2,1)S(1)} %pad_maximum_fusion.3), channel_id=1, source_target_pairs={{0,2},{1,3},{2,0},{3,1},{4,6},{5,7},{6,4},{7,5},{8,10},{9,11},{10,... | collective-permute-start | bytes 884744 | tf_op jit(solution)/shard_map/ppermute | solution.py:25
  54.9 10.0 %all-to-all-start.1 = ((f32[16,8,128]{2,1,0:T(8,128)}), f32[16,8,128]{2,1,0:T(8,128)S(1)}, u32[]{:S(2)}, u32[]{:S(2)}) async-start(f32[16,8,128]{2,1,0:T(8,128)} %shard_map.87), calls=%async_computation.1 | async-start | bytes 131072 | tf_op jit(solution)/shard_map/all_to_all | solution.py:313
  65.2 23.3 %collective-permute-start.11 = (bf16[4,192,384]{2,1,0:T(8,128)(2,1)S(1)}, bf16[4,192,384]{2,1,0:T(8,128)(2,1)S(1)}, u32[]{:S(2)}, u32[]{:S(2)}) collective-permute-start(bf16[4,192,384]{2,1,0:T(8,128)(2,1)S(1)} %pad_maximum_fusion.f0), channel_id=1, source_target_pairs={{0,12},{1,13},{2,14},{3,15},{4,8},{5,9},{6,10},{7,11},{8,4},{9,5},... | collective-permute-start | bytes 1769480 | tf_op jit(solution)/shard_map/ppermute | solution.py:25
  66.3 22.3 %collective-permute-start.10 = (bf16[4,192,384]{2,1,0:T(8,128)(2,1)S(1)}, bf16[4,192,384]{2,1,0:T(8,128)(2,1)S(1)}, u32[]{:S(2)}, u32[]{:S(2)}) collective-permute-start(bf16[4,192,384]{2,1,0:T(8,128)(2,1)S(1)} %pad_maximum_fusion.f0), channel_id=1, source_target_pairs={{0,4},{1,5},{2,6},{3,7},{4,0},{5,1},{6,2},{7,3},{8,12},{9,13},{10,... | collective-permute-start | bytes 1769480 | tf_op jit(solution)/shard_map/ppermute | solution.py:25
  66.3 4.3 %collective-permute-start.12 = (f32[8,128]{1,0:T(8,128)S(1)}, f32[8,128]{1,0:T(8,128)S(1)}, u32[]{:S(2)}, u32[]{:S(2)}) collective-permute-start(f32[8,128]{1,0:T(8,128)S(1)} %shard_map.88), channel_id=1, source_target_pairs={{0,1},{1,0},{2,3},{3,2},{4,5},{5,4},{6,7},{7,6},{8,9},{9,8},{10,11... | collective-permute-start | bytes 12296 | tf_op jit(solution)/shard_map/ppermute | solution.py:25
  70.6 4.0 %collective-permute-start.15 = (f32[8,128]{1,0:T(8,128)S(1)}, f32[8,128]{1,0:T(8,128)S(1)}, u32[]{:S(2)}, u32[]{:S(2)}) collective-permute-start(f32[8,128]{1,0:T(8,128)S(1)} %log_add_fusion.1.a), channel_id=1, source_target_pairs={{0,18},{1,19},{2,16},{3,17},{4,22},{5,23},{6,20},{7,21},{8,26},{9,... | collective-permute-start | bytes 12296 | tf_op jit(solution)/shard_map/ppermute | solution.py:25
  72.9 4.0 %collective-permute-start.14 = (f32[8,128]{1,0:T(8,128)S(1)}, f32[8,128]{1,0:T(8,128)S(1)}, u32[]{:S(2)}, u32[]{:S(2)}) collective-permute-start(f32[8,128]{1,0:T(8,128)S(1)} %log_add_fusion.1.a), channel_id=1, source_target_pairs={{0,16},{1,17},{2,18},{3,19},{4,20},{5,21},{6,22},{7,23},{8,24},{9,... | collective-permute-start | bytes 12296 | tf_op jit(solution)/shard_map/ppermute | solution.py:25
  74.1 2.8 %collective-permute-start.13 = (f32[8,128]{1,0:T(8,128)S(1)}, f32[8,128]{1,0:T(8,128)S(1)}, u32[]{:S(2)}, u32[]{:S(2)}) collective-permute-start(f32[8,128]{1,0:T(8,128)S(1)} %log_add_fusion.1.a), channel_id=1, source_target_pairs={{0,2},{1,3},{2,0},{3,1},{4,6},{5,7},{6,4},{7,5},{8,10},{9,11},{10,... | collective-permute-start | bytes 12296 | tf_op jit(solution)/shard_map/ppermute | solution.py:25
  88.6 21.0 %copy-start.1 = (bf16[4,192,384]{2,1,0:T(8,128)(2,1)}, bf16[4,192,384]{2,1,0:T(8,128)(2,1)S(1)}, u32[]{:S(2)}) copy-start(bf16[4,192,384]{2,1,0:T(8,128)(2,1)S(1)} %collective-permute-done.10.f1) | copy-start | bytes 1769476
  88.9 20.7 %collective-permute-start.16 = (bf16[4,192,384]{2,1,0:T(8,128)(2,1)S(1)}, bf16[4,192,384]{2,1,0:T(8,128)(2,1)S(1)}, u32[]{:S(2)}, u32[]{:S(2)}) collective-permute-start(bf16[4,192,384]{2,1,0:T(8,128)(2,1)S(1)} %pad_maximum_fusion.f0), channel_id=1, source_target_pairs={{0,8},{1,9},{2,10},{3,11},{4,12},{5,13},{6,14},{7,15},{8,0},{9,1},... | collective-permute-start | bytes 1769480 | tf_op jit(solution)/shard_map/ppermute | solution.py:25
  90.1 4.3 %collective-permute-start.17 = (f32[8,128]{1,0:T(8,128)S(1)}, f32[8,128]{1,0:T(8,128)S(1)}, u32[]{:S(2)}, u32[]{:S(2)}) collective-permute-start(f32[8,128]{1,0:T(8,128)S(1)} %shard_map.90), channel_id=1, source_target_pairs={{0,1},{1,0},{2,3},{3,2},{4,5},{5,4},{6,7},{7,6},{8,9},{9,8},{10,11... | collective-permute-start | bytes 12296 | tf_op jit(solution)/shard_map/ppermute | solution.py:25
  94.4 4.0 %collective-permute-start.20 = (f32[8,128]{1,0:T(8,128)S(1)}, f32[8,128]{1,0:T(8,128)S(1)}, u32[]{:S(2)}, u32[]{:S(2)}) collective-permute-start(f32[8,128]{1,0:T(8,128)S(1)} %log_add_fusion.a), channel_id=1, source_target_pairs={{0,18},{1,19},{2,16},{3,17},{4,22},{5,23},{6,20},{7,21},{8,26},{9,... | collective-permute-start | bytes 12296 | tf_op jit(solution)/shard_map/ppermute | solution.py:25
  95.1 4.3 %collective-permute-start.19 = (f32[8,128]{1,0:T(8,128)S(1)}, f32[8,128]{1,0:T(8,128)S(1)}, u32[]{:S(2)}, u32[]{:S(2)}) collective-permute-start(f32[8,128]{1,0:T(8,128)S(1)} %log_add_fusion.a), channel_id=1, source_target_pairs={{0,16},{1,17},{2,18},{3,19},{4,20},{5,21},{6,22},{7,23},{8,24},{9,... | collective-permute-start | bytes 12296 | tf_op jit(solution)/shard_map/ppermute | solution.py:25
  96.3 3.1 %collective-permute-start.18 = (f32[8,128]{1,0:T(8,128)S(1)}, f32[8,128]{1,0:T(8,128)S(1)}, u32[]{:S(2)}, u32[]{:S(2)}) collective-permute-start(f32[8,128]{1,0:T(8,128)S(1)} %log_add_fusion.a), channel_id=1, source_target_pairs={{0,2},{1,3},{2,0},{3,1},{4,6},{5,7},{6,4},{7,5},{8,10},{9,11},{10,... | collective-permute-start | bytes 12296 | tf_op jit(solution)/shard_map/ppermute | solution.py:25
  109.6 13.9 %copy-start.15 = (bf16[64,2048]{1,0:T(8,128)(2,1)S(1)}, bf16[64,2048]{1,0:T(8,128)(2,1)}, u32[]{:S(2)}) copy-start(bf16[64,2048]{1,0:T(8,128)(2,1)} %param.10) | copy-start | bytes 786436
  109.6 13.9 %copy-start.17 = (bf16[32,2048]{1,0:T(8,128)(2,1)S(1)}, bf16[32,2048]{1,0:T(8,128)(2,1)}, u32[]{:S(2)}) copy-start(bf16[32,2048]{1,0:T(8,128)(2,1)} %param.11) | copy-start | bytes 393220
  109.6 0.8 copy-start.3
  113.0 4.9 %collective-permute-start.21 = (bf16[4,32,2176]{2,1,0:T(8,128)(2,1)S(1)}, bf16[4,32,2176]{2,1,0:T(8,128)(2,1)S(1)}, u32[]{:S(2)}, u32[]{:S(2)}) collective-permute-start(bf16[4,32,2176]{2,1,0:T(8,128)(2,1)S(1)} %get-tuple-element.45), channel_id=1, source_target_pairs={{0,1},{1,0},{2,3},{3,2},{4,5},{5,4},{6,7},{7,6},{8,9},{9,8},{10,11... | collective-permute-start | bytes 1671176 | tf_op jit(solution)/shard_map/ppermute | solution.py:25
  118.9 0.7 copy-start.7
  119.7 4.0 %copy-start.10 = (f32[32,128]{1,0:T(8,128)}, f32[32,128]{1,0:T(8,128)S(1)}, u32[]{:S(2)}) copy-start(f32[32,128]{1,0:T(8,128)S(1)} %get-tuple-element.47.log_ref) | copy-start | bytes 49156
  119.7 5.4 %collective-permute-start.22 = (bf16[32,2176]{1,0:T(8,128)(2,1)}, bf16[32,2176]{1,0:T(8,128)(2,1)}, u32[]{:S(2)}, u32[]{:S(2)}) collective-permute-start(bf16[32,2176]{1,0:T(8,128)(2,1)} %get-tuple-element.48), channel_id=1, source_target_pairs={{0,2},{1,3},{2,0},{3,1},{4,6},{5,7},{6,4},{7,5},{8,10},{9,11},{10,... | collective-permute-start | bytes 417800 | tf_op jit(solution)/shard_map/ppermute | solution.py:25
  121.0 8.6 %collective-permute-start.23 = (bf16[32,2176]{1,0:T(8,128)(2,1)}, bf16[32,2176]{1,0:T(8,128)(2,1)}, u32[]{:S(2)}, u32[]{:S(2)}) collective-permute-start(bf16[32,2176]{1,0:T(8,128)(2,1)} %get-tuple-element.49), channel_id=1, source_target_pairs={{0,16},{1,17},{2,18},{3,19},{4,20},{5,21},{6,22},{7,23},{8,24},{9,... | collective-permute-start | bytes 417800 | tf_op jit(solution)/shard_map/ppermute | solution.py:25
  122.8 9.2 %collective-permute-start.24 = (bf16[32,2176]{1,0:T(8,128)(2,1)}, bf16[32,2176]{1,0:T(8,128)(2,1)}, u32[]{:S(2)}, u32[]{:S(2)}) collective-permute-start(bf16[32,2176]{1,0:T(8,128)(2,1)} %get-tuple-element.50), channel_id=1, source_target_pairs={{0,18},{1,19},{2,16},{3,17},{4,22},{5,23},{6,20},{7,21},{8,26},{9,... | collective-permute-start | bytes 417800 | tf_op jit(solution)/shard_map/ppermute | solution.py:25
  132.1 0.9 copy-start.6
  133.0 0.9 copy-start.8
  133.9 0.7 copy-start.11
  136.7 0.6 copy-start.9
  137.3 4.2 %copy-start.13 = (s32[4]{0:T(128)S(1)}, s32[4]{0:T(128)}, u32[]{:S(2)}) copy-start(s32[4]{0:T(128)} %copy-done.12) | copy-start | bytes 52
  139.2 2.4 %copy-start.2 = (bf16[4,192,384]{2,1,0:T(8,128)(2,1)S(1)}, bf16[4,192,384]{2,1,0:T(8,128)(2,1)}, u32[]{:S(2)}) copy-start(bf16[4,192,384]{2,1,0:T(8,128)(2,1)} %copy-done.1) | copy-start | bytes 1769476
  139.2 2.4 %copy-start.4 = (bf16[4,192,384]{2,1,0:T(8,128)(2,1)S(1)}, bf16[4,192,384]{2,1,0:T(8,128)(2,1)}, u32[]{:S(2)}) copy-start(bf16[4,192,384]{2,1,0:T(8,128)(2,1)} %copy-done.3) | copy-start | bytes 1769476

commit v4 on v3

--- a/solution.py
+++ b/solution.py
@@ -11,6 +11,7 @@
 TGRID = 1000
 BOTH = ("src", "tgt")
 CORE = 1
+ROW_MASK, COL_MASK = 108, 19
 Z_STEPS = (2, 16, 18)
 Y_STEPS = (4, 8, 12)
 X_STEPS = (32, 64, 96)
@@ -25,11 +26,15 @@
     return lax.ppermute(value, BOTH, [(i, i ^ mask) for i in range(128)])
 
 
-def column_groups():
+def groups_by(mask):
     groups = {}
     for i in range(128):
-        groups.setdefault(((i >> 4) & 1, i & 3), []).append(i)
+        groups.setdefault(i & mask, []).append(i)
     return [groups[key] for key in sorted(groups)]
+
+
+def exchange(value, mask):
+    return lax.all_to_all(value, BOTH, 0, 0, axis_index_groups=groups_by(mask), tiled=True)
 
 
 def vmem_call(kernel, out_shape, scratch=(), smem=0, inputs=0, flops=0, nbytes=0):
@@ -98,9 +103,16 @@
 
 
 def pack(lse, out_ref):
-    out_ref[...] = jnp.zeros(out_ref.shape, F32)
+    place = lax.broadcasted_iota(jnp.int32, (8, 128), 0)
+    packed = jnp.zeros((8, 128), F32)
     for part in range(lse.shape[0] // 128):
-        out_ref[part : part + 1, :] = to_lanes(lse[part * 128 : part * 128 + 128])
+        packed = jnp.where(place == part, to_lanes(lse[part * 128 : part * 128 + 128]), packed)
+    out_ref[...] = jnp.broadcast_to(packed[None], out_ref.shape)
+
+
+def spread_lse(parts):
+    peak = jnp.max(parts, axis=0)
+    return peak + jnp.log(jnp.sum(jnp.exp(parts - peak[None]), axis=0))
 
 
 def cost_kernel(place, data_ref, a, b, c, d, cost_ref, lse_ref, noise_ref):
@@ -133,9 +145,9 @@
     pack(row_lse(cost_ref, None, 1.0 / epsilon_of(0)), lse_ref)
 
 
-def col_kernel(step, cost_ref, a, b, c, d, out_ref):
+def col_kernel(step, cost_ref, parts_ref, out_ref):
     epsilon = epsilon_of(step)
-    joined = -epsilon * join_lse([a[...], b[...], c[...], d[...]])
+    joined = -epsilon * spread_lse(parts_ref[...])
     halfway = cost_ref.shape[0] // 2
     inverse = 1.0 / epsilon
     upper = (to_rows(joined[0:1, :]) - cost_ref[0:halfway, :]) * inverse
@@ -153,10 +165,7 @@
 
 
 def col_potential(step, parts_ref):
-    parts = parts_ref[...]
-    peak = jnp.max(parts, axis=0)
-    total = jnp.sum(jnp.exp(parts - peak[None]), axis=0)
-    return -epsilon_of(step) * (peak + jnp.log(total))
+    return -epsilon_of(step) * spread_lse(parts_ref[...])
 
 
 def row_kernel(step, cost_ref, parts_ref, lse_ref):
@@ -218,41 +227,88 @@
             out[:, latent : latent + 128] = packed_log(total)
 
 
-def finish_kernel(own_ref, log_ref, a, b, c, noise_ref, time_ref, velocity_ref, mixed_ref):
-    latent = own_ref.shape[1]
-    logs = [log_ref[...]] + [
-        jnp.broadcast_to(read_log(got[:, latent : latent + 128]), log_ref.shape)
-        for got in (a, b, c)
+def spread_kernel(value_ref, out_ref, sems):
+    copies = [
+        pltpu.make_async_copy(value_ref, out_ref.at[k], sems.at[k])
+        for k in range(out_ref.shape[0])
     ]
-    total = join_lse(logs)
-    shares = [jnp.exp(log - total)[:, 0:1] for log in logs]
-    times = time_ref[...].astype(F32) / TGRID
-    for at in range(0, latent, 256):
-        cut = slice(at, at + 256)
-        target = own_ref[:, cut] * shares[0]
-        for got, share in zip((a, b, c), shares[1:]):
-            target = target + got[:, cut].astype(F32) * share
-        noise = noise_ref[:, cut].astype(F32)
-        velocity_ref[:, cut] = (target - noise).astype(BF)
-        mixed_ref[:, cut] = ((1.0 - times) * noise + times * target).astype(BF)
-
-
-def qkv_kernel(place, tokens_ref, table_ref, f0, f1, f2, f3, out_ref):
+    for copy in copies:
+        copy.start()
+    for copy in copies:
+        copy.wait()
+
+
+def qkv_kernel(
+    place, own_ref, log_ref, noise_ref, time_ref, table_ref, *refs
+):
+    far = refs[:7]
+    out_ref, velocity_ref, tokens = refs[7:10]
+    near = refs[10:17]
+    sems = refs[17]
+    a, b, c, f0, f1, f2, f3 = near
+    rows, latent = own_ref.shape
+    step = pl.program_id(0)
+
+    @pl.when(step == 0)
+    def _():
+        copies = [
+            pltpu.make_async_copy(there, here, sems.at[k])
+            for k, (there, here) in enumerate(zip(far, near))
+        ]
+        for copy in copies:
+            copy.start()
+        for copy in copies[:3]:
+            copy.wait()
+        logs = [log_ref[...]] + [
+            jnp.broadcast_to(read_log(got[:, latent : latent + 128]), log_ref.shape)
+            for got in (a, b, c)
+        ]
+        total = join_lse(logs)
+        shares = [jnp.exp(log - total) for log in logs]
+        times = jnp.broadcast_to(time_ref[...].astype(F32) / TGRID, (rows, 128))
+        first = lax.broadcasted_iota(jnp.int32, (rows, 128), 1) < 64
+        for tile in range(latent // 128):
+            cut = slice(tile * 128, tile * 128 + 128)
+            target = own_ref[:, cut] * shares[0]
+            for got, share in zip((a, b, c), shares[1:]):
+                target = target + got[:, cut].astype(F32) * share
+            noise = noise_ref[:, cut].astype(F32)
+            velocity_ref[:, cut] = (target - noise).astype(BF)
+            mixed = ((1.0 - times) * noise + times * target).astype(BF).astype(F32)
+            turned = pltpu.roll(mixed, 64, 1)
+            tokens[pl.ds(2 * tile, rows, stride=latent // 64), :] = jnp.where(
+                first, mixed, turned
+            )
+            tokens[pl.ds(2 * tile + 1, rows, stride=latent // 64), :] = jnp.where(
+                first, turned, mixed
+            )
+        for copy in copies[3:]:
+            copy.wait()
+
+    count = out_ref.shape[0]
     width = table_ref.shape[1]
-    chunk = tokens_ref[...]
-    count = chunk.shape[0]
+    patches = tokens[pl.ds(pl.multiple_of(step * count, count), count), :].astype(BF)
+    spot = lax.broadcasted_iota(jnp.int32, (count, 128), 0) % 32
+    lane = lax.broadcasted_iota(jnp.int32, (count, 128), 1)
+    spots = jnp.where(spot == lane % 32, 1.0, 0.0).astype(BF)
+    chunk = jnp.concatenate([patches, spots[:, 0:64]], axis=1)
     total = jnp.zeros((count, 128), F32)
     for col in range(0, width, 256):
         part = jnp.dot(chunk, table_ref[:, col : col + 256], preferred_element_type=F32)
         part = part * part
         total = total + part[:, 0:128] + part[:, 128:256]
     scale = lax.rsqrt(jnp.sum(total, axis=1, keepdims=True) / width + 1e-06)
-    columns = f0.shape[2]
-    for k in range(16):
-        folded = (f0, f1, f2, f3)[k // 4][k % 4]
-        product = jnp.dot(chunk, folded, preferred_element_type=F32) * scale
-        at = pl.multiple_of((place[3] ^ k) * columns, 128)
-        out_ref[:, pl.ds(at, columns)] = product.astype(BF)
+    columns = f0.shape[1] // 4
+    for k in range(0, 16, 2):
+        at = (k % 4) * columns
+        product = jnp.dot(
+            chunk, (f0, f1, f2, f3)[k // 4][:, at : at + 2 * columns], preferred_element_type=F32
+        )
+        for side in range(2):
+            to = pl.multiple_of((place[3] ^ (k + side)) * columns, 128)
+            out_ref[:, pl.ds(to, columns)] = (
+                product[:, side * columns : (side + 1) * columns] * scale
+            ).astype(BF)
 
 
 def halves(value):
@@ -266,26 +322,31 @@
     high, low = halves(scaled)
     both = jnp.dot(jnp.concatenate([high, low], 0), qkv_weight, preferred_element_type=F32)
     rows = scaled.shape[0]
-    return jnp.concatenate(halves(both[:rows] + both[rows:]), 0)
+    high, low = halves(both[:rows] + both[rows:])
+    split = embed_weight.shape[0]
+    return jnp.concatenate([high[:split], low[:split], high[split:], low[split:]], 0)
 
 
 def together(*values):
     return lax.optimization_barrier(values)
 
 
-def coupled_target(noise, data, t_index, place, folded):
+def coupled_target(noise, data, place, folded):
     rows, latent = noise.shape
-    groups = column_groups()
     noise_pair = jnp.stack([noise, swap(noise, CORE)])
     noises = [noise_pair] + [swap(noise_pair, mask) for mask in Z_STEPS]
-    spread = jnp.broadcast_to(data[None], (16, rows, latent)).reshape(16 * rows, latent)
-    data_all = lax.all_to_all(
-        lax.optimization_barrier(spread), BOTH, 0, 0, axis_index_groups=groups, tiled=True
-    ).reshape(16, rows, latent)
+    spread = pl.pallas_call(
+        spread_kernel,
+        out_shape=shape((16, rows, latent), BF),
+        in_specs=[pl.BlockSpec(memory_space=pltpu.VMEM)],
+        out_specs=pl.BlockSpec(memory_space=pl.ANY),
+        scratch_shapes=[pltpu.SemaphoreType.DMA((16,))],
+    )(data)
+    data_all = exchange(spread, COL_MASK)
     flops = 2 * 8 * rows * 16 * rows * latent
     cost, row_part = vmem_call(
         cost_kernel,
-        (shape((8 * rows, 16 * rows)), shape((8, 128))),
+        (shape((8 * rows, 16 * rows)), shape((8, 8, 128))),
         scratch=[pltpu.VMEM((8, rows, latent), BF)],
         smem=1,
         inputs=5,
@@ -294,7 +355,7 @@
     )(place, data_all, *noises)
     quads = [None] * 4
     folded, row_part = together(folded, row_part)
-    folded = jnp.stack([folded, swap(folded, CORE)])
+    folded = jnp.concatenate([folded, swap(folded, CORE)], 1)
     for step in range(ITERS):
         if step == 1:
             folded, row_part = together(folded, row_part)
@@ -302,17 +363,14 @@
         elif step == 2:
             folded, row_part = together(folded, row_part)
             quads[2] = swap(folded, Y_STEPS[1])
-        row_pair = join_lse([row_part, swap(row_part, CORE)])
-        parts = [row_pair] + [swap(row_pair, mask) for mask in Z_STEPS]
+        row_parts = exchange(row_part, ROW_MASK)
         col_part = vmem_call(
-            functools.partial(col_kernel, step), shape((16, 8, 128)), inputs=5, nbytes=1024 * 1024
-        )(cost, *parts)
+            functools.partial(col_kernel, step), shape((16, 8, 128)), inputs=2, nbytes=1024 * 1024
+        )(cost, row_parts)
         if step == 0:
             folded, col_part = together(folded, col_part)
-            folded = jnp.concatenate([folded, swap(folded, Z_STEPS[0])])
-        col_parts = lax.all_to_all(
-            col_part, BOTH, 0, 0, axis_index_groups=groups, tiled=True
-        )
+            folded = jnp.concatenate([folded, swap(folded, Z_STEPS[0])], 1)
+        col_parts = exchange(col_part, COL_MASK)
         if step == 0:
             folded, col_parts = together(folded, col_parts)
         elif step == 1:
@@ -322,7 +380,7 @@
         if step + 1 < ITERS:
             row_part = vmem_call(
                 functools.partial(row_kernel, step + 1),
-                shape((8, 128)),
+                shape((8, 8, 128)),
                 inputs=2,
                 nbytes=1024 * 1024,
             )(cost, col_parts)
@@ -350,10 +408,7 @@
         nbytes=2 * 1024 * 1024,
     )(keep, log, swap(send, CORE))
     others = [swap(value, mask) for value, mask in zip(sends, Z_STEPS)]
-    velocity, mixed = vmem_call(
-        finish_kernel, (shape((rows, latent), BF),) * 2, inputs=7, nbytes=1024 * 1024
-    )(own, own_log, *others, noise, t_index[:, None])
-    return velocity, mixed, quads
+    return [own, own_log] + others, quads
 
 
 def local(noise, data, t_index, embed_weight, position, norm_gain, qkv_weight):
@@ -362,38 +417,40 @@
     ring = (src % 2) * 4 + tgt % 4
     place = jnp.stack([src // 2, tgt // 4, ring, tgt]).astype(jnp.int32)
     folded = folded_weights(embed_weight, position, norm_gain, qkv_weight)
-    velocity, mixed, quads = coupled_target(noise, data, t_index, place, folded)
-    patch_in, width = embed_weight.shape
+    parts, quads = coupled_target(noise, data, place, folded)
+    split, width = embed_weight.shape
     patch_count = position.shape[0]
-    patches = mixed.reshape(own * patch_count, patch_in)
-    spots = jnp.tile(jnp.eye(patch_count, dtype=BF), (own, 1))
-    tokens = jnp.concatenate([patches, spots, patches, spots], 1)
-    table = jnp.concatenate([embed_weight, position], 0)
-    table = jnp.concatenate([table, jnp.zeros_like(table)], 0)
-    quad, depth, columns = quads[0].shape
-    count = 4 * quad
+    table = jnp.concatenate(
+        [embed_weight, jnp.zeros_like(embed_weight), position, jnp.zeros_like(position)], 0
+    )
+    depth, columns = quads[0].shape
+    columns = 4 * columns
     chunk = 256
-    whole = pl.BlockSpec((quad, depth, columns), lambda j, where: (0, 0, 0))
-    qkv = pl.pallas_call(
+    values = [*parts[:2], noise, t_index[:, None], table]
+    far = [*parts[2:], *quads]
+    qkv, velocity = pl.pallas_call(
         qkv_kernel,
-        out_shape=shape((own * patch_count, count * columns), BF),
+        out_shape=(shape((own * patch_count, columns), BF), shape(noise.shape, BF)),
         grid_spec=pltpu.PrefetchScalarGridSpec(
             num_scalar_prefetch=1,
             grid=(own * patch_count // chunk,),
-            in_specs=[
-                pl.BlockSpec((chunk, depth), lambda j, where: (j, 0)),
-                pl.BlockSpec((depth, width), lambda j, where: (0, 0)),
-            ]
-            + [whole] * 4,
-            out_specs=pl.BlockSpec((chunk, count * columns), lambda j, where: (j, 0)),
+            in_specs=[pl.BlockSpec(value.shape, lambda j, where: (0, 0)) for value in values]
+            + [pl.BlockSpec(memory_space=pltpu.HBM)] * len(far),
+            out_specs=(
+                pl.BlockSpec((chunk, columns), lambda j, where: (j, 0)),
+                pl.BlockSpec(noise.shape, lambda j, where: (0, 0)),
+            ),
+            scratch_shapes=[pltpu.VMEM((own * patch_count, 2 * split), F32)]
+            + [pltpu.VMEM(value.shape, BF) for value in far]
+            + [pltpu.SemaphoreType.DMA((len(far),))],
         ),
-        compiler_params=pltpu.CompilerParams(vmem_limit_bytes=48 * 1024 * 1024),
+        compiler_params=pltpu.CompilerParams(vmem_limit_bytes=58 * 1024 * 1024),
         cost_estimate=pl.CostEstimate(
-            flops=2 * own * patch_count * depth * count * columns,
+            flops=2 * own * patch_count * depth * columns,
             bytes_accessed=16 * 1024 * 1024,
             transcendentals=0,
         ),
-    )(place, tokens, table, *quads)
+    )(place, *values, *far)
     return (velocity, qkv)
 
 

time: 151 us -> 143 us (0.947)
  blocking collectives: 21.3 us -> 51.7 us
  starting transfers between devices: 48.2 us -> 29 us
  waiting for transfers between devices: 45.6 us -> 32.9 us
  local copies, waits for them, and re-layouts: 10.9 us -> 2.88 us
  Pallas kernels: 18.9 us -> 21.7 us
    all_to_all x2 -> x5, blocking collectives: 21.3 us -> 51.7 us  [exchange(): lax.all_to_all(value, BOTH, 0, 0, axis_index_groups=groups_by(mask), tile...]
    ppermute x25 -> x13, starting transfers between devices: 37 us -> 17.7 us  [swap(): return lax.ppermute(value, BOTH, [(i, i ^ mask) for i in range(128)])]
    ppermute x25 -> x13, waiting for transfers between devices: 33.9 us -> 22 us  [swap(): return lax.ppermute(value, BOTH, [(i, i ^ mask) for i in range(128)])]
    pallas_call x5, Pallas kernels: 13.8 us -> 17.3 us  [the longest x1 11.5 us: local(): pl.pallas_call(qkv_kernel, out_shape=(shape((own * patch_count, columns),...]
    unnamed x38 -> x32, local copies, waits for them, and re-layouts: 4.78 us -> 2 us
    broadcast_in_dim x3, local copies, waits for them, and re-layouts: 3.34 us -> 0.7 us  [the longest x1 0.69 us: local(): values = [*parts[:2], noise, t_index[:, None], table]]
    reshape x1 -> x0, local copies, waits for them, and re-layouts: 1.89 us -> none  [local(): patches = mixed.reshape(own * patch_count, patch_in)]
  transfers between devices with their start and end apart: 27 -> 15, of which waited for: 18 -> 9; matrix products, arithmetic and copies ran while one was open for 2% -> 3% of each run, Pallas kernels for 1% -> 1%
where the time goes in v4:
time: 143 us
  blocking collectives  51.7 us (36%)
  waiting for transfers between devices  32.9 us (23%)
  starting transfers between devices  29 us (20%)
  Pallas kernels  21.7 us (15%)
  other arithmetic  3.08 us (2%)
  local copies, waits for them, and re-layouts  2.88 us (2%)
    all_to_all x5, blocking collectives, exchange(): lax.all_to_all(value, BOTH, 0, 0, axis_index_groups=groups_by(mask), tile...  51.7 us
    ppermute x13, waiting for transfers between devices, swap(): return lax.ppermute(value, BOTH, [(i, i ^ mask) for i in range(128)])  22 us
    ppermute x13, starting transfers between devices, swap(): return lax.ppermute(value, BOTH, [(i, i ^ mask) for i in range(128)])  17.7 us
    pallas_call x1, Pallas kernels, local(): pl.pallas_call(qkv_kernel, out_shape=(shape((own * patch_count, columns),...  11.5 us
    all_to_all x2, starting transfers between devices, exchange(): lax.all_to_all(value, BOTH, 0, 0, axis_index_groups=groups_by(mask), tile...  11.3 us
    all_to_all x2, waiting for transfers between devices, exchange(): lax.all_to_all(value, BOTH, 0, 0, axis_index_groups=groups_by(mask), tile...  10.9 us
  transfers between devices with their start and end apart: 15, of which 9 were waited for; matrix products, arithmetic and copies ran while one was open for 3% of the time, Pallas kernels for 1%

profile of v4, /device:TPU:1, one launch (start us, length us, event | category | flops | bytes accessed | tf_op | source)
XLA Modules:
  0.0 142.8 jit_solution(17085500636339377800)
XLA Ops:
  0.6 2.5 %shard_map.86 = bf16[16,32,2048]{2,1,0:T(8,128)(2,1)} custom-call(bf16[32,2048]{1,0:T(8,128)(2,1)} %value_ref.1), custom_call_target="tpu_custom_call" | custom-call | tf_op jit(solution)/shard_map/pallas_call | solution.py:338
  3.2 7.8 %all-to-all-start = ((bf16[16,32,2048]{2,1,0:T(8,128)(2,1)}), bf16[16,32,2048]{2,1,0:T(8,128)(2,1)}, u32[]{:S(2)}, u32[]{:S(2)}) async-start(bf16[16,32,2048]{2,1,0:T(8,128)(2,1)} %shard_map.86), calls=%async_computation | async-start | bytes 4194304 | tf_op jit(solution)/shard_map/all_to_all | solution.py:37
  11.0 1.0 collective-permute-start
  12.0 0.1 fusion.4
  12.2 0.6 fusion
  12.7 0.3 collective-permute-done
  13.0 3.8 %collective-permute-start.3 = (bf16[2,32,2048]{2,1,0:T(8,128)(2,1)S(1)}, bf16[2,32,2048]{2,1,0:T(8,128)(2,1)S(1)}, u32[]{:S(2)}, u32[]{:S(2)}) collective-permute-start(bf16[2,32,2048]{2,1,0:T(8,128)(2,1)S(1)} %pad_maximum_fusion.3.a), channel_id=1, source_target_pairs={{0,18},{1,19},{2,16},{3,17},{4,22},{5,23},{6,20},{7,21},{8,26},{9,... | collective-permute-start | bytes 786440 | tf_op jit(solution)/shard_map/ppermute | solution.py:26
  16.8 0.7 collective-permute-start.1
  17.7 0.7 pad_maximum_fusion.4
  18.4 10.5 %collective-permute-done.3.d = bf16[2,32,2048]{2,1,0:T(8,128)(2,1)S(1)} collective-permute-done((bf16[2,32,2048]{2,1,0:T(8,128)(2,1)S(1)}, bf16[2,32,2048]{2,1,0:T(8,128)(2,1)S(1)}, u32[]{:S(2)}, u32[]{:S(2)}) %collective-permute-start.3) | collective-permute-done | bytes 262176 | tf_op jit(solution)/shard_map/ppermute | solution.py:26
  29.0 0.4 collective-permute-done.1.b
  29.3 9.5 %all-to-all-done.data_ref = bf16[16,32,2048]{2,1,0:T(8,128)(2,1)} async-done(((bf16[16,32,2048]{2,1,0:T(8,128)(2,1)}), bf16[16,32,2048]{2,1,0:T(8,128)(2,1)}, u32[]{:S(2)}, u32[]{:S(2)}) %all-to-all-start) | async-done | bytes 2097184 | tf_op jit(solution)/shard_map/all_to_all | solution.py:37
  38.9 2.8 %shard_map.87 = (f32[256,512]{1,0:T(8,128)S(1)}, f32[8,8,128]{2,1,0:T(8,128)S(1)}) custom-call(s32[4]{0:T(128)S(1)} %pad_add_fusion.place, bf16[16,32,2048]{2,1,0:T(8,128)(2,1)} %all-to-all-done.data_ref, bf16[2,32,2048]{2,1,0:T(8,128)(2,1)S(1)} %pad_maximum_fusion.3.a, bf16[2,32,2048]{2,1,0:T(8,128)(2,1)S(1)} %collective-permute-done.1.b, ...), custom_call_target="tpu_custom_call" | custom-call | flops 536870912 | bytes 4194304 | tf_op jit(solution)/shard_map/pallas_call | solution.py:347
  41.7 3.5 %collective-permute-start.4 = (bf16[192,384]{1,0:T(8,128)(2,1)S(1)}, bf16[192,384]{1,0:T(8,128)(2,1)S(1)}, u32[]{:S(2)}, u32[]{:S(2)}) collective-permute-start(bf16[192,384]{1,0:T(8,128)(2,1)S(1)} %copy-done.6), channel_id=1, source_target_pairs={{0,1},{1,0},{2,3},{3,2},{4,5},{5,4},{6,7},{7,6},{8,9},{9,8},{10,11... | collective-permute-start | bytes 442376 | tf_op jit(solution)/shard_map/ppermute | solution.py:26
  45.2 9.9 %all_to_all.35.parts_ref = f32[8,8,128]{2,1,0:T(8,128)S(1)} all-to-all(f32[8,8,128]{2,1,0:T(8,128)S(1)} %get-tuple-element.32), channel_id=1, replica_groups={{0,1,2,3,16,17,18,19},{4,5,6,7,20,21,22,23},{8,9,10,11,24,25,26,27},{12..., dimensions={0} | all-to-all | bytes 65536 | tf_op jit(solution)/shard_map/all_to_all | solution.py:37
  55.2 0.9 shard_map.88
  56.1 0.4 collective-permute-start.5
  56.5 3.5 %all-to-all-start.2 = ((f32[16,8,128]{2,1,0:T(8,128)}), f32[16,8,128]{2,1,0:T(8,128)S(1)}, u32[]{:S(2)}, u32[]{:S(2)}) async-start(f32[16,8,128]{2,1,0:T(8,128)} %shard_map.88), calls=%async_computation.2 | async-start | bytes 131072 | tf_op jit(solution)/shard_map/all_to_all | solution.py:37
  60.0 4.1 %collective-permute-done.5 = bf16[192,768]{1,0:T(8,128)(2,1)} collective-permute-done((bf16[192,768]{1,0:T(8,128)(2,1)S(1)}, bf16[192,768]{1,0:T(8,128)(2,1)}, u32[]{:S(2)}, u32[]{:S(2)}) %collective-permute-start.5) | collective-permute-done | bytes 294944 | tf_op jit(solution)/shard_map/ppermute | solution.py:26
  64.1 1.0 pad_maximum_fusion.refs_3_
  65.1 1.3 all-to-all-done.2.parts_ref
  66.4 0.3 shard_map.89
  66.7 1.0 collective-permute-start.7
  67.8 10.6 %all_to_all.36.parts_ref = f32[8,8,128]{2,1,0:T(8,128)S(1)} all-to-all(f32[8,8,128]{2,1,0:T(8,128)S(1)} %shard_map.89), channel_id=1, replica_groups={{0,1,2,3,16,17,18,19},{4,5,6,7,20,21,22,23},{8,9,10,11,24,25,26,27},{12..., dimensions={0} | all-to-all | bytes 65536 | tf_op jit(solution)/shard_map/all_to_all | solution.py:37
  78.3 0.3 shard_map.90
  78.6 11.4 %all_to_all.37.parts_ref = f32[16,8,128]{2,1,0:T(8,128)S(1)} all-to-all(f32[16,8,128]{2,1,0:T(8,128)S(1)} %shard_map.90), channel_id=1, replica_groups={{0,4,8,12,32,36,40,44,64,68,72,76,96,100,104,108},{1,5,9,13,33,37,41,45..., dimensions={0} | all-to-all | bytes 131072 | tf_op jit(solution)/shard_map/all_to_all | solution.py:37
  90.1 0.3 shard_map.91
  90.3 1.2 collective-permute-start.8
  91.5 9.9 %all_to_all.38.parts_ref = f32[8,8,128]{2,1,0:T(8,128)S(1)} all-to-all(f32[8,8,128]{2,1,0:T(8,128)S(1)} %shard_map.91), channel_id=1, replica_groups={{0,1,2,3,16,17,18,19},{4,5,6,7,20,21,22,23},{8,9,10,11,24,25,26,27},{12..., dimensions={0} | all-to-all | bytes 65536 | tf_op jit(solution)/shard_map/all_to_all | solution.py:37
  101.4 0.3 shard_map.92
  101.7 9.9 %all_to_all.39.parts_ref = f32[16,8,128]{2,1,0:T(8,128)S(1)} all-to-all(f32[16,8,128]{2,1,0:T(8,128)S(1)} %shard_map.92), channel_id=1, replica_groups={{0,4,8,12,32,36,40,44,64,68,72,76,96,100,104,108},{1,5,9,13,33,37,41,45..., dimensions={0} | all-to-all | bytes 131072 | tf_op jit(solution)/shard_map/all_to_all | solution.py:37
  111.6 2.6 %shard_map.93 = (f32[4,32,2048]{2,1,0:T(8,128)S(1)}, f32[4,32,128]{2,1,0:T(8,128)S(1)}, bf16[4,32,2176]{2,1,0:T(8,128)(2,1)S(1)}) custom-call(s32[4]{0:T(128)S(1)} %pad_add_fusion.place, f32[256,512]{1,0:T(8,128)S(1)} %get-tuple-element.29.cost_ref, bf16[16,32,2048]{2,1,0:T(8,128)(2,1)} %all-to-all-done.data_ref, f32[16,8,128]{2,1,0:T(8,128)S(1)} %all_to_all.39.parts_ref), custom_call_target="tpu_custom_call" | custom-call | flops 536870912 | bytes 6291456 | tf_op jit(solution)/shard_map/pallas_call | solution.py:387
  114.2 2.1 %collective-permute-start.9 = (bf16[4,32,2176]{2,1,0:T(8,128)(2,1)S(1)}, bf16[4,32,2176]{2,1,0:T(8,128)(2,1)S(1)}, u32[]{:S(2)}, u32[]{:S(2)}) collective-permute-start(bf16[4,32,2176]{2,1,0:T(8,128)(2,1)S(1)} %get-tuple-element.45), channel_id=1, source_target_pairs={{0,1},{1,0},{2,3},{3,2},{4,5},{5,4},{6,7},{7,6},{8,9},{9,8},{10,11... | collective-permute-start | bytes 1671176 | tf_op jit(solution)/shard_map/ppermute | solution.py:26
  116.4 0.1 pad.3.clone
  116.5 0.1 pad.1.clone
  116.5 1.4 collective-permute-done.9.got_ref
  118.0 0.3 shard_map.94
  118.3 0.7 copy-done.2
  119.0 0.6 copy-done.3
  119.6 0.3 collective-permute-start.10
  119.9 1.8 %collective-permute-start.11 = (bf16[32,2176]{1,0:T(8,128)(2,1)S(1)}, bf16[32,2176]{1,0:T(8,128)(2,1)S(1)}, u32[]{:S(2)}, u32[]{:S(2)}) collective-permute-start(bf16[32,2176]{1,0:T(8,128)(2,1)S(1)} %get-tuple-element.49), channel_id=1, source_target_pairs={{0,16},{1,17},{2,18},{3,19},{4,20},{5,21},{6,22},{7,23},{8,24},{9,... | collective-permute-start | bytes 417800 | tf_op jit(solution)/shard_map/ppermute | solution.py:26
  121.7 1.8 %collective-permute-start.12 = (bf16[32,2176]{1,0:T(8,128)(2,1)S(1)}, bf16[32,2176]{1,0:T(8,128)(2,1)S(1)}, u32[]{:S(2)}, u32[]{:S(2)}) collective-permute-start(bf16[32,2176]{1,0:T(8,128)(2,1)S(1)} %get-tuple-element.50), channel_id=1, source_target_pairs={{0,18},{1,19},{2,16},{3,17},{4,22},{5,23},{6,20},{7,21},{8,26},{9,... | collective-permute-start | bytes 417800 | tf_op jit(solution)/shard_map/ppermute | solution.py:26
  123.5 1.1 maximum_maximum_fusion.table_ref
  124.6 0.7 copy.9.time_ref
  125.3 2.8 %collective-permute-done.11.refs_1_ = bf16[32,2176]{1,0:T(8,128)(2,1)S(1)} collective-permute-done((bf16[32,2176]{1,0:T(8,128)(2,1)S(1)}, bf16[32,2176]{1,0:T(8,128)(2,1)S(1)}, u32[]{:S(2)}, u32[]{:S(2)}) %collective-permute-start.11) | collective-permute-done | bytes 139296 | tf_op jit(solution)/shard_map/ppermute | solution.py:26
  128.1 2.5 %collective-permute-done.12.refs_2_ = bf16[32,2176]{1,0:T(8,128)(2,1)S(1)} collective-permute-done((bf16[32,2176]{1,0:T(8,128)(2,1)S(1)}, bf16[32,2176]{1,0:T(8,128)(2,1)S(1)}, u32[]{:S(2)}, u32[]{:S(2)}) %collective-permute-start.12) | collective-permute-done | bytes 139296 | tf_op jit(solution)/shard_map/ppermute | solution.py:26
  130.6 0.6 copy-done.15
  131.3 11.5 %shard_map.95 = (bf16[1024,6144]{1,0:T(8,128)(2,1)}, bf16[32,2048]{1,0:T(8,128)(2,1)}) custom-call(s32[4]{0:T(128)} %copy-done.1, f32[32,2048]{1,0:T(8,128)} %copy-done.2, f32[32,128]{1,0:T(8,128)} %copy-done.3, bf16[32,2048]{1,0:T(8,128)(2,1)} %noise_ref.1, s32[32,1]{1,0:T(8,128)} %copy.9.time_ref, bf16[192,2048]{1,0:T(8,128)(2,1)} %maximum_maximum_fusion.table_ref, ...), custom_call_target="tpu_custom_call" | custom-call | flops 2415919104 | bytes 16777216 | tf_op jit(solution)/shard_map/pallas_call | solution.py:431
  (47 shorter events, 0.3 us)
Async XLA Ops:
  0.6 11.5 %copy-start = (bf16[2048,384]{1,0:T(8,128)(2,1)S(1)}, bf16[2048,384]{1,0:T(8,128)(2,1)}, u32[]{:S(2)}) copy-start(bf16[2048,384]{1,0:T(8,128)(2,1)} %param.13) | copy-start | bytes 4718596
  3.1 7.8 %copy-start.8 = (bf16[32,2048]{1,0:T(8,128)(2,1)S(1)}, bf16[32,2048]{1,0:T(8,128)(2,1)}, u32[]{:S(2)}) copy-start(bf16[32,2048]{1,0:T(8,128)(2,1)} %noise_ref.1) | copy-start | bytes 393220
  3.1 8.9 %copy-start.4 = (bf16[64,2048]{1,0:T(8,128)(2,1)S(1)}, bf16[64,2048]{1,0:T(8,128)(2,1)}, u32[]{:S(2)}) copy-start(bf16[64,2048]{1,0:T(8,128)(2,1)} %param.10) | copy-start | bytes 786436
  3.1 8.9 %copy-start.7 = (bf16[32,2048]{1,0:T(8,128)(2,1)S(1)}, bf16[32,2048]{1,0:T(8,128)(2,1)}, u32[]{:S(2)}) copy-start(bf16[32,2048]{1,0:T(8,128)(2,1)} %param.11) | copy-start | bytes 393220
  3.1 8.9 %copy-start.9 = (f32[2048]{0:T(1024)S(1)}, f32[2048]{0:T(1024)}, u32[]{:S(2)}) copy-start(f32[2048]{0:T(1024)} %param.12) | copy-start | bytes 24580
  3.2 35.7 %all-to-all-start = ((bf16[16,32,2048]{2,1,0:T(8,128)(2,1)}), bf16[16,32,2048]{2,1,0:T(8,128)(2,1)}, u32[]{:S(2)}, u32[]{:S(2)}) async-start(bf16[16,32,2048]{2,1,0:T(8,128)(2,1)} %shard_map.86), calls=%async_computation | async-start | bytes 4194304 | tf_op jit(solution)/shard_map/all_to_all | solution.py:37
  11.0 2.0 %collective-permute-start = (bf16[32,2048]{1,0:T(8,128)(2,1)S(1)}, bf16[32,2048]{1,0:T(8,128)(2,1)S(1)}, u32[]{:S(2)}, u32[]{:S(2)}) collective-permute-start(bf16[32,2048]{1,0:T(8,128)(2,1)S(1)} %copy-done.8), channel_id=1, source_target_pairs={{0,1},{1,0},{2,3},{3,2},{4,5},{5,4},{6,7},{7,6},{8,9},{9,8},{10,11... | collective-permute-start | bytes 393224 | tf_op jit(solution)/shard_map/ppermute | solution.py:26
  13.0 15.9 %collective-permute-start.3 = (bf16[2,32,2048]{2,1,0:T(8,128)(2,1)S(1)}, bf16[2,32,2048]{2,1,0:T(8,128)(2,1)S(1)}, u32[]{:S(2)}, u32[]{:S(2)}) collective-permute-start(bf16[2,32,2048]{2,1,0:T(8,128)(2,1)S(1)} %pad_maximum_fusion.3.a), channel_id=1, source_target_pairs={{0,18},{1,19},{2,16},{3,17},{4,22},{5,23},{6,20},{7,21},{8,26},{9,... | collective-permute-start | bytes 786440 | tf_op jit(solution)/shard_map/ppermute | solution.py:26
  16.8 12.1 %collective-permute-start.2 = (bf16[2,32,2048]{2,1,0:T(8,128)(2,1)S(1)}, bf16[2,32,2048]{2,1,0:T(8,128)(2,1)S(1)}, u32[]{:S(2)}, u32[]{:S(2)}) collective-permute-start(bf16[2,32,2048]{2,1,0:T(8,128)(2,1)S(1)} %pad_maximum_fusion.3.a), channel_id=1, source_target_pairs={{0,16},{1,17},{2,18},{3,19},{4,20},{5,21},{6,22},{7,23},{8,24},{9,... | collective-permute-start | bytes 786440 | tf_op jit(solution)/shard_map/ppermute | solution.py:26
  16.8 12.5 %collective-permute-start.1 = (bf16[2,32,2048]{2,1,0:T(8,128)(2,1)S(1)}, bf16[2,32,2048]{2,1,0:T(8,128)(2,1)S(1)}, u32[]{:S(2)}, u32[]{:S(2)}) collective-permute-start(bf16[2,32,2048]{2,1,0:T(8,128)(2,1)S(1)} %pad_maximum_fusion.3.a), channel_id=1, source_target_pairs={{0,2},{1,3},{2,0},{3,1},{4,6},{5,7},{6,4},{7,5},{8,10},{9,11},{10,... | collective-permute-start | bytes 786440 | tf_op jit(solution)/shard_map/ppermute | solution.py:26
  17.7 93.9 %copy-start.1 = (s32[4]{0:T(128)}, s32[4]{0:T(128)S(1)}, u32[]{:S(2)}) copy-start(s32[4]{0:T(128)S(1)} %pad_add_fusion.place) | copy-start | bytes 52
  38.9 2.8 %copy-start.6 = (bf16[192,384]{1,0:T(8,128)(2,1)S(1)}, bf16[192,384]{1,0:T(8,128)(2,1)}, u32[]{:S(2)}) copy-start(bf16[192,384]{1,0:T(8,128)(2,1)} %pad_maximum_fusion.4) | copy-start | bytes 442372
  41.7 14.4 %collective-permute-start.4 = (bf16[192,384]{1,0:T(8,128)(2,1)S(1)}, bf16[192,384]{1,0:T(8,128)(2,1)S(1)}, u32[]{:S(2)}, u32[]{:S(2)}) collective-permute-start(bf16[192,384]{1,0:T(8,128)(2,1)S(1)} %copy-done.6), channel_id=1, source_target_pairs={{0,1},{1,0},{2,3},{3,2},{4,5},{5,4},{6,7},{7,6},{8,9},{9,8},{10,11... | collective-permute-start | bytes 442376 | tf_op jit(solution)/shard_map/ppermute | solution.py:26
  56.1 8.0 %collective-permute-start.5 = (bf16[192,768]{1,0:T(8,128)(2,1)S(1)}, bf16[192,768]{1,0:T(8,128)(2,1)}, u32[]{:S(2)}, u32[]{:S(2)}) collective-permute-start(bf16[192,768]{1,0:T(8,128)(2,1)S(1)} %pad_maximum_fusion.2), channel_id=1, source_target_pairs={{0,2},{1,3},{2,0},{3,1},{4,6},{5,7},{6,4},{7,5},{8,10},{9,11},{10,... | collective-permute-start | bytes 884744 | tf_op jit(solution)/shard_map/ppermute | solution.py:26
  56.5 10.0 %all-to-all-start.2 = ((f32[16,8,128]{2,1,0:T(8,128)}), f32[16,8,128]{2,1,0:T(8,128)S(1)}, u32[]{:S(2)}, u32[]{:S(2)}) async-start(f32[16,8,128]{2,1,0:T(8,128)} %shard_map.88), calls=%async_computation.2 | async-start | bytes 131072 | tf_op jit(solution)/shard_map/all_to_all | solution.py:37
  65.1 46.5 %copy-start.5 = (bf16[192,1536]{1,0:T(8,128)(2,1)}, bf16[192,1536]{1,0:T(8,128)(2,1)S(1)}, u32[]{:S(2)}) copy-start(bf16[192,1536]{1,0:T(8,128)(2,1)S(1)} %pad_maximum_fusion.refs_3_) | copy-start | bytes 1769476
  66.7 23.3 %collective-permute-start.7 = (bf16[192,1536]{1,0:T(8,128)(2,1)S(1)}, bf16[192,1536]{1,0:T(8,128)(2,1)S(1)}, u32[]{:S(2)}, u32[]{:S(2)}) collective-permute-start(bf16[192,1536]{1,0:T(8,128)(2,1)S(1)} %pad_maximum_fusion.refs_3_), channel_id=1, source_target_pairs={{0,12},{1,13},{2,14},{3,15},{4,8},{5,9},{6,10},{7,11},{8,4},{9,5},... | collective-permute-start | bytes 1769480 | tf_op jit(solution)/shard_map/ppermute | solution.py:26
  67.8 22.3 %collective-permute-start.6 = (bf16[192,1536]{1,0:T(8,128)(2,1)S(1)}, bf16[192,1536]{1,0:T(8,128)(2,1)S(1)}, u32[]{:S(2)}, u32[]{:S(2)}) collective-permute-start(bf16[192,1536]{1,0:T(8,128)(2,1)S(1)} %pad_maximum_fusion.refs_3_), channel_id=1, source_target_pairs={{0,4},{1,5},{2,6},{3,7},{4,0},{5,1},{6,2},{7,3},{8,12},{9,13},{10,... | collective-permute-start | bytes 1769480 | tf_op jit(solution)/shard_map/ppermute | solution.py:26
  90.0 21.6 %copy-start.11 = (bf16[192,1536]{1,0:T(8,128)(2,1)}, bf16[192,1536]{1,0:T(8,128)(2,1)S(1)}, u32[]{:S(2)}) copy-start(bf16[192,1536]{1,0:T(8,128)(2,1)S(1)} %collective-permute-done.7.refs_6_) | copy-start | bytes 1769476
  90.0 11.4 %copy-start.12 = (bf16[192,1536]{1,0:T(8,128)(2,1)}, bf16[192,1536]{1,0:T(8,128)(2,1)S(1)}, u32[]{:S(2)}) copy-start(bf16[192,1536]{1,0:T(8,128)(2,1)S(1)} %collective-permute-done.6.refs_4_) | copy-start | bytes 1769476
  90.3 21.3 %collective-permute-start.8 = (bf16[192,1536]{1,0:T(8,128)(2,1)S(1)}, bf16[192,1536]{1,0:T(8,128)(2,1)}, u32[]{:S(2)}, u32[]{:S(2)}) collective-permute-start(bf16[192,1536]{1,0:T(8,128)(2,1)S(1)} %pad_maximum_fusion.refs_3_), channel_id=1, source_target_pairs={{0,8},{1,9},{2,10},{3,11},{4,12},{5,13},{6,14},{7,15},{8,0},{9,1},... | collective-permute-start | bytes 1769480 | tf_op jit(solution)/shard_map/ppermute | solution.py:26
  114.2 10.4 %copy-start.10 = (s32[32]{0:T(128)S(1)}, s32[32]{0:T(128)}, u32[]{:S(2)}) copy-start(s32[32]{0:T(128)} %param.9) | copy-start | bytes 388
  114.2 3.7 %collective-permute-start.9 = (bf16[4,32,2176]{2,1,0:T(8,128)(2,1)S(1)}, bf16[4,32,2176]{2,1,0:T(8,128)(2,1)S(1)}, u32[]{:S(2)}, u32[]{:S(2)}) collective-permute-start(bf16[4,32,2176]{2,1,0:T(8,128)(2,1)S(1)} %get-tuple-element.45), channel_id=1, source_target_pairs={{0,1},{1,0},{2,3},{3,2},{4,5},{5,4},{6,7},{7,6},{8,9},{9,8},{10,11... | collective-permute-start | bytes 1671176 | tf_op jit(solution)/shard_map/ppermute | solution.py:26
  118.3 0.7 copy-start.2
  119.0 0.6 copy-start.3
  119.6 5.7 %collective-permute-start.10 = (bf16[32,2176]{1,0:T(8,128)(2,1)S(1)}, bf16[32,2176]{1,0:T(8,128)(2,1)S(1)}, u32[]{:S(2)}, u32[]{:S(2)}) collective-permute-start(bf16[32,2176]{1,0:T(8,128)(2,1)S(1)} %get-tuple-element.48), channel_id=1, source_target_pairs={{0,2},{1,3},{2,0},{3,1},{4,6},{5,7},{6,4},{7,5},{8,10},{9,11},{10,... | collective-permute-start | bytes 417800 | tf_op jit(solution)/shard_map/ppermute | solution.py:26
  119.9 8.2 %collective-permute-start.11 = (bf16[32,2176]{1,0:T(8,128)(2,1)S(1)}, bf16[32,2176]{1,0:T(8,128)(2,1)S(1)}, u32[]{:S(2)}, u32[]{:S(2)}) collective-permute-start(bf16[32,2176]{1,0:T(8,128)(2,1)S(1)} %get-tuple-element.49), channel_id=1, source_target_pairs={{0,16},{1,17},{2,18},{3,19},{4,20},{5,21},{6,22},{7,23},{8,24},{9,... | collective-permute-start | bytes 417800 | tf_op jit(solution)/shard_map/ppermute | solution.py:26
  121.7 8.9 %collective-permute-start.12 = (bf16[32,2176]{1,0:T(8,128)(2,1)S(1)}, bf16[32,2176]{1,0:T(8,128)(2,1)S(1)}, u32[]{:S(2)}, u32[]{:S(2)}) collective-permute-start(bf16[32,2176]{1,0:T(8,128)(2,1)S(1)} %get-tuple-element.50), channel_id=1, source_target_pairs={{0,18},{1,19},{2,16},{3,17},{4,22},{5,23},{6,20},{7,21},{8,26},{9,... | collective-permute-start | bytes 417800 | tf_op jit(solution)/shard_map/ppermute | solution.py:26
  125.3 5.3 %copy-start.13 = (bf16[32,2176]{1,0:T(8,128)(2,1)}, bf16[32,2176]{1,0:T(8,128)(2,1)S(1)}, u32[]{:S(2)}) copy-start(bf16[32,2176]{1,0:T(8,128)(2,1)S(1)} %collective-permute-done.10.refs_0_) | copy-start | bytes 417796
  128.1 2.5 %copy-start.14 = (bf16[32,2176]{1,0:T(8,128)(2,1)}, bf16[32,2176]{1,0:T(8,128)(2,1)S(1)}, u32[]{:S(2)}) copy-start(bf16[32,2176]{1,0:T(8,128)(2,1)S(1)} %collective-permute-done.11.refs_1_) | copy-start | bytes 417796
  130.6 0.7 copy-start.15

commit v5 on v4

--- a/solution.py
+++ b/solution.py
@@ -9,6 +9,7 @@
 
 ITERS = 3
 TGRID = 1000
+TILE = 1024
 BOTH = ("src", "tgt")
 CORE = 1
 ROW_MASK, COL_MASK = 108, 19
@@ -243,9 +244,7 @@
 ):
     far = refs[:7]
     out_ref, velocity_ref, tokens = refs[7:10]
-    near = refs[10:17]
-    sems = refs[17]
-    a, b, c, f0, f1, f2, f3 = near
+    a, b, c, folded, sems = refs[10:15]
     rows, latent = own_ref.shape
     step = pl.program_id(0)
 
@@ -253,8 +252,18 @@
     def _():
         copies = [
             pltpu.make_async_copy(there, here, sems.at[k])
-            for k, (there, here) in enumerate(zip(far, near))
+            for k, (there, here) in enumerate(zip(far, (a, b, c)))
         ]
+        for k in range(16):
+            columns = folded.shape[1] // 16
+            to = pl.multiple_of((place[3] ^ k) * columns, 128)
+            copies.append(
+                pltpu.make_async_copy(
+                    far[3 + k // 4].at[:, pl.ds((k % 4) * columns, columns)],
+                    folded.at[:, pl.ds(to, columns)],
+                    sems.at[3 + k],
+                )
+            )
         for copy in copies:
             copy.start()
         for copy in copies[:3]:
@@ -298,17 +307,9 @@
         part = part * part
         total = total + part[:, 0:128] + part[:, 128:256]
     scale = lax.rsqrt(jnp.sum(total, axis=1, keepdims=True) / width + 1e-06)
-    columns = f0.shape[1] // 4
-    for k in range(0, 16, 2):
-        at = (k % 4) * columns
-        product = jnp.dot(
-            chunk, (f0, f1, f2, f3)[k // 4][:, at : at + 2 * columns], preferred_element_type=F32
-        )
-        for side in range(2):
-            to = pl.multiple_of((place[3] ^ (k + side)) * columns, 128)
-            out_ref[:, pl.ds(to, columns)] = (
-                product[:, side * columns : (side + 1) * columns] * scale
-            ).astype(BF)
+    for at in range(0, folded.shape[1], TILE):
+        product = jnp.dot(chunk, folded[:, at : at + TILE], preferred_element_type=F32)
+        out_ref[:, at : at + TILE] = (product * scale).astype(BF)
 
 
 def halves(value):
@@ -441,10 +442,10 @@
                 pl.BlockSpec(noise.shape, lambda j, where: (0, 0)),
             ),
             scratch_shapes=[pltpu.VMEM((own * patch_count, 2 * split), F32)]
-            + [pltpu.VMEM(value.shape, BF) for value in far]
-            + [pltpu.SemaphoreType.DMA((len(far),))],
+            + [pltpu.VMEM(value.shape, BF) for value in far[:3]]
+            + [pltpu.VMEM((depth, columns), BF), pltpu.SemaphoreType.DMA((19,))],
         ),
-        compiler_params=pltpu.CompilerParams(vmem_limit_bytes=58 * 1024 * 1024),
+        compiler_params=pltpu.CompilerParams(vmem_limit_bytes=53 * 1024 * 1024),
         cost_estimate=pl.CostEstimate(
             flops=2 * own * patch_count * depth * columns,
             bytes_accessed=16 * 1024 * 1024,

time: 143 us -> 141 us (0.986)
  local copies, waits for them, and re-layouts: 2.88 us -> 0.33 us
    unnamed x32 -> x22, local copies, waits for them, and re-layouts: 2 us -> 0.06 us
where the time goes in v5:
time: 141 us
  blocking collectives  51.7 us (37%)
  waiting for transfers between devices  33.5 us (24%)
  starting transfers between devices  29 us (21%)
  Pallas kernels  21.5 us (15%)
  other arithmetic  3.1 us (2%)
    all_to_all x5, blocking collectives, exchange(): lax.all_to_all(value, BOTH, 0, 0, axis_index_groups=groups_by(mask), tile...  51.7 us
    ppermute x13, waiting for transfers between devices, swap(): return lax.ppermute(value, BOTH, [(i, i ^ mask) for i in range(128)])  22.6 us
    ppermute x13, starting transfers between devices, swap(): return lax.ppermute(value, BOTH, [(i, i ^ mask) for i in range(128)])  17.8 us
    all_to_all x2, starting transfers between devices, exchange(): lax.all_to_all(value, BOTH, 0, 0, axis_index_groups=groups_by(mask), tile...  11.3 us
    pallas_call x1, Pallas kernels, local(): pl.pallas_call(qkv_kernel, out_shape=(shape((own * patch_count, columns),...  11.3 us
    all_to_all x2, waiting for transfers between devices, exchange(): lax.all_to_all(value, BOTH, 0, 0, axis_index_groups=groups_by(mask), tile...  10.9 us
  transfers between devices with their start and end apart: 15, of which 9 were waited for; matrix products, arithmetic and copies ran while one was open for 3% of the time, Pallas kernels for 1%

profile of v5, /device:TPU:1, one launch (start us, length us, event | category | flops | bytes accessed | tf_op | source)
XLA Modules:
  0.0 140.7 jit_solution(2859251993186134226)
XLA Ops:
  0.6 0.0 copy-start
  0.6 2.5 %shard_map.86 = bf16[16,32,2048]{2,1,0:T(8,128)(2,1)} custom-call(bf16[32,2048]{1,0:T(8,128)(2,1)} %value_ref.1), custom_call_target="tpu_custom_call" | custom-call | tf_op jit(solution)/shard_map/pallas_call | solution.py:339
  3.1 0.0 copy-start.2
  3.2 7.8 %all-to-all-start = ((bf16[16,32,2048]{2,1,0:T(8,128)(2,1)}), bf16[16,32,2048]{2,1,0:T(8,128)(2,1)}, u32[]{:S(2)}, u32[]{:S(2)}) async-start(bf16[16,32,2048]{2,1,0:T(8,128)(2,1)} %shard_map.86), calls=%async_computation | async-start | bytes 4194304 | tf_op jit(solution)/shard_map/all_to_all | solution.py:38
  11.0 1.0 collective-permute-start
  12.0 0.1 fusion.4
  12.2 0.6 fusion
  12.7 0.3 collective-permute-done
  13.0 3.8 %collective-permute-start.3 = (bf16[2,32,2048]{2,1,0:T(8,128)(2,1)S(1)}, bf16[2,32,2048]{2,1,0:T(8,128)(2,1)S(1)}, u32[]{:S(2)}, u32[]{:S(2)}) collective-permute-start(bf16[2,32,2048]{2,1,0:T(8,128)(2,1)S(1)} %pad_maximum_fusion.3.a), channel_id=1, source_target_pairs={{0,18},{1,19},{2,16},{3,17},{4,22},{5,23},{6,20},{7,21},{8,26},{9,... | collective-permute-start | bytes 786440 | tf_op jit(solution)/shard_map/ppermute | solution.py:27
  16.8 0.7 collective-permute-start.1
  17.7 0.1 pad_add_fusion.place
  17.7 0.7 pad_maximum_fusion.4
  18.4 10.5 %collective-permute-done.3.d = bf16[2,32,2048]{2,1,0:T(8,128)(2,1)S(1)} collective-permute-done((bf16[2,32,2048]{2,1,0:T(8,128)(2,1)S(1)}, bf16[2,32,2048]{2,1,0:T(8,128)(2,1)S(1)}, u32[]{:S(2)}, u32[]{:S(2)}) %collective-permute-start.3) | collective-permute-done | bytes 262176 | tf_op jit(solution)/shard_map/ppermute | solution.py:27
  29.0 0.4 collective-permute-done.1.b
  29.3 9.5 %all-to-all-done.data_ref = bf16[16,32,2048]{2,1,0:T(8,128)(2,1)} async-done(((bf16[16,32,2048]{2,1,0:T(8,128)(2,1)}), bf16[16,32,2048]{2,1,0:T(8,128)(2,1)}, u32[]{:S(2)}, u32[]{:S(2)}) %all-to-all-start) | async-done | bytes 2097184 | tf_op jit(solution)/shard_map/all_to_all | solution.py:38
  38.9 2.8 %shard_map.87 = (f32[256,512]{1,0:T(8,128)S(1)}, f32[8,8,128]{2,1,0:T(8,128)S(1)}) custom-call(s32[4]{0:T(128)S(1)} %pad_add_fusion.place, bf16[16,32,2048]{2,1,0:T(8,128)(2,1)} %all-to-all-done.data_ref, bf16[2,32,2048]{2,1,0:T(8,128)(2,1)S(1)} %pad_maximum_fusion.3.a, bf16[2,32,2048]{2,1,0:T(8,128)(2,1)S(1)} %collective-permute-done.1.b, ...), custom_call_target="tpu_custom_call" | custom-call | flops 536870912 | bytes 4194304 | tf_op jit(solution)/shard_map/pallas_call | solution.py:348
  41.7 3.5 %collective-permute-start.4 = (bf16[192,384]{1,0:T(8,128)(2,1)S(1)}, bf16[192,384]{1,0:T(8,128)(2,1)S(1)}, u32[]{:S(2)}, u32[]{:S(2)}) collective-permute-start(bf16[192,384]{1,0:T(8,128)(2,1)S(1)} %copy-done.4), channel_id=1, source_target_pairs={{0,1},{1,0},{2,3},{3,2},{4,5},{5,4},{6,7},{7,6},{8,9},{9,8},{10,11... | collective-permute-start | bytes 442376 | tf_op jit(solution)/shard_map/ppermute | solution.py:27
  45.2 9.9 %all_to_all.35.parts_ref = f32[8,8,128]{2,1,0:T(8,128)S(1)} all-to-all(f32[8,8,128]{2,1,0:T(8,128)S(1)} %get-tuple-element.32), channel_id=1, replica_groups={{0,1,2,3,16,17,18,19},{4,5,6,7,20,21,22,23},{8,9,10,11,24,25,26,27},{12..., dimensions={0} | all-to-all | bytes 65536 | tf_op jit(solution)/shard_map/all_to_all | solution.py:38
  55.2 0.9 shard_map.88
  56.1 0.4 collective-permute-start.5
  56.5 3.5 %all-to-all-start.2 = ((f32[16,8,128]{2,1,0:T(8,128)}), f32[16,8,128]{2,1,0:T(8,128)S(1)}, u32[]{:S(2)}, u32[]{:S(2)}) async-start(f32[16,8,128]{2,1,0:T(8,128)} %shard_map.88), calls=%async_computation.2 | async-start | bytes 131072 | tf_op jit(solution)/shard_map/all_to_all | solution.py:38
  60.0 4.1 %collective-permute-done.5 = bf16[192,768]{1,0:T(8,128)(2,1)} collective-permute-done((bf16[192,768]{1,0:T(8,128)(2,1)S(1)}, bf16[192,768]{1,0:T(8,128)(2,1)}, u32[]{:S(2)}, u32[]{:S(2)}) %collective-permute-start.5) | collective-permute-done | bytes 294944 | tf_op jit(solution)/shard_map/ppermute | solution.py:27
  64.1 1.0 pad_maximum_fusion.refs_3_
  65.1 1.3 all-to-all-done.2.parts_ref
  66.4 0.3 shard_map.89
  66.7 1.0 collective-permute-start.7
  67.8 10.6 %all_to_all.36.parts_ref = f32[8,8,128]{2,1,0:T(8,128)S(1)} all-to-all(f32[8,8,128]{2,1,0:T(8,128)S(1)} %shard_map.89), channel_id=1, replica_groups={{0,1,2,3,16,17,18,19},{4,5,6,7,20,21,22,23},{8,9,10,11,24,25,26,27},{12..., dimensions={0} | all-to-all | bytes 65536 | tf_op jit(solution)/shard_map/all_to_all | solution.py:38
  78.3 0.3 shard_map.90
  78.6 11.4 %all_to_all.37.parts_ref = f32[16,8,128]{2,1,0:T(8,128)S(1)} all-to-all(f32[16,8,128]{2,1,0:T(8,128)S(1)} %shard_map.90), channel_id=1, replica_groups={{0,4,8,12,32,36,40,44,64,68,72,76,96,100,104,108},{1,5,9,13,33,37,41,45..., dimensions={0} | all-to-all | bytes 131072 | tf_op jit(solution)/shard_map/all_to_all | solution.py:38
  90.1 0.3 shard_map.91
  90.3 1.2 collective-permute-start.8
  91.5 9.9 %all_to_all.38.parts_ref = f32[8,8,128]{2,1,0:T(8,128)S(1)} all-to-all(f32[8,8,128]{2,1,0:T(8,128)S(1)} %shard_map.91), channel_id=1, replica_groups={{0,1,2,3,16,17,18,19},{4,5,6,7,20,21,22,23},{8,9,10,11,24,25,26,27},{12..., dimensions={0} | all-to-all | bytes 65536 | tf_op jit(solution)/shard_map/all_to_all | solution.py:38
  101.4 0.3 shard_map.92
  101.7 9.9 %all_to_all.39.parts_ref = f32[16,8,128]{2,1,0:T(8,128)S(1)} all-to-all(f32[16,8,128]{2,1,0:T(8,128)S(1)} %shard_map.92), channel_id=1, replica_groups={{0,4,8,12,32,36,40,44,64,68,72,76,96,100,104,108},{1,5,9,13,33,37,41,45..., dimensions={0} | all-to-all | bytes 131072 | tf_op jit(solution)/shard_map/all_to_all | solution.py:38
  111.6 2.6 %shard_map.93 = (f32[4,32,2048]{2,1,0:T(8,128)S(1)}, f32[4,32,128]{2,1,0:T(8,128)S(1)}, bf16[4,32,2176]{2,1,0:T(8,128)(2,1)S(1)}) custom-call(s32[4]{0:T(128)S(1)} %pad_add_fusion.place, f32[256,512]{1,0:T(8,128)S(1)} %get-tuple-element.29.cost_ref, bf16[16,32,2048]{2,1,0:T(8,128)(2,1)} %all-to-all-done.data_ref, f32[16,8,128]{2,1,0:T(8,128)S(1)} %all_to_all.39.parts_ref), custom_call_target="tpu_custom_call" | custom-call | flops 536870912 | bytes 6291456 | tf_op jit(solution)/shard_map/pallas_call | solution.py:388
  114.3 2.1 %collective-permute-start.9 = (bf16[4,32,2176]{2,1,0:T(8,128)(2,1)S(1)}, bf16[4,32,2176]{2,1,0:T(8,128)(2,1)S(1)}, u32[]{:S(2)}, u32[]{:S(2)}) collective-permute-start(bf16[4,32,2176]{2,1,0:T(8,128)(2,1)S(1)} %get-tuple-element.45), channel_id=1, source_target_pairs={{0,1},{1,0},{2,3},{3,2},{4,5},{5,4},{6,7},{7,6},{8,9},{9,8},{10,11... | collective-permute-start | bytes 1671176 | tf_op jit(solution)/shard_map/ppermute | solution.py:27
  116.4 0.1 pad.3.clone
  116.5 0.1 pad.1.clone
  116.6 1.4 %collective-permute-done.9.got_ref = bf16[4,32,2176]{2,1,0:T(8,128)(2,1)S(1)} collective-permute-done((bf16[4,32,2176]{2,1,0:T(8,128)(2,1)S(1)}, bf16[4,32,2176]{2,1,0:T(8,128)(2,1)S(1)}, u32[]{:S(2)}, u32[]{:S(2)}) %collective-permute-start.9) | collective-permute-done | bytes 557088 | tf_op jit(solution)/shard_map/ppermute | solution.py:27
  118.0 0.3 shard_map.94
  118.3 0.4 collective-permute-start.10
  118.7 1.8 %collective-permute-start.11 = (bf16[32,2176]{1,0:T(8,128)(2,1)S(1)}, bf16[32,2176]{1,0:T(8,128)(2,1)S(1)}, u32[]{:S(2)}, u32[]{:S(2)}) collective-permute-start(bf16[32,2176]{1,0:T(8,128)(2,1)S(1)} %get-tuple-element.49), channel_id=1, source_target_pairs={{0,16},{1,17},{2,18},{3,19},{4,20},{5,21},{6,22},{7,23},{8,24},{9,... | collective-permute-start | bytes 417800 | tf_op jit(solution)/shard_map/ppermute | solution.py:27
  120.5 1.8 %collective-permute-start.12 = (bf16[32,2176]{1,0:T(8,128)(2,1)S(1)}, bf16[32,2176]{1,0:T(8,128)(2,1)S(1)}, u32[]{:S(2)}, u32[]{:S(2)}) collective-permute-start(bf16[32,2176]{1,0:T(8,128)(2,1)S(1)} %get-tuple-element.50), channel_id=1, source_target_pairs={{0,18},{1,19},{2,16},{3,17},{4,22},{5,23},{6,20},{7,21},{8,26},{9,... | collective-permute-start | bytes 417800 | tf_op jit(solution)/shard_map/ppermute | solution.py:27
  122.3 1.1 maximum_maximum_fusion.table_ref
  123.4 0.1 copy.9.time_ref
  123.5 3.4 %collective-permute-done.11.refs_1_ = bf16[32,2176]{1,0:T(8,128)(2,1)S(1)} collective-permute-done((bf16[32,2176]{1,0:T(8,128)(2,1)S(1)}, bf16[32,2176]{1,0:T(8,128)(2,1)S(1)}, u32[]{:S(2)}, u32[]{:S(2)}) %collective-permute-start.11) | collective-permute-done | bytes 139296 | tf_op jit(solution)/shard_map/ppermute | solution.py:27
  126.9 2.5 %collective-permute-done.12.refs_2_ = bf16[32,2176]{1,0:T(8,128)(2,1)S(1)} collective-permute-done((bf16[32,2176]{1,0:T(8,128)(2,1)S(1)}, bf16[32,2176]{1,0:T(8,128)(2,1)S(1)}, u32[]{:S(2)}, u32[]{:S(2)}) %collective-permute-start.12) | collective-permute-done | bytes 139296 | tf_op jit(solution)/shard_map/ppermute | solution.py:27
  129.4 11.3 %shard_map.95 = (bf16[1024,6144]{1,0:T(8,128)(2,1)}, bf16[32,2048]{1,0:T(8,128)(2,1)}) custom-call(s32[4]{0:T(128)S(1)} %pad_add_fusion.place, f32[32,2048]{1,0:T(8,128)S(1)} %get-tuple-element.46.own_ref, f32[32,128]{1,0:T(8,128)S(1)} %get-tuple-element.47.log_ref, bf16[32,2048]{1,0:T(8,128)(2,1)S(1)} %copy-done.1, s32[32,1]{1,0:T(8,128)S(1)} %copy.9.time_ref, ...), custom_call_target="tpu_custom_call" | custom-call | flops 2415919104 | bytes 16777216 | tf_op jit(solution)/shard_map/pallas_call | solution.py:432
  (37 shorter events, 0.2 us)
Async XLA Ops:
  0.6 11.5 %copy-start = (bf16[2048,384]{1,0:T(8,128)(2,1)S(1)}, bf16[2048,384]{1,0:T(8,128)(2,1)}, u32[]{:S(2)}) copy-start(bf16[2048,384]{1,0:T(8,128)(2,1)} %param.13) | copy-start | bytes 4718596
  3.1 7.8 %copy-start.1 = (bf16[32,2048]{1,0:T(8,128)(2,1)S(1)}, bf16[32,2048]{1,0:T(8,128)(2,1)}, u32[]{:S(2)}) copy-start(bf16[32,2048]{1,0:T(8,128)(2,1)} %noise_ref.1) | copy-start | bytes 393220
  3.1 8.9 %copy-start.2 = (bf16[64,2048]{1,0:T(8,128)(2,1)S(1)}, bf16[64,2048]{1,0:T(8,128)(2,1)}, u32[]{:S(2)}) copy-start(bf16[64,2048]{1,0:T(8,128)(2,1)} %param.10) | copy-start | bytes 786436
  3.1 8.9 %copy-start.5 = (bf16[32,2048]{1,0:T(8,128)(2,1)S(1)}, bf16[32,2048]{1,0:T(8,128)(2,1)}, u32[]{:S(2)}) copy-start(bf16[32,2048]{1,0:T(8,128)(2,1)} %param.11) | copy-start | bytes 393220
  3.1 8.9 %copy-start.7 = (f32[2048]{0:T(1024)S(1)}, f32[2048]{0:T(1024)}, u32[]{:S(2)}) copy-start(f32[2048]{0:T(1024)} %param.12) | copy-start | bytes 24580
  3.2 35.7 %all-to-all-start = ((bf16[16,32,2048]{2,1,0:T(8,128)(2,1)}), bf16[16,32,2048]{2,1,0:T(8,128)(2,1)}, u32[]{:S(2)}, u32[]{:S(2)}) async-start(bf16[16,32,2048]{2,1,0:T(8,128)(2,1)} %shard_map.86), calls=%async_computation | async-start | bytes 4194304 | tf_op jit(solution)/shard_map/all_to_all | solution.py:38
  11.0 2.0 %collective-permute-start = (bf16[32,2048]{1,0:T(8,128)(2,1)S(1)}, bf16[32,2048]{1,0:T(8,128)(2,1)S(1)}, u32[]{:S(2)}, u32[]{:S(2)}) collective-permute-start(bf16[32,2048]{1,0:T(8,128)(2,1)S(1)} %copy-done.1), channel_id=1, source_target_pairs={{0,1},{1,0},{2,3},{3,2},{4,5},{5,4},{6,7},{7,6},{8,9},{9,8},{10,11... | collective-permute-start | bytes 393224 | tf_op jit(solution)/shard_map/ppermute | solution.py:27
  13.0 15.9 %collective-permute-start.3 = (bf16[2,32,2048]{2,1,0:T(8,128)(2,1)S(1)}, bf16[2,32,2048]{2,1,0:T(8,128)(2,1)S(1)}, u32[]{:S(2)}, u32[]{:S(2)}) collective-permute-start(bf16[2,32,2048]{2,1,0:T(8,128)(2,1)S(1)} %pad_maximum_fusion.3.a), channel_id=1, source_target_pairs={{0,18},{1,19},{2,16},{3,17},{4,22},{5,23},{6,20},{7,21},{8,26},{9,... | collective-permute-start | bytes 786440 | tf_op jit(solution)/shard_map/ppermute | solution.py:27
  16.8 12.1 %collective-permute-start.2 = (bf16[2,32,2048]{2,1,0:T(8,128)(2,1)S(1)}, bf16[2,32,2048]{2,1,0:T(8,128)(2,1)S(1)}, u32[]{:S(2)}, u32[]{:S(2)}) collective-permute-start(bf16[2,32,2048]{2,1,0:T(8,128)(2,1)S(1)} %pad_maximum_fusion.3.a), channel_id=1, source_target_pairs={{0,16},{1,17},{2,18},{3,19},{4,20},{5,21},{6,22},{7,23},{8,24},{9,... | collective-permute-start | bytes 786440 | tf_op jit(solution)/shard_map/ppermute | solution.py:27
  16.8 12.5 %collective-permute-start.1 = (bf16[2,32,2048]{2,1,0:T(8,128)(2,1)S(1)}, bf16[2,32,2048]{2,1,0:T(8,128)(2,1)S(1)}, u32[]{:S(2)}, u32[]{:S(2)}) collective-permute-start(bf16[2,32,2048]{2,1,0:T(8,128)(2,1)S(1)} %pad_maximum_fusion.3.a), channel_id=1, source_target_pairs={{0,2},{1,3},{2,0},{3,1},{4,6},{5,7},{6,4},{7,5},{8,10},{9,11},{10,... | collective-permute-start | bytes 786440 | tf_op jit(solution)/shard_map/ppermute | solution.py:27
  38.9 2.8 %copy-start.4 = (bf16[192,384]{1,0:T(8,128)(2,1)S(1)}, bf16[192,384]{1,0:T(8,128)(2,1)}, u32[]{:S(2)}) copy-start(bf16[192,384]{1,0:T(8,128)(2,1)} %pad_maximum_fusion.4) | copy-start | bytes 442372
  41.7 14.4 %collective-permute-start.4 = (bf16[192,384]{1,0:T(8,128)(2,1)S(1)}, bf16[192,384]{1,0:T(8,128)(2,1)S(1)}, u32[]{:S(2)}, u32[]{:S(2)}) collective-permute-start(bf16[192,384]{1,0:T(8,128)(2,1)S(1)} %copy-done.4), channel_id=1, source_target_pairs={{0,1},{1,0},{2,3},{3,2},{4,5},{5,4},{6,7},{7,6},{8,9},{9,8},{10,11... | collective-permute-start | bytes 442376 | tf_op jit(solution)/shard_map/ppermute | solution.py:27
  56.1 8.0 %collective-permute-start.5 = (bf16[192,768]{1,0:T(8,128)(2,1)S(1)}, bf16[192,768]{1,0:T(8,128)(2,1)}, u32[]{:S(2)}, u32[]{:S(2)}) collective-permute-start(bf16[192,768]{1,0:T(8,128)(2,1)S(1)} %pad_maximum_fusion.2), channel_id=1, source_target_pairs={{0,2},{1,3},{2,0},{3,1},{4,6},{5,7},{6,4},{7,5},{8,10},{9,11},{10,... | collective-permute-start | bytes 884744 | tf_op jit(solution)/shard_map/ppermute | solution.py:27
  56.5 10.0 %all-to-all-start.2 = ((f32[16,8,128]{2,1,0:T(8,128)}), f32[16,8,128]{2,1,0:T(8,128)S(1)}, u32[]{:S(2)}, u32[]{:S(2)}) async-start(f32[16,8,128]{2,1,0:T(8,128)} %shard_map.88), calls=%async_computation.2 | async-start | bytes 131072 | tf_op jit(solution)/shard_map/all_to_all | solution.py:38
  65.1 49.2 %copy-start.3 = (bf16[192,1536]{1,0:T(8,128)(2,1)}, bf16[192,1536]{1,0:T(8,128)(2,1)S(1)}, u32[]{:S(2)}) copy-start(bf16[192,1536]{1,0:T(8,128)(2,1)S(1)} %pad_maximum_fusion.refs_3_) | copy-start | bytes 1769476
  66.7 23.3 %collective-permute-start.7 = (bf16[192,1536]{1,0:T(8,128)(2,1)S(1)}, bf16[192,1536]{1,0:T(8,128)(2,1)S(1)}, u32[]{:S(2)}, u32[]{:S(2)}) collective-permute-start(bf16[192,1536]{1,0:T(8,128)(2,1)S(1)} %pad_maximum_fusion.refs_3_), channel_id=1, source_target_pairs={{0,12},{1,13},{2,14},{3,15},{4,8},{5,9},{6,10},{7,11},{8,4},{9,5},... | collective-permute-start | bytes 1769480 | tf_op jit(solution)/shard_map/ppermute | solution.py:27
  67.8 22.3 %collective-permute-start.6 = (bf16[192,1536]{1,0:T(8,128)(2,1)S(1)}, bf16[192,1536]{1,0:T(8,128)(2,1)S(1)}, u32[]{:S(2)}, u32[]{:S(2)}) collective-permute-start(bf16[192,1536]{1,0:T(8,128)(2,1)S(1)} %pad_maximum_fusion.refs_3_), channel_id=1, source_target_pairs={{0,4},{1,5},{2,6},{3,7},{4,0},{5,1},{6,2},{7,3},{8,12},{9,13},{10,... | collective-permute-start | bytes 1769480 | tf_op jit(solution)/shard_map/ppermute | solution.py:27
  90.0 21.6 %copy-start.9 = (bf16[192,1536]{1,0:T(8,128)(2,1)}, bf16[192,1536]{1,0:T(8,128)(2,1)S(1)}, u32[]{:S(2)}) copy-start(bf16[192,1536]{1,0:T(8,128)(2,1)S(1)} %collective-permute-done.7.refs_6_) | copy-start | bytes 1769476
  90.0 11.4 %copy-start.10 = (bf16[192,1536]{1,0:T(8,128)(2,1)}, bf16[192,1536]{1,0:T(8,128)(2,1)S(1)}, u32[]{:S(2)}) copy-start(bf16[192,1536]{1,0:T(8,128)(2,1)S(1)} %collective-permute-done.6.refs_4_) | copy-start | bytes 1769476
  90.3 21.3 %collective-permute-start.8 = (bf16[192,1536]{1,0:T(8,128)(2,1)S(1)}, bf16[192,1536]{1,0:T(8,128)(2,1)}, u32[]{:S(2)}, u32[]{:S(2)}) collective-permute-start(bf16[192,1536]{1,0:T(8,128)(2,1)S(1)} %pad_maximum_fusion.refs_3_), channel_id=1, source_target_pairs={{0,8},{1,9},{2,10},{3,11},{4,12},{5,13},{6,14},{7,15},{8,0},{9,1},... | collective-permute-start | bytes 1769480 | tf_op jit(solution)/shard_map/ppermute | solution.py:27
  111.6 10.7 %copy-start.6 = (bf16[32,2048]{1,0:T(8,128)(2,1)S(1)}, bf16[32,2048]{1,0:T(8,128)(2,1)}, u32[]{:S(2)}) copy-start(bf16[32,2048]{1,0:T(8,128)(2,1)} %param.11) | copy-start | bytes 393220
  114.3 9.2 %copy-start.8 = (s32[32]{0:T(128)S(1)}, s32[32]{0:T(128)}, u32[]{:S(2)}) copy-start(s32[32]{0:T(128)} %param.9) | copy-start | bytes 388
  114.3 3.7 %collective-permute-start.9 = (bf16[4,32,2176]{2,1,0:T(8,128)(2,1)S(1)}, bf16[4,32,2176]{2,1,0:T(8,128)(2,1)S(1)}, u32[]{:S(2)}, u32[]{:S(2)}) collective-permute-start(bf16[4,32,2176]{2,1,0:T(8,128)(2,1)S(1)} %get-tuple-element.45), channel_id=1, source_target_pairs={{0,1},{1,0},{2,3},{3,2},{4,5},{5,4},{6,7},{7,6},{8,9},{9,8},{10,11... | collective-permute-start | bytes 1671176 | tf_op jit(solution)/shard_map/ppermute | solution.py:27
  118.3 5.2 %collective-permute-start.10 = (bf16[32,2176]{1,0:T(8,128)(2,1)S(1)}, bf16[32,2176]{1,0:T(8,128)(2,1)S(1)}, u32[]{:S(2)}, u32[]{:S(2)}) collective-permute-start(bf16[32,2176]{1,0:T(8,128)(2,1)S(1)} %get-tuple-element.48), channel_id=1, source_target_pairs={{0,2},{1,3},{2,0},{3,1},{4,6},{5,7},{6,4},{7,5},{8,10},{9,11},{10,... | collective-permute-start | bytes 417800 | tf_op jit(solution)/shard_map/ppermute | solution.py:27
  118.7 8.2 %collective-permute-start.11 = (bf16[32,2176]{1,0:T(8,128)(2,1)S(1)}, bf16[32,2176]{1,0:T(8,128)(2,1)S(1)}, u32[]{:S(2)}, u32[]{:S(2)}) collective-permute-start(bf16[32,2176]{1,0:T(8,128)(2,1)S(1)} %get-tuple-element.49), channel_id=1, source_target_pairs={{0,16},{1,17},{2,18},{3,19},{4,20},{5,21},{6,22},{7,23},{8,24},{9,... | collective-permute-start | bytes 417800 | tf_op jit(solution)/shard_map/ppermute | solution.py:27
  120.5 8.9 %collective-permute-start.12 = (bf16[32,2176]{1,0:T(8,128)(2,1)S(1)}, bf16[32,2176]{1,0:T(8,128)(2,1)S(1)}, u32[]{:S(2)}, u32[]{:S(2)}) collective-permute-start(bf16[32,2176]{1,0:T(8,128)(2,1)S(1)} %get-tuple-element.50), channel_id=1, source_target_pairs={{0,18},{1,19},{2,16},{3,17},{4,22},{5,23},{6,20},{7,21},{8,26},{9,... | collective-permute-start | bytes 417800 | tf_op jit(solution)/shard_map/ppermute | solution.py:27

commit v6 on v5

--- a/solution.py
+++ b/solution.py
@@ -116,22 +116,28 @@
     return peak + jnp.log(jnp.sum(jnp.exp(parts - peak[None]), axis=0))
 
 
-def cost_kernel(place, data_ref, a, b, c, d, cost_ref, lse_ref, noise_ref):
+def square_sum(value):
+    total = jnp.zeros((value.shape[0], 128), F32)
+    for tile in range(value.shape[1] // 128):
+        part = value[:, tile * 128 : (tile + 1) * 128].astype(F32)
+        total = total + part * part
+    return jnp.sum(total, axis=1, keepdims=True)
+
+
+def noise_kernel(place, a, b, c, d, noise_ref, square_ref):
     h = place[2]
     rows, latent = a.shape[1:]
     for k, pair in enumerate((a, b, c, d)):
         noise_ref[h ^ (2 * k)] = pair[0]
         noise_ref[h ^ (2 * k + 1)] = pair[1]
+    squares = square_sum(noise_ref[...].reshape(8 * rows, latent))
+    square_ref[...] = jnp.broadcast_to(squares, square_ref.shape)
+
+
+def cost_kernel(data_ref, noise_ref, square_ref, cost_ref, lse_ref):
+    rows, latent = noise_ref.shape[1:]
     noise = noise_ref[...].reshape(8 * rows, latent)
 
-    def square_sum(value):
-        total = jnp.zeros((value.shape[0], 128), F32)
-        for tile in range(latent // 128):
-            part = value[:, tile * 128 : (tile + 1) * 128].astype(F32)
-            total = total + part * part
-        return jnp.sum(total, axis=1, keepdims=True)
-
-    noise_sq = square_sum(noise)
     for group in range(2):
         part = data_ref[group * 8 : group * 8 + 8].reshape(8 * rows, latent)
         cross = lax.dot_general(
@@ -141,7 +147,7 @@
             data_sq = to_lanes(square_sum(part[side * 128 : side * 128 + 128]))
             at = group * 256 + side * 128
             cost_ref[:, at : at + 128] = (
-                noise_sq + data_sq - 2.0 * cross[:, side * 128 : side * 128 + 128]
+                square_ref[...] + data_sq - 2.0 * cross[:, side * 128 : side * 128 + 128]
             ) / latent
     pack(row_lse(cost_ref, None, 1.0 / epsilon_of(0)), lse_ref)
 
@@ -211,21 +217,32 @@
     return jnp.sum(ref_value.astype(F32), axis=1, keepdims=True)
 
 
-def pair_kernel(keep_ref, log_ref, got_ref, own_ref, own_log_ref, s1, s2, s3):
+def pair_parts(keep_ref, log_ref, got_ref, k):
     latent = keep_ref.shape[2]
-    for k, out in enumerate((own_ref, s1, s2, s3)):
-        first = log_ref[k]
-        second = jnp.broadcast_to(read_log(got_ref[k, :, latent : latent + 128]), first.shape)
-        total = join_lse([first, second])
-        mixed = keep_ref[k] * jnp.exp(first - total)[:, 0:1] + got_ref[
-            k, :, 0:latent
-        ].astype(F32) * jnp.exp(second - total)[:, 0:1]
-        if k == 0:
-            out[...] = mixed
-            own_log_ref[...] = total
-        else:
-            out[:, 0:latent] = mixed.astype(BF)
-            out[:, latent : latent + 128] = packed_log(total)
+    first = log_ref[k]
+    second = jnp.broadcast_to(read_log(got_ref[k, :, latent : latent + 128]), first.shape)
+    total = join_lse([first, second])
+    mixed = keep_ref[k] * jnp.exp(first - total)[:, 0:1] + got_ref[k, :, 0:latent].astype(
+        F32
+    ) * jnp.exp(second - total)[:, 0:1]
+    return mixed, total
+
+
+def pair_send(keep_ref, log_ref, got_ref, k, out):
+    latent = keep_ref.shape[2]
+    mixed, total = pair_parts(keep_ref, log_ref, got_ref, k)
+    out[:, 0:latent] = mixed.astype(BF)
+    out[:, latent : latent + 128] = packed_log(total)
+
+
+def far_kernel(keep_ref, log_ref, got_ref, out):
+    pair_send(keep_ref, log_ref, got_ref, 2, out)
+
+
+def pair_kernel(keep_ref, log_ref, got_ref, own_ref, own_log_ref, s1, s3):
+    own_ref[...], own_log_ref[...] = pair_parts(keep_ref, log_ref, got_ref, 0)
+    pair_send(keep_ref, log_ref, got_ref, 1, s1)
+    pair_send(keep_ref, log_ref, got_ref, 3, s3)
 
 
 def spread_kernel(value_ref, out_ref, sems):
@@ -345,15 +362,20 @@
     )(data)
     data_all = exchange(spread, COL_MASK)
     flops = 2 * 8 * rows * 16 * rows * latent
+    noise_all, squares = vmem_call(
+        noise_kernel,
+        (shape((8, rows, latent), BF), shape((8 * rows, 128))),
+        smem=1,
+        inputs=4,
+        nbytes=2 * 1024 * 1024,
+    )(place, *noises)
     cost, row_part = vmem_call(
         cost_kernel,
         (shape((8 * rows, 16 * rows)), shape((8, 8, 128))),
-        scratch=[pltpu.VMEM((8, rows, latent), BF)],
-        smem=1,
-        inputs=5,
+        inputs=3,
         flops=flops,
         nbytes=4 * 1024 * 1024,
-    )(place, data_all, *noises)
+    )(data_all, noise_all, squares)
     quads = [None] * 4
     folded, row_part = together(folded, row_part)
     folded = jnp.concatenate([folded, swap(folded, CORE)], 1)
@@ -402,13 +424,17 @@
         flops=flops,
         nbytes=6 * 1024 * 1024,
     )(place, cost, data_all, col_parts)
+    got = swap(send, CORE)
+    message = shape((rows, latent + 128), BF)
+    far_send = vmem_call(far_kernel, message, inputs=3, nbytes=1024 * 1024)(keep, log, got)
+    far_send, keep = together(far_send, keep)
     own, own_log, *sends = vmem_call(
         pair_kernel,
-        (shape((rows, latent)), shape((rows, 128))) + (shape((rows, latent + 128), BF),) * 3,
+        (shape((rows, latent)), shape((rows, 128)), message, message),
         inputs=3,
         nbytes=2 * 1024 * 1024,
-    )(keep, log, swap(send, CORE))
-    others = [swap(value, mask) for value, mask in zip(sends, Z_STEPS)]
+    )(keep, log, got)
+    others = [swap(sends[0], Z_STEPS[0]), swap(far_send, Z_STEPS[1]), swap(sends[1], Z_STEPS[2])]
     return [own, own_log] + others, quads
 
 

time: 141 us -> 140 us (level)
  waiting for transfers between devices: 33.5 us -> 29.1 us
  local copies, waits for them, and re-layouts: 0.33 us -> 1.99 us
    all_to_all x2, waiting for transfers between devices: 10.9 us -> 8.31 us  [exchange(): lax.all_to_all(value, BOTH, 0, 0, axis_index_groups=groups_by(mask), tile...]
    ppermute x13, waiting for transfers between devices: 22.6 us -> 20.8 us  [swap(): return lax.ppermute(value, BOTH, [(i, i ^ mask) for i in range(128)])]
    unnamed x22 -> x30, local copies, waits for them, and re-layouts: 0.06 us -> 1.72 us
  transfers between devices with their start and end apart: 15 -> 15, of which waited for: 9 -> 10; matrix products, arithmetic and copies ran while one was open for 3% -> 3% of each run, Pallas kernels for 1% -> 2%
where the time goes in v6:
time: 140 us; the launch traced here: 138 us
  blocking collectives  51.7 us (37%)
  waiting for transfers between devices  29.1 us (21%)
  starting transfers between devices  28.4 us (20%)
  Pallas kernels  22.5 us (16%)
  other arithmetic  3.09 us (2%)
  local copies, waits for them, and re-layouts  1.99 us (1%)
    all_to_all x5, blocking collectives, exchange(): lax.all_to_all(value, BOTH, 0, 0, axis_index_groups=groups_by(mask), tile...  51.7 us
    ppermute x13, waiting for transfers between devices, swap(): return lax.ppermute(value, BOTH, [(i, i ^ mask) for i in range(128)])  20.8 us
    ppermute x13, starting transfers between devices, swap(): return lax.ppermute(value, BOTH, [(i, i ^ mask) for i in range(128)])  17.1 us
    all_to_all x2, starting transfers between devices, exchange(): lax.all_to_all(value, BOTH, 0, 0, axis_index_groups=groups_by(mask), tile...  11.3 us
    pallas_call x1, Pallas kernels, local(): pl.pallas_call(qkv_kernel, out_shape=(shape((own * patch_count, columns),...  11.3 us
    all_to_all x2, waiting for transfers between devices, exchange(): lax.all_to_all(value, BOTH, 0, 0, axis_index_groups=groups_by(mask), tile...  8.31 us
  transfers between devices with their start and end apart: 15, of which 10 were waited for; matrix products, arithmetic and copies ran while one was open for 3% of the time, Pallas kernels for 2%

profile of v6, /device:TPU:1, one launch (start us, length us, event | category | flops | bytes accessed | tf_op | source)
XLA Modules:
  0.0 138.3 jit_solution(3700840665181339691)
XLA Ops:
  0.6 2.5 %shard_map.86 = bf16[16,32,2048]{2,1,0:T(8,128)(2,1)} custom-call(bf16[32,2048]{1,0:T(8,128)(2,1)} %value_ref.1), custom_call_target="tpu_custom_call" | custom-call | tf_op jit(solution)/shard_map/pallas_call | solution.py:356
  3.2 7.8 %all-to-all-start = ((bf16[16,32,2048]{2,1,0:T(8,128)(2,1)}), bf16[16,32,2048]{2,1,0:T(8,128)(2,1)}, u32[]{:S(2)}, u32[]{:S(2)}) async-start(bf16[16,32,2048]{2,1,0:T(8,128)(2,1)} %shard_map.86), calls=%async_computation | async-start | bytes 4194304 | tf_op jit(solution)/shard_map/all_to_all | solution.py:38
  11.0 1.0 collective-permute-start
  12.0 0.1 fusion.4
  12.1 0.6 fusion
  12.7 0.2 collective-permute-done
  13.0 3.8 %collective-permute-start.3 = (bf16[2,32,2048]{2,1,0:T(8,128)(2,1)S(1)}, bf16[2,32,2048]{2,1,0:T(8,128)(2,1)S(1)}, u32[]{:S(2)}, u32[]{:S(2)}) collective-permute-start(bf16[2,32,2048]{2,1,0:T(8,128)(2,1)S(1)} %pad_maximum_fusion.3.a), channel_id=1, source_target_pairs={{0,18},{1,19},{2,16},{3,17},{4,22},{5,23},{6,20},{7,21},{8,26},{9,... | collective-permute-start | bytes 786440 | tf_op jit(solution)/shard_map/ppermute | solution.py:27
  16.8 0.7 collective-permute-start.1
  17.7 0.7 pad_maximum_fusion.4
  18.4 10.5 %collective-permute-done.3.d = bf16[2,32,2048]{2,1,0:T(8,128)(2,1)S(1)} collective-permute-done((bf16[2,32,2048]{2,1,0:T(8,128)(2,1)S(1)}, bf16[2,32,2048]{2,1,0:T(8,128)(2,1)S(1)}, u32[]{:S(2)}, u32[]{:S(2)}) %collective-permute-start.3) | collective-permute-done | bytes 262176 | tf_op jit(solution)/shard_map/ppermute | solution.py:27
  29.0 0.4 collective-permute-done.1.b
  29.4 0.7 copy-done.1
  30.1 0.9 copy-done.2
  31.0 0.9 shard_map.87
  31.9 7.0 %all-to-all-done.data_ref = bf16[16,32,2048]{2,1,0:T(8,128)(2,1)} async-done(((bf16[16,32,2048]{2,1,0:T(8,128)(2,1)}), bf16[16,32,2048]{2,1,0:T(8,128)(2,1)}, u32[]{:S(2)}, u32[]{:S(2)}) %all-to-all-start) | async-done | bytes 2097184 | tf_op jit(solution)/shard_map/all_to_all | solution.py:38
  38.9 2.7 %shard_map.88 = (f32[256,512]{1,0:T(8,128)S(1)}, f32[8,8,128]{2,1,0:T(8,128)S(1)}) custom-call(bf16[16,32,2048]{2,1,0:T(8,128)(2,1)} %all-to-all-done.data_ref, bf16[8,32,2048]{2,1,0:T(8,128)(2,1)S(1)} %get-tuple-element.32.noise_ref, f32[256,128]{1,0:T(8,128)S(1)} %get-tuple-element.33.square_ref), custom_call_target="tpu_custom_call" | custom-call | flops 536870912 | bytes 4194304 | tf_op jit(solution)/shard_map/pallas_call | solution.py:372
  41.6 3.5 %collective-permute-start.4 = (bf16[192,384]{1,0:T(8,128)(2,1)S(1)}, bf16[192,384]{1,0:T(8,128)(2,1)S(1)}, u32[]{:S(2)}, u32[]{:S(2)}) collective-permute-start(bf16[192,384]{1,0:T(8,128)(2,1)S(1)} %copy-done.8), channel_id=1, source_target_pairs={{0,1},{1,0},{2,3},{3,2},{4,5},{5,4},{6,7},{7,6},{8,9},{9,8},{10,11... | collective-permute-start | bytes 442376 | tf_op jit(solution)/shard_map/ppermute | solution.py:27
  45.2 9.9 %all_to_all.35.parts_ref = f32[8,8,128]{2,1,0:T(8,128)S(1)} all-to-all(f32[8,8,128]{2,1,0:T(8,128)S(1)} %get-tuple-element.37), channel_id=1, replica_groups={{0,1,2,3,16,17,18,19},{4,5,6,7,20,21,22,23},{8,9,10,11,24,25,26,27},{12..., dimensions={0} | all-to-all | bytes 65536 | tf_op jit(solution)/shard_map/all_to_all | solution.py:38
  55.1 0.9 shard_map.89
  56.0 0.4 collective-permute-start.5
  56.4 3.5 %all-to-all-start.2 = ((f32[16,8,128]{2,1,0:T(8,128)}), f32[16,8,128]{2,1,0:T(8,128)S(1)}, u32[]{:S(2)}, u32[]{:S(2)}) async-start(f32[16,8,128]{2,1,0:T(8,128)} %shard_map.89), calls=%async_computation.2 | async-start | bytes 131072 | tf_op jit(solution)/shard_map/all_to_all | solution.py:38
  59.9 4.1 %collective-permute-done.5 = bf16[192,768]{1,0:T(8,128)(2,1)} collective-permute-done((bf16[192,768]{1,0:T(8,128)(2,1)S(1)}, bf16[192,768]{1,0:T(8,128)(2,1)}, u32[]{:S(2)}, u32[]{:S(2)}) %collective-permute-start.5) | collective-permute-done | bytes 294944 | tf_op jit(solution)/shard_map/ppermute | solution.py:27
  64.0 1.0 pad_maximum_fusion.refs_3_
  65.0 1.3 all-to-all-done.2.parts_ref
  66.3 0.3 shard_map.90
  66.6 1.0 collective-permute-start.7
  67.7 10.6 %all_to_all.36.parts_ref = f32[8,8,128]{2,1,0:T(8,128)S(1)} all-to-all(f32[8,8,128]{2,1,0:T(8,128)S(1)} %shard_map.90), channel_id=1, replica_groups={{0,1,2,3,16,17,18,19},{4,5,6,7,20,21,22,23},{8,9,10,11,24,25,26,27},{12..., dimensions={0} | all-to-all | bytes 65536 | tf_op jit(solution)/shard_map/all_to_all | solution.py:38
  78.2 0.3 shard_map.91
  78.5 11.4 %all_to_all.37.parts_ref = f32[16,8,128]{2,1,0:T(8,128)S(1)} all-to-all(f32[16,8,128]{2,1,0:T(8,128)S(1)} %shard_map.91), channel_id=1, replica_groups={{0,4,8,12,32,36,40,44,64,68,72,76,96,100,104,108},{1,5,9,13,33,37,41,45..., dimensions={0} | all-to-all | bytes 131072 | tf_op jit(solution)/shard_map/all_to_all | solution.py:38
  90.0 0.3 shard_map.92
  90.3 1.2 collective-permute-start.8
  91.5 9.9 %all_to_all.38.parts_ref = f32[8,8,128]{2,1,0:T(8,128)S(1)} all-to-all(f32[8,8,128]{2,1,0:T(8,128)S(1)} %shard_map.92), channel_id=1, replica_groups={{0,1,2,3,16,17,18,19},{4,5,6,7,20,21,22,23},{8,9,10,11,24,25,26,27},{12..., dimensions={0} | all-to-all | bytes 65536 | tf_op jit(solution)/shard_map/all_to_all | solution.py:38
  101.3 0.3 shard_map.93
  101.6 9.9 %all_to_all.39.parts_ref = f32[16,8,128]{2,1,0:T(8,128)S(1)} all-to-all(f32[16,8,128]{2,1,0:T(8,128)S(1)} %shard_map.93), channel_id=1, replica_groups={{0,4,8,12,32,36,40,44,64,68,72,76,96,100,104,108},{1,5,9,13,33,37,41,45..., dimensions={0} | all-to-all | bytes 131072 | tf_op jit(solution)/shard_map/all_to_all | solution.py:38
  111.5 2.6 %shard_map.94 = (f32[4,32,2048]{2,1,0:T(8,128)S(1)}, f32[4,32,128]{2,1,0:T(8,128)S(1)}, bf16[4,32,2176]{2,1,0:T(8,128)(2,1)S(1)}) custom-call(s32[4]{0:T(128)S(1)} %pad_add_fusion.place, f32[256,512]{1,0:T(8,128)S(1)} %get-tuple-element.34.cost_ref, bf16[16,32,2048]{2,1,0:T(8,128)(2,1)} %all-to-all-done.data_ref, f32[16,8,128]{2,1,0:T(8,128)S(1)} %all_to_all.39.parts_ref), custom_call_target="tpu_custom_call" | custom-call | flops 536870912 | bytes 6291456 | tf_op jit(solution)/shard_map/pallas_call | solution.py:410
  114.1 2.1 %collective-permute-start.9 = (bf16[4,32,2176]{2,1,0:T(8,128)(2,1)S(1)}, bf16[4,32,2176]{2,1,0:T(8,128)(2,1)S(1)}, u32[]{:S(2)}, u32[]{:S(2)}) collective-permute-start(bf16[4,32,2176]{2,1,0:T(8,128)(2,1)S(1)} %get-tuple-element.50), channel_id=1, source_target_pairs={{0,1},{1,0},{2,3},{3,2},{4,5},{5,4},{6,7},{7,6},{8,9},{9,8},{10,11... | collective-permute-start | bytes 1671176 | tf_op jit(solution)/shard_map/ppermute | solution.py:27
  116.4 1.4 %collective-permute-done.9.got_ref = bf16[4,32,2176]{2,1,0:T(8,128)(2,1)S(1)} collective-permute-done((bf16[4,32,2176]{2,1,0:T(8,128)(2,1)S(1)}, bf16[4,32,2176]{2,1,0:T(8,128)(2,1)S(1)}, u32[]{:S(2)}, u32[]{:S(2)}) %collective-permute-start.9) | collective-permute-done | bytes 557088 | tf_op jit(solution)/shard_map/ppermute | solution.py:27
  117.9 0.2 shard_map.95
  118.1 0.3 shard_map.96
  118.4 0.4 collective-permute-start.10
  118.8 0.8 collective-permute-start.12
  119.6 2.2 %collective-permute-start.11 = (bf16[32,2176]{1,0:T(8,128)(2,1)S(1)}, bf16[32,2176]{1,0:T(8,128)(2,1)S(1)}, u32[]{:S(2)}, u32[]{:S(2)}) collective-permute-start(bf16[32,2176]{1,0:T(8,128)(2,1)S(1)} %shard_map.95), channel_id=1, source_target_pairs={{0,16},{1,17},{2,18},{3,19},{4,20},{5,21},{6,22},{7,23},{8,24},{9,... | collective-permute-start | bytes 417800 | tf_op jit(solution)/shard_map/ppermute | solution.py:27
  121.8 1.1 maximum_maximum_fusion.table_ref
  122.9 0.1 copy.9.time_ref
  123.0 0.4 collective-permute-done.10.refs_0_
  123.4 1.7 %collective-permute-done.12.refs_2_ = bf16[32,2176]{1,0:T(8,128)(2,1)S(1)} collective-permute-done((bf16[32,2176]{1,0:T(8,128)(2,1)S(1)}, bf16[32,2176]{1,0:T(8,128)(2,1)S(1)}, u32[]{:S(2)}, u32[]{:S(2)}) %collective-permute-start.12) | collective-permute-done | bytes 139296 | tf_op jit(solution)/shard_map/ppermute | solution.py:27
  125.2 1.9 %collective-permute-done.11.refs_1_ = bf16[32,2176]{1,0:T(8,128)(2,1)S(1)} collective-permute-done((bf16[32,2176]{1,0:T(8,128)(2,1)S(1)}, bf16[32,2176]{1,0:T(8,128)(2,1)S(1)}, u32[]{:S(2)}, u32[]{:S(2)}) %collective-permute-start.11) | collective-permute-done | bytes 139296 | tf_op jit(solution)/shard_map/ppermute | solution.py:27
  127.0 11.3 %shard_map.97 = (bf16[1024,6144]{1,0:T(8,128)(2,1)}, bf16[32,2048]{1,0:T(8,128)(2,1)}) custom-call(s32[4]{0:T(128)S(1)} %pad_add_fusion.place, f32[32,2048]{1,0:T(8,128)S(1)} %get-tuple-element.52.own_ref, f32[32,128]{1,0:T(8,128)S(1)} %get-tuple-element.53.log_ref, bf16[32,2048]{1,0:T(8,128)(2,1)S(1)} %copy-done.4, s32[32,1]{1,0:T(8,128)S(1)} %copy.9.time_ref, ...), custom_call_target="tpu_custom_call" | custom-call | flops 2415919104 | bytes 16777216 | tf_op jit(solution)/shard_map/pallas_call | solution.py:458
  (47 shorter events, 0.4 us)
Async XLA Ops:
  0.6 11.5 %copy-start = (bf16[2048,384]{1,0:T(8,128)(2,1)S(1)}, bf16[2048,384]{1,0:T(8,128)(2,1)}, u32[]{:S(2)}) copy-start(bf16[2048,384]{1,0:T(8,128)(2,1)} %param.13) | copy-start | bytes 4718596
  3.1 7.8 %copy-start.3 = (bf16[32,2048]{1,0:T(8,128)(2,1)S(1)}, bf16[32,2048]{1,0:T(8,128)(2,1)}, u32[]{:S(2)}) copy-start(bf16[32,2048]{1,0:T(8,128)(2,1)} %noise_ref.1) | copy-start | bytes 393220
  3.1 8.9 %copy-start.5 = (bf16[64,2048]{1,0:T(8,128)(2,1)S(1)}, bf16[64,2048]{1,0:T(8,128)(2,1)}, u32[]{:S(2)}) copy-start(bf16[64,2048]{1,0:T(8,128)(2,1)} %param.10) | copy-start | bytes 786436
  3.1 8.9 %copy-start.9 = (bf16[32,2048]{1,0:T(8,128)(2,1)S(1)}, bf16[32,2048]{1,0:T(8,128)(2,1)}, u32[]{:S(2)}) copy-start(bf16[32,2048]{1,0:T(8,128)(2,1)} %param.11) | copy-start | bytes 393220
  3.1 8.9 %copy-start.11 = (f32[2048]{0:T(1024)S(1)}, f32[2048]{0:T(1024)}, u32[]{:S(2)}) copy-start(f32[2048]{0:T(1024)} %param.12) | copy-start | bytes 24580
  3.2 35.7 %all-to-all-start = ((bf16[16,32,2048]{2,1,0:T(8,128)(2,1)}), bf16[16,32,2048]{2,1,0:T(8,128)(2,1)}, u32[]{:S(2)}, u32[]{:S(2)}) async-start(bf16[16,32,2048]{2,1,0:T(8,128)(2,1)} %shard_map.86), calls=%async_computation | async-start | bytes 4194304 | tf_op jit(solution)/shard_map/all_to_all | solution.py:38
  11.0 2.0 %collective-permute-start = (bf16[32,2048]{1,0:T(8,128)(2,1)S(1)}, bf16[32,2048]{1,0:T(8,128)(2,1)S(1)}, u32[]{:S(2)}, u32[]{:S(2)}) collective-permute-start(bf16[32,2048]{1,0:T(8,128)(2,1)S(1)} %copy-done.3), channel_id=1, source_target_pairs={{0,1},{1,0},{2,3},{3,2},{4,5},{5,4},{6,7},{7,6},{8,9},{9,8},{10,11... | collective-permute-start | bytes 393224 | tf_op jit(solution)/shard_map/ppermute | solution.py:27
  13.0 15.9 %collective-permute-start.3 = (bf16[2,32,2048]{2,1,0:T(8,128)(2,1)S(1)}, bf16[2,32,2048]{2,1,0:T(8,128)(2,1)S(1)}, u32[]{:S(2)}, u32[]{:S(2)}) collective-permute-start(bf16[2,32,2048]{2,1,0:T(8,128)(2,1)S(1)} %pad_maximum_fusion.3.a), channel_id=1, source_target_pairs={{0,18},{1,19},{2,16},{3,17},{4,22},{5,23},{6,20},{7,21},{8,26},{9,... | collective-permute-start | bytes 786440 | tf_op jit(solution)/shard_map/ppermute | solution.py:27
  16.8 12.1 %collective-permute-start.2 = (bf16[2,32,2048]{2,1,0:T(8,128)(2,1)S(1)}, bf16[2,32,2048]{2,1,0:T(8,128)(2,1)S(1)}, u32[]{:S(2)}, u32[]{:S(2)}) collective-permute-start(bf16[2,32,2048]{2,1,0:T(8,128)(2,1)S(1)} %pad_maximum_fusion.3.a), channel_id=1, source_target_pairs={{0,16},{1,17},{2,18},{3,19},{4,20},{5,21},{6,22},{7,23},{8,24},{9,... | collective-permute-start | bytes 786440 | tf_op jit(solution)/shard_map/ppermute | solution.py:27
  16.8 12.5 %collective-permute-start.1 = (bf16[2,32,2048]{2,1,0:T(8,128)(2,1)S(1)}, bf16[2,32,2048]{2,1,0:T(8,128)(2,1)S(1)}, u32[]{:S(2)}, u32[]{:S(2)}) collective-permute-start(bf16[2,32,2048]{2,1,0:T(8,128)(2,1)S(1)} %pad_maximum_fusion.3.a), channel_id=1, source_target_pairs={{0,2},{1,3},{2,0},{3,1},{4,6},{5,7},{6,4},{7,5},{8,10},{9,11},{10,... | collective-permute-start | bytes 786440 | tf_op jit(solution)/shard_map/ppermute | solution.py:27
  29.3 0.7 copy-start.1
  30.0 0.9 copy-start.2
  38.9 2.7 %copy-start.8 = (bf16[192,384]{1,0:T(8,128)(2,1)S(1)}, bf16[192,384]{1,0:T(8,128)(2,1)}, u32[]{:S(2)}) copy-start(bf16[192,384]{1,0:T(8,128)(2,1)} %pad_maximum_fusion.4) | copy-start | bytes 442372
  41.6 14.4 %collective-permute-start.4 = (bf16[192,384]{1,0:T(8,128)(2,1)S(1)}, bf16[192,384]{1,0:T(8,128)(2,1)S(1)}, u32[]{:S(2)}, u32[]{:S(2)}) collective-permute-start(bf16[192,384]{1,0:T(8,128)(2,1)S(1)} %copy-done.8), channel_id=1, source_target_pairs={{0,1},{1,0},{2,3},{3,2},{4,5},{5,4},{6,7},{7,6},{8,9},{9,8},{10,11... | collective-permute-start | bytes 442376 | tf_op jit(solution)/shard_map/ppermute | solution.py:27
  56.0 8.0 %collective-permute-start.5 = (bf16[192,768]{1,0:T(8,128)(2,1)S(1)}, bf16[192,768]{1,0:T(8,128)(2,1)}, u32[]{:S(2)}, u32[]{:S(2)}) collective-permute-start(bf16[192,768]{1,0:T(8,128)(2,1)S(1)} %pad_maximum_fusion.2), channel_id=1, source_target_pairs={{0,2},{1,3},{2,0},{3,1},{4,6},{5,7},{6,4},{7,5},{8,10},{9,11},{10,... | collective-permute-start | bytes 884744 | tf_op jit(solution)/shard_map/ppermute | solution.py:27
  56.4 10.0 %all-to-all-start.2 = ((f32[16,8,128]{2,1,0:T(8,128)}), f32[16,8,128]{2,1,0:T(8,128)S(1)}, u32[]{:S(2)}, u32[]{:S(2)}) async-start(f32[16,8,128]{2,1,0:T(8,128)} %shard_map.89), calls=%async_computation.2 | async-start | bytes 131072 | tf_op jit(solution)/shard_map/all_to_all | solution.py:38
  65.0 49.1 %copy-start.7 = (bf16[192,1536]{1,0:T(8,128)(2,1)}, bf16[192,1536]{1,0:T(8,128)(2,1)S(1)}, u32[]{:S(2)}) copy-start(bf16[192,1536]{1,0:T(8,128)(2,1)S(1)} %pad_maximum_fusion.refs_3_) | copy-start | bytes 1769476
  66.6 23.3 %collective-permute-start.7 = (bf16[192,1536]{1,0:T(8,128)(2,1)S(1)}, bf16[192,1536]{1,0:T(8,128)(2,1)S(1)}, u32[]{:S(2)}, u32[]{:S(2)}) collective-permute-start(bf16[192,1536]{1,0:T(8,128)(2,1)S(1)} %pad_maximum_fusion.refs_3_), channel_id=1, source_target_pairs={{0,12},{1,13},{2,14},{3,15},{4,8},{5,9},{6,10},{7,11},{8,4},{9,5},... | collective-permute-start | bytes 1769480 | tf_op jit(solution)/shard_map/ppermute | solution.py:27
  67.7 22.3 %collective-permute-start.6 = (bf16[192,1536]{1,0:T(8,128)(2,1)S(1)}, bf16[192,1536]{1,0:T(8,128)(2,1)S(1)}, u32[]{:S(2)}, u32[]{:S(2)}) collective-permute-start(bf16[192,1536]{1,0:T(8,128)(2,1)S(1)} %pad_maximum_fusion.refs_3_), channel_id=1, source_target_pairs={{0,4},{1,5},{2,6},{3,7},{4,0},{5,1},{6,2},{7,3},{8,12},{9,13},{10,... | collective-permute-start | bytes 1769480 | tf_op jit(solution)/shard_map/ppermute | solution.py:27
  90.0 21.6 %copy-start.13 = (bf16[192,1536]{1,0:T(8,128)(2,1)}, bf16[192,1536]{1,0:T(8,128)(2,1)S(1)}, u32[]{:S(2)}) copy-start(bf16[192,1536]{1,0:T(8,128)(2,1)S(1)} %collective-permute-done.7.refs_6_) | copy-start | bytes 1769476
  90.0 21.6 %copy-start.14 = (bf16[192,1536]{1,0:T(8,128)(2,1)}, bf16[192,1536]{1,0:T(8,128)(2,1)S(1)}, u32[]{:S(2)}) copy-start(bf16[192,1536]{1,0:T(8,128)(2,1)S(1)} %collective-permute-done.6.refs_4_) | copy-start | bytes 1769476
  90.3 21.3 %collective-permute-start.8 = (bf16[192,1536]{1,0:T(8,128)(2,1)S(1)}, bf16[192,1536]{1,0:T(8,128)(2,1)}, u32[]{:S(2)}, u32[]{:S(2)}) collective-permute-start(bf16[192,1536]{1,0:T(8,128)(2,1)S(1)} %pad_maximum_fusion.refs_3_), channel_id=1, source_target_pairs={{0,8},{1,9},{2,10},{3,11},{4,12},{5,13},{6,14},{7,15},{8,0},{9,1},... | collective-permute-start | bytes 1769480 | tf_op jit(solution)/shard_map/ppermute | solution.py:27
  114.1 3.7 %collective-permute-start.9 = (bf16[4,32,2176]{2,1,0:T(8,128)(2,1)S(1)}, bf16[4,32,2176]{2,1,0:T(8,128)(2,1)S(1)}, u32[]{:S(2)}, u32[]{:S(2)}) collective-permute-start(bf16[4,32,2176]{2,1,0:T(8,128)(2,1)S(1)} %get-tuple-element.50), channel_id=1, source_target_pairs={{0,1},{1,0},{2,3},{3,2},{4,5},{5,4},{6,7},{7,6},{8,9},{9,8},{10,11... | collective-permute-start | bytes 1671176 | tf_op jit(solution)/shard_map/ppermute | solution.py:27
  117.9 3.9 %copy-start.6 = (bf16[64,2048]{1,0:T(8,128)(2,1)S(1)}, bf16[64,2048]{1,0:T(8,128)(2,1)}, u32[]{:S(2)}) copy-start(bf16[64,2048]{1,0:T(8,128)(2,1)} %param.10) | copy-start | bytes 786436
  117.9 3.9 %copy-start.10 = (bf16[32,2048]{1,0:T(8,128)(2,1)S(1)}, bf16[32,2048]{1,0:T(8,128)(2,1)}, u32[]{:S(2)}) copy-start(bf16[32,2048]{1,0:T(8,128)(2,1)} %param.11) | copy-start | bytes 393220
  118.1 4.8 %copy-start.12 = (s32[32]{0:T(128)S(1)}, s32[32]{0:T(128)}, u32[]{:S(2)}) copy-start(s32[32]{0:T(128)} %param.9) | copy-start | bytes 388
  118.1 8.9 %copy-start.4 = (bf16[32,2048]{1,0:T(8,128)(2,1)S(1)}, bf16[32,2048]{1,0:T(8,128)(2,1)}, u32[]{:S(2)}) copy-start(bf16[32,2048]{1,0:T(8,128)(2,1)} %noise_ref.1) | copy-start | bytes 393220
  118.4 5.0 %collective-permute-start.10 = (bf16[32,2176]{1,0:T(8,128)(2,1)S(1)}, bf16[32,2176]{1,0:T(8,128)(2,1)S(1)}, u32[]{:S(2)}, u32[]{:S(2)}) collective-permute-start(bf16[32,2176]{1,0:T(8,128)(2,1)S(1)} %get-tuple-element.54), channel_id=1, source_target_pairs={{0,2},{1,3},{2,0},{3,1},{4,6},{5,7},{6,4},{7,5},{8,10},{9,11},{10,... | collective-permute-start | bytes 417800 | tf_op jit(solution)/shard_map/ppermute | solution.py:27
  118.8 6.3 %collective-permute-start.12 = (bf16[32,2176]{1,0:T(8,128)(2,1)S(1)}, bf16[32,2176]{1,0:T(8,128)(2,1)S(1)}, u32[]{:S(2)}, u32[]{:S(2)}) collective-permute-start(bf16[32,2176]{1,0:T(8,128)(2,1)S(1)} %get-tuple-element.56), channel_id=1, source_target_pairs={{0,18},{1,19},{2,16},{3,17},{4,22},{5,23},{6,20},{7,21},{8,26},{9,... | collective-permute-start | bytes 417800 | tf_op jit(solution)/shard_map/ppermute | solution.py:27
  119.6 7.4 %collective-permute-start.11 = (bf16[32,2176]{1,0:T(8,128)(2,1)S(1)}, bf16[32,2176]{1,0:T(8,128)(2,1)S(1)}, u32[]{:S(2)}, u32[]{:S(2)}) collective-permute-start(bf16[32,2176]{1,0:T(8,128)(2,1)S(1)} %shard_map.95), channel_id=1, source_target_pairs={{0,16},{1,17},{2,18},{3,19},{4,20},{5,21},{6,22},{7,23},{8,24},{9,... | collective-permute-start | bytes 417800 | tf_op jit(solution)/shard_map/ppermute | solution.py:27

commit v7 on v6

--- a/solution.py
+++ b/solution.py
@@ -189,7 +189,7 @@
     ).astype(BF)
 
 
-def target_kernel(place, cost_ref, data_ref, parts_ref, keep_ref, log_ref, send_ref, coupling, sums, lses):
+def target_kernel(place, cost_ref, data_ref, parts_ref, keep_ref, log_ref, far_ref, send_ref, coupling, sums, lses):
     h = place[2]
     col_pot = col_potential(ITERS - 1, parts_ref)
     score, peak = row_stats(cost_ref, col_pot, 1.0 / epsilon_of(ITERS - 1))
@@ -209,8 +209,9 @@
     for k in range(4):
         keep_ref[k] = sums[h ^ (2 * k)]
         log_ref[k] = lses[h ^ (2 * k)]
-        send_ref[k, :, 0:latent] = sums[h ^ (2 * k + 1)].astype(BF)
-        send_ref[k, :, latent : latent + 128] = packed_log(lses[h ^ (2 * k + 1)])
+        out = far_ref if k == 2 else send_ref.at[min(k, 2)]
+        out[:, 0:latent] = sums[h ^ (2 * k + 1)].astype(BF)
+        out[:, latent : latent + 128] = packed_log(lses[h ^ (2 * k + 1)])
 
 
 def read_log(ref_value):
@@ -220,11 +221,9 @@
 def pair_parts(keep_ref, log_ref, got_ref, k):
     latent = keep_ref.shape[2]
     first = log_ref[k]
-    second = jnp.broadcast_to(read_log(got_ref[k, :, latent : latent + 128]), first.shape)
+    second = jnp.broadcast_to(read_log(got_ref[:, latent : latent + 128]), first.shape)
     total = join_lse([first, second])
-    mixed = keep_ref[k] * jnp.exp(first - total)[:, 0:1] + got_ref[k, :, 0:latent].astype(
-        F32
-    ) * jnp.exp(second - total)[:, 0:1]
+    mixed = keep_ref[k] * jnp.exp(first - total)[:, 0:1] + got_ref[:, 0:latent].astype(F32) * jnp.exp(second - total)[:, 0:1]
     return mixed, total
 
 
@@ -240,9 +239,9 @@
 
 
 def pair_kernel(keep_ref, log_ref, got_ref, own_ref, own_log_ref, s1, s3):
-    own_ref[...], own_log_ref[...] = pair_parts(keep_ref, log_ref, got_ref, 0)
-    pair_send(keep_ref, log_ref, got_ref, 1, s1)
-    pair_send(keep_ref, log_ref, got_ref, 3, s3)
+    own_ref[...], own_log_ref[...] = pair_parts(keep_ref, log_ref, got_ref.at[0], 0)
+    pair_send(keep_ref, log_ref, got_ref.at[1], 1, s1)
+    pair_send(keep_ref, log_ref, got_ref.at[2], 3, s3)
 
 
 def spread_kernel(value_ref, out_ref, sems):
@@ -407,12 +406,13 @@
                 inputs=2,
                 nbytes=1024 * 1024,
             )(cost, col_parts)
-    keep, log, send = vmem_call(
+    keep, log, first, send = vmem_call(
         target_kernel,
         (
             shape((4, rows, latent)),
             shape((4, rows, 128)),
-            shape((4, rows, latent + 128), BF),
+            shape((rows, latent + 128), BF),
+            shape((3, rows, latent + 128), BF),
         ),
         scratch=[
             pltpu.VMEM((8 * rows, 16 * rows), BF),
@@ -424,9 +424,9 @@
         flops=flops,
         nbytes=6 * 1024 * 1024,
     )(place, cost, data_all, col_parts)
-    got = swap(send, CORE)
+    got_far, got = swap(first, CORE), swap(send, CORE)
     message = shape((rows, latent + 128), BF)
-    far_send = vmem_call(far_kernel, message, inputs=3, nbytes=1024 * 1024)(keep, log, got)
+    far_send = vmem_call(far_kernel, message, inputs=3, nbytes=1024 * 1024)(keep, log, got_far)
     far_send, keep = together(far_send, keep)
     own, own_log, *sends = vmem_call(
         pair_kernel,

time: 140 us -> 140 us (level)
    ppermute x13 -> x14, waiting for transfers between devices: 20.8 us -> 21.5 us  [swap(): return lax.ppermute(value, BOTH, [(i, i ^ mask) for i in range(128)])]
    ppermute x13 -> x14, starting transfers between devices: 17.1 us -> 17.3 us  [swap(): return lax.ppermute(value, BOTH, [(i, i ^ mask) for i in range(128)])]
  transfers between devices with their start and end apart: 15 -> 16, of which waited for: 10 -> 10; matrix products, arithmetic and copies ran while one was open for 3% -> 3% of each run, Pallas kernels for 2% -> 2%
where the time goes in v7:
time: 140 us; the launch traced here: 139 us
  blocking collectives  51.7 us (37%)
  waiting for transfers between devices  29.8 us (21%)
  starting transfers between devices  28.6 us (20%)
  Pallas kernels  22.5 us (16%)
  other arithmetic  3.09 us (2%)
  local copies, waits for them, and re-layouts  2 us (1%)
    all_to_all x5, blocking collectives, exchange(): lax.all_to_all(value, BOTH, 0, 0, axis_index_groups=groups_by(mask), tile...  51.7 us
    ppermute x14, waiting for transfers between devices, swap(): return lax.ppermute(value, BOTH, [(i, i ^ mask) for i in range(128)])  21.5 us
    ppermute x14, starting transfers between devices, swap(): return lax.ppermute(value, BOTH, [(i, i ^ mask) for i in range(128)])  17.3 us
    all_to_all x2, starting transfers between devices, exchange(): lax.all_to_all(value, BOTH, 0, 0, axis_index_groups=groups_by(mask), tile...  11.3 us
    pallas_call x1, Pallas kernels, local(): pl.pallas_call(qkv_kernel, out_shape=(shape((own * patch_count, columns),...  11.3 us
    all_to_all x2, waiting for transfers between devices, exchange(): lax.all_to_all(value, BOTH, 0, 0, axis_index_groups=groups_by(mask), tile...  8.31 us
  transfers between devices with their start and end apart: 16, of which 10 were waited for; matrix products, arithmetic and copies ran while one was open for 3% of the time, Pallas kernels for 2%

profile of v7, /device:TPU:1, one launch (start us, length us, event | category | flops | bytes accessed | tf_op | source)
XLA Modules:
  0.0 139.2 jit_solution(18363930338117308520)
XLA Ops:
  0.6 2.5 %shard_map.86 = bf16[16,32,2048]{2,1,0:T(8,128)(2,1)} custom-call(bf16[32,2048]{1,0:T(8,128)(2,1)} %value_ref.1), custom_call_target="tpu_custom_call" | custom-call | tf_op jit(solution)/shard_map/pallas_call | solution.py:355
  3.2 7.8 %all-to-all-start = ((bf16[16,32,2048]{2,1,0:T(8,128)(2,1)}), bf16[16,32,2048]{2,1,0:T(8,128)(2,1)}, u32[]{:S(2)}, u32[]{:S(2)}) async-start(bf16[16,32,2048]{2,1,0:T(8,128)(2,1)} %shard_map.86), calls=%async_computation | async-start | bytes 4194304 | tf_op jit(solution)/shard_map/all_to_all | solution.py:38
  11.0 1.0 collective-permute-start
  12.0 0.1 fusion.4
  12.1 0.6 fusion
  12.7 0.2 collective-permute-done
  13.0 3.8 %collective-permute-start.3 = (bf16[2,32,2048]{2,1,0:T(8,128)(2,1)S(1)}, bf16[2,32,2048]{2,1,0:T(8,128)(2,1)S(1)}, u32[]{:S(2)}, u32[]{:S(2)}) collective-permute-start(bf16[2,32,2048]{2,1,0:T(8,128)(2,1)S(1)} %pad_maximum_fusion.3.a), channel_id=1, source_target_pairs={{0,18},{1,19},{2,16},{3,17},{4,22},{5,23},{6,20},{7,21},{8,26},{9,... | collective-permute-start | bytes 786440 | tf_op jit(solution)/shard_map/ppermute | solution.py:27
  16.8 0.7 collective-permute-start.1
  17.7 0.7 pad_maximum_fusion.4
  18.4 10.5 %collective-permute-done.3.d = bf16[2,32,2048]{2,1,0:T(8,128)(2,1)S(1)} collective-permute-done((bf16[2,32,2048]{2,1,0:T(8,128)(2,1)S(1)}, bf16[2,32,2048]{2,1,0:T(8,128)(2,1)S(1)}, u32[]{:S(2)}, u32[]{:S(2)}) %collective-permute-start.3) | collective-permute-done | bytes 262176 | tf_op jit(solution)/shard_map/ppermute | solution.py:27
  29.0 0.4 collective-permute-done.1.b
  29.4 0.7 copy-done.1
  30.1 0.9 copy-done.2
  31.0 0.9 shard_map.87
  31.9 7.0 %all-to-all-done.data_ref = bf16[16,32,2048]{2,1,0:T(8,128)(2,1)} async-done(((bf16[16,32,2048]{2,1,0:T(8,128)(2,1)}), bf16[16,32,2048]{2,1,0:T(8,128)(2,1)}, u32[]{:S(2)}, u32[]{:S(2)}) %all-to-all-start) | async-done | bytes 2097184 | tf_op jit(solution)/shard_map/all_to_all | solution.py:38
  38.9 2.7 %shard_map.88 = (f32[256,512]{1,0:T(8,128)S(1)}, f32[8,8,128]{2,1,0:T(8,128)S(1)}) custom-call(bf16[16,32,2048]{2,1,0:T(8,128)(2,1)} %all-to-all-done.data_ref, bf16[8,32,2048]{2,1,0:T(8,128)(2,1)S(1)} %get-tuple-element.33.noise_ref, f32[256,128]{1,0:T(8,128)S(1)} %get-tuple-element.34.square_ref), custom_call_target="tpu_custom_call" | custom-call | flops 536870912 | bytes 4194304 | tf_op jit(solution)/shard_map/pallas_call | solution.py:371
  41.6 3.5 %collective-permute-start.4 = (bf16[192,384]{1,0:T(8,128)(2,1)S(1)}, bf16[192,384]{1,0:T(8,128)(2,1)S(1)}, u32[]{:S(2)}, u32[]{:S(2)}) collective-permute-start(bf16[192,384]{1,0:T(8,128)(2,1)S(1)} %copy-done.8), channel_id=1, source_target_pairs={{0,1},{1,0},{2,3},{3,2},{4,5},{5,4},{6,7},{7,6},{8,9},{9,8},{10,11... | collective-permute-start | bytes 442376 | tf_op jit(solution)/shard_map/ppermute | solution.py:27
  45.1 9.9 %all_to_all.35.parts_ref = f32[8,8,128]{2,1,0:T(8,128)S(1)} all-to-all(f32[8,8,128]{2,1,0:T(8,128)S(1)} %get-tuple-element.38), channel_id=1, replica_groups={{0,1,2,3,16,17,18,19},{4,5,6,7,20,21,22,23},{8,9,10,11,24,25,26,27},{12..., dimensions={0} | all-to-all | bytes 65536 | tf_op jit(solution)/shard_map/all_to_all | solution.py:38
  55.1 0.9 shard_map.89
  56.0 0.4 collective-permute-start.5
  56.4 3.5 %all-to-all-start.2 = ((f32[16,8,128]{2,1,0:T(8,128)}), f32[16,8,128]{2,1,0:T(8,128)S(1)}, u32[]{:S(2)}, u32[]{:S(2)}) async-start(f32[16,8,128]{2,1,0:T(8,128)} %shard_map.89), calls=%async_computation.2 | async-start | bytes 131072 | tf_op jit(solution)/shard_map/all_to_all | solution.py:38
  59.9 4.1 %collective-permute-done.5 = bf16[192,768]{1,0:T(8,128)(2,1)} collective-permute-done((bf16[192,768]{1,0:T(8,128)(2,1)S(1)}, bf16[192,768]{1,0:T(8,128)(2,1)}, u32[]{:S(2)}, u32[]{:S(2)}) %collective-permute-start.5) | collective-permute-done | bytes 294944 | tf_op jit(solution)/shard_map/ppermute | solution.py:27
  64.0 1.0 pad_maximum_fusion.refs_3_
  65.0 1.3 all-to-all-done.2.parts_ref
  66.3 0.3 shard_map.90
  66.6 1.0 collective-permute-start.7
  67.7 10.6 %all_to_all.36.parts_ref = f32[8,8,128]{2,1,0:T(8,128)S(1)} all-to-all(f32[8,8,128]{2,1,0:T(8,128)S(1)} %shard_map.90), channel_id=1, replica_groups={{0,1,2,3,16,17,18,19},{4,5,6,7,20,21,22,23},{8,9,10,11,24,25,26,27},{12..., dimensions={0} | all-to-all | bytes 65536 | tf_op jit(solution)/shard_map/all_to_all | solution.py:38
  78.2 0.3 shard_map.91
  78.5 11.4 %all_to_all.37.parts_ref = f32[16,8,128]{2,1,0:T(8,128)S(1)} all-to-all(f32[16,8,128]{2,1,0:T(8,128)S(1)} %shard_map.91), channel_id=1, replica_groups={{0,4,8,12,32,36,40,44,64,68,72,76,96,100,104,108},{1,5,9,13,33,37,41,45..., dimensions={0} | all-to-all | bytes 131072 | tf_op jit(solution)/shard_map/all_to_all | solution.py:38
  90.0 0.3 shard_map.92
  90.3 1.2 collective-permute-start.8
  91.5 9.9 %all_to_all.38.parts_ref = f32[8,8,128]{2,1,0:T(8,128)S(1)} all-to-all(f32[8,8,128]{2,1,0:T(8,128)S(1)} %shard_map.92), channel_id=1, replica_groups={{0,1,2,3,16,17,18,19},{4,5,6,7,20,21,22,23},{8,9,10,11,24,25,26,27},{12..., dimensions={0} | all-to-all | bytes 65536 | tf_op jit(solution)/shard_map/all_to_all | solution.py:38
  101.3 0.3 shard_map.93
  101.6 9.9 %all_to_all.39.parts_ref = f32[16,8,128]{2,1,0:T(8,128)S(1)} all-to-all(f32[16,8,128]{2,1,0:T(8,128)S(1)} %shard_map.93), channel_id=1, replica_groups={{0,4,8,12,32,36,40,44,64,68,72,76,96,100,104,108},{1,5,9,13,33,37,41,45..., dimensions={0} | all-to-all | bytes 131072 | tf_op jit(solution)/shard_map/all_to_all | solution.py:38
  111.5 2.6 %shard_map.94 = (f32[4,32,2048]{2,1,0:T(8,128)S(1)}, f32[4,32,128]{2,1,0:T(8,128)S(1)}, bf16[32,2176]{1,0:T(8,128)(2,1)S(1)}, bf16[3,32,2176]{2,1,0:T(8,128)(2,1)S(1)}) custom-call(s32[4]{0:T(128)S(1)} %pad_add_fusion.place, f32[256,512]{1,0:T(8,128)S(1)} %get-tuple-element.35.cost_ref, bf16[16,32,2048]{2,1,0:T(8,128)(2,1)} %all-to-all-done.data_ref, ...), custom_call_target="tpu_custom_call" | custom-call | flops 536870912 | bytes 6291456 | tf_op jit(solution)/shard_map/pallas_call | solution.py:409
  114.2 2.1 %collective-permute-start.10 = (bf16[3,32,2176]{2,1,0:T(8,128)(2,1)S(1)}, bf16[3,32,2176]{2,1,0:T(8,128)(2,1)S(1)}, u32[]{:S(2)}, u32[]{:S(2)}) collective-permute-start(bf16[3,32,2176]{2,1,0:T(8,128)(2,1)S(1)} %get-tuple-element.53), channel_id=1, source_target_pairs={{0,1},{1,0},{2,3},{3,2},{4,5},{5,4},{6,7},{7,6},{8,9},{9,8},{10,11... | collective-permute-start | bytes 1253384 | tf_op jit(solution)/shard_map/ppermute | solution.py:27
  116.3 0.1 collective-permute-start.9
  116.6 1.3 collective-permute-done.9.got_ref
  117.9 0.2 shard_map.95
  118.2 0.9 collective-permute-start.12
  119.0 0.3 shard_map.96
  119.4 0.7 collective-permute-start.11
  120.1 1.8 %collective-permute-start.13 = (bf16[32,2176]{1,0:T(8,128)(2,1)S(1)}, bf16[32,2176]{1,0:T(8,128)(2,1)S(1)}, u32[]{:S(2)}, u32[]{:S(2)}) collective-permute-start(bf16[32,2176]{1,0:T(8,128)(2,1)S(1)} %get-tuple-element.58), channel_id=1, source_target_pairs={{0,18},{1,19},{2,16},{3,17},{4,22},{5,23},{6,20},{7,21},{8,26},{9,... | collective-permute-start | bytes 417800 | tf_op jit(solution)/shard_map/ppermute | solution.py:27
  121.9 1.1 maximum_maximum_fusion.table_ref
  123.1 1.5 %collective-permute-done.12.refs_1_ = bf16[32,2176]{1,0:T(8,128)(2,1)S(1)} collective-permute-done((bf16[32,2176]{1,0:T(8,128)(2,1)S(1)}, bf16[32,2176]{1,0:T(8,128)(2,1)S(1)}, u32[]{:S(2)}, u32[]{:S(2)}) %collective-permute-start.12) | collective-permute-done | bytes 139296 | tf_op jit(solution)/shard_map/ppermute | solution.py:27
  124.6 1.5 %collective-permute-done.11.refs_0_ = bf16[32,2176]{1,0:T(8,128)(2,1)S(1)} collective-permute-done((bf16[32,2176]{1,0:T(8,128)(2,1)S(1)}, bf16[32,2176]{1,0:T(8,128)(2,1)S(1)}, u32[]{:S(2)}, u32[]{:S(2)}) %collective-permute-start.11) | collective-permute-done | bytes 139296 | tf_op jit(solution)/shard_map/ppermute | solution.py:27
  126.1 1.9 %collective-permute-done.13.refs_2_ = bf16[32,2176]{1,0:T(8,128)(2,1)S(1)} collective-permute-done((bf16[32,2176]{1,0:T(8,128)(2,1)S(1)}, bf16[32,2176]{1,0:T(8,128)(2,1)S(1)}, u32[]{:S(2)}, u32[]{:S(2)}) %collective-permute-start.13) | collective-permute-done | bytes 139296 | tf_op jit(solution)/shard_map/ppermute | solution.py:27
  128.0 11.3 %shard_map.97 = (bf16[1024,6144]{1,0:T(8,128)(2,1)}, bf16[32,2048]{1,0:T(8,128)(2,1)}) custom-call(s32[4]{0:T(128)S(1)} %pad_add_fusion.place, f32[32,2048]{1,0:T(8,128)S(1)} %get-tuple-element.54.own_ref, f32[32,128]{1,0:T(8,128)S(1)} %get-tuple-element.55.log_ref, bf16[32,2048]{1,0:T(8,128)(2,1)S(1)} %copy-done.4, s32[32,1]{1,0:T(8,128)S(1)} %copy.9.time_ref, ...), custom_call_target="tpu_custom_call" | custom-call | flops 2415919104 | bytes 16777216 | tf_op jit(solution)/shard_map/pallas_call | solution.py:458
  (49 shorter events, 0.5 us)
Async XLA Ops:
  0.6 11.5 %copy-start = (bf16[2048,384]{1,0:T(8,128)(2,1)S(1)}, bf16[2048,384]{1,0:T(8,128)(2,1)}, u32[]{:S(2)}) copy-start(bf16[2048,384]{1,0:T(8,128)(2,1)} %param.13) | copy-start | bytes 4718596
  3.1 7.8 %copy-start.3 = (bf16[32,2048]{1,0:T(8,128)(2,1)S(1)}, bf16[32,2048]{1,0:T(8,128)(2,1)}, u32[]{:S(2)}) copy-start(bf16[32,2048]{1,0:T(8,128)(2,1)} %noise_ref.1) | copy-start | bytes 393220
  3.1 8.9 %copy-start.5 = (bf16[64,2048]{1,0:T(8,128)(2,1)S(1)}, bf16[64,2048]{1,0:T(8,128)(2,1)}, u32[]{:S(2)}) copy-start(bf16[64,2048]{1,0:T(8,128)(2,1)} %param.10) | copy-start | bytes 786436
  3.1 8.9 %copy-start.9 = (bf16[32,2048]{1,0:T(8,128)(2,1)S(1)}, bf16[32,2048]{1,0:T(8,128)(2,1)}, u32[]{:S(2)}) copy-start(bf16[32,2048]{1,0:T(8,128)(2,1)} %param.11) | copy-start | bytes 393220
  3.1 8.9 %copy-start.11 = (f32[2048]{0:T(1024)S(1)}, f32[2048]{0:T(1024)}, u32[]{:S(2)}) copy-start(f32[2048]{0:T(1024)} %param.12) | copy-start | bytes 24580
  3.2 35.7 %all-to-all-start = ((bf16[16,32,2048]{2,1,0:T(8,128)(2,1)}), bf16[16,32,2048]{2,1,0:T(8,128)(2,1)}, u32[]{:S(2)}, u32[]{:S(2)}) async-start(bf16[16,32,2048]{2,1,0:T(8,128)(2,1)} %shard_map.86), calls=%async_computation | async-start | bytes 4194304 | tf_op jit(solution)/shard_map/all_to_all | solution.py:38
  11.0 2.0 %collective-permute-start = (bf16[32,2048]{1,0:T(8,128)(2,1)S(1)}, bf16[32,2048]{1,0:T(8,128)(2,1)S(1)}, u32[]{:S(2)}, u32[]{:S(2)}) collective-permute-start(bf16[32,2048]{1,0:T(8,128)(2,1)S(1)} %copy-done.3), channel_id=1, source_target_pairs={{0,1},{1,0},{2,3},{3,2},{4,5},{5,4},{6,7},{7,6},{8,9},{9,8},{10,11... | collective-permute-start | bytes 393224 | tf_op jit(solution)/shard_map/ppermute | solution.py:27
  13.0 15.9 %collective-permute-start.3 = (bf16[2,32,2048]{2,1,0:T(8,128)(2,1)S(1)}, bf16[2,32,2048]{2,1,0:T(8,128)(2,1)S(1)}, u32[]{:S(2)}, u32[]{:S(2)}) collective-permute-start(bf16[2,32,2048]{2,1,0:T(8,128)(2,1)S(1)} %pad_maximum_fusion.3.a), channel_id=1, source_target_pairs={{0,18},{1,19},{2,16},{3,17},{4,22},{5,23},{6,20},{7,21},{8,26},{9,... | collective-permute-start | bytes 786440 | tf_op jit(solution)/shard_map/ppermute | solution.py:27
  16.8 12.1 %collective-permute-start.2 = (bf16[2,32,2048]{2,1,0:T(8,128)(2,1)S(1)}, bf16[2,32,2048]{2,1,0:T(8,128)(2,1)S(1)}, u32[]{:S(2)}, u32[]{:S(2)}) collective-permute-start(bf16[2,32,2048]{2,1,0:T(8,128)(2,1)S(1)} %pad_maximum_fusion.3.a), channel_id=1, source_target_pairs={{0,16},{1,17},{2,18},{3,19},{4,20},{5,21},{6,22},{7,23},{8,24},{9,... | collective-permute-start | bytes 786440 | tf_op jit(solution)/shard_map/ppermute | solution.py:27
  16.8 12.5 %collective-permute-start.1 = (bf16[2,32,2048]{2,1,0:T(8,128)(2,1)S(1)}, bf16[2,32,2048]{2,1,0:T(8,128)(2,1)S(1)}, u32[]{:S(2)}, u32[]{:S(2)}) collective-permute-start(bf16[2,32,2048]{2,1,0:T(8,128)(2,1)S(1)} %pad_maximum_fusion.3.a), channel_id=1, source_target_pairs={{0,2},{1,3},{2,0},{3,1},{4,6},{5,7},{6,4},{7,5},{8,10},{9,11},{10,... | collective-permute-start | bytes 786440 | tf_op jit(solution)/shard_map/ppermute | solution.py:27
  29.3 0.7 copy-start.1
  30.1 0.9 copy-start.2
  38.9 2.7 %copy-start.8 = (bf16[192,384]{1,0:T(8,128)(2,1)S(1)}, bf16[192,384]{1,0:T(8,128)(2,1)}, u32[]{:S(2)}) copy-start(bf16[192,384]{1,0:T(8,128)(2,1)} %pad_maximum_fusion.4) | copy-start | bytes 442372
  41.6 14.4 %collective-permute-start.4 = (bf16[192,384]{1,0:T(8,128)(2,1)S(1)}, bf16[192,384]{1,0:T(8,128)(2,1)S(1)}, u32[]{:S(2)}, u32[]{:S(2)}) collective-permute-start(bf16[192,384]{1,0:T(8,128)(2,1)S(1)} %copy-done.8), channel_id=1, source_target_pairs={{0,1},{1,0},{2,3},{3,2},{4,5},{5,4},{6,7},{7,6},{8,9},{9,8},{10,11... | collective-permute-start | bytes 442376 | tf_op jit(solution)/shard_map/ppermute | solution.py:27
  56.0 8.0 %collective-permute-start.5 = (bf16[192,768]{1,0:T(8,128)(2,1)S(1)}, bf16[192,768]{1,0:T(8,128)(2,1)}, u32[]{:S(2)}, u32[]{:S(2)}) collective-permute-start(bf16[192,768]{1,0:T(8,128)(2,1)S(1)} %pad_maximum_fusion.2), channel_id=1, source_target_pairs={{0,2},{1,3},{2,0},{3,1},{4,6},{5,7},{6,4},{7,5},{8,10},{9,11},{10,... | collective-permute-start | bytes 884744 | tf_op jit(solution)/shard_map/ppermute | solution.py:27
  56.4 10.0 %all-to-all-start.2 = ((f32[16,8,128]{2,1,0:T(8,128)}), f32[16,8,128]{2,1,0:T(8,128)S(1)}, u32[]{:S(2)}, u32[]{:S(2)}) async-start(f32[16,8,128]{2,1,0:T(8,128)} %shard_map.89), calls=%async_computation.2 | async-start | bytes 131072 | tf_op jit(solution)/shard_map/all_to_all | solution.py:38
  65.0 49.1 %copy-start.7 = (bf16[192,1536]{1,0:T(8,128)(2,1)}, bf16[192,1536]{1,0:T(8,128)(2,1)S(1)}, u32[]{:S(2)}) copy-start(bf16[192,1536]{1,0:T(8,128)(2,1)S(1)} %pad_maximum_fusion.refs_3_) | copy-start | bytes 1769476
  66.6 23.3 %collective-permute-start.7 = (bf16[192,1536]{1,0:T(8,128)(2,1)S(1)}, bf16[192,1536]{1,0:T(8,128)(2,1)S(1)}, u32[]{:S(2)}, u32[]{:S(2)}) collective-permute-start(bf16[192,1536]{1,0:T(8,128)(2,1)S(1)} %pad_maximum_fusion.refs_3_), channel_id=1, source_target_pairs={{0,12},{1,13},{2,14},{3,15},{4,8},{5,9},{6,10},{7,11},{8,4},{9,5},... | collective-permute-start | bytes 1769480 | tf_op jit(solution)/shard_map/ppermute | solution.py:27
  67.7 22.3 %collective-permute-start.6 = (bf16[192,1536]{1,0:T(8,128)(2,1)S(1)}, bf16[192,1536]{1,0:T(8,128)(2,1)S(1)}, u32[]{:S(2)}, u32[]{:S(2)}) collective-permute-start(bf16[192,1536]{1,0:T(8,128)(2,1)S(1)} %pad_maximum_fusion.refs_3_), channel_id=1, source_target_pairs={{0,4},{1,5},{2,6},{3,7},{4,0},{5,1},{6,2},{7,3},{8,12},{9,13},{10,... | collective-permute-start | bytes 1769480 | tf_op jit(solution)/shard_map/ppermute | solution.py:27
  90.0 21.6 %copy-start.13 = (bf16[192,1536]{1,0:T(8,128)(2,1)}, bf16[192,1536]{1,0:T(8,128)(2,1)S(1)}, u32[]{:S(2)}) copy-start(bf16[192,1536]{1,0:T(8,128)(2,1)S(1)} %collective-permute-done.7.refs_6_) | copy-start | bytes 1769476
  90.0 21.6 %copy-start.14 = (bf16[192,1536]{1,0:T(8,128)(2,1)}, bf16[192,1536]{1,0:T(8,128)(2,1)S(1)}, u32[]{:S(2)}) copy-start(bf16[192,1536]{1,0:T(8,128)(2,1)S(1)} %collective-permute-done.6.refs_4_) | copy-start | bytes 1769476
  90.3 21.3 %collective-permute-start.8 = (bf16[192,1536]{1,0:T(8,128)(2,1)S(1)}, bf16[192,1536]{1,0:T(8,128)(2,1)}, u32[]{:S(2)}, u32[]{:S(2)}) collective-permute-start(bf16[192,1536]{1,0:T(8,128)(2,1)S(1)} %pad_maximum_fusion.refs_3_), channel_id=1, source_target_pairs={{0,8},{1,9},{2,10},{3,11},{4,12},{5,13},{6,14},{7,15},{8,0},{9,1},... | collective-permute-start | bytes 1769480 | tf_op jit(solution)/shard_map/ppermute | solution.py:27
  114.1 7.7 %copy-start.6 = (bf16[64,2048]{1,0:T(8,128)(2,1)S(1)}, bf16[64,2048]{1,0:T(8,128)(2,1)}, u32[]{:S(2)}) copy-start(bf16[64,2048]{1,0:T(8,128)(2,1)} %param.10) | copy-start | bytes 786436
  114.2 7.7 %copy-start.10 = (bf16[32,2048]{1,0:T(8,128)(2,1)S(1)}, bf16[32,2048]{1,0:T(8,128)(2,1)}, u32[]{:S(2)}) copy-start(bf16[32,2048]{1,0:T(8,128)(2,1)} %param.11) | copy-start | bytes 393220
  114.2 4.9 %collective-permute-start.10 = (bf16[3,32,2176]{2,1,0:T(8,128)(2,1)S(1)}, bf16[3,32,2176]{2,1,0:T(8,128)(2,1)S(1)}, u32[]{:S(2)}, u32[]{:S(2)}) collective-permute-start(bf16[3,32,2176]{2,1,0:T(8,128)(2,1)S(1)} %get-tuple-element.53), channel_id=1, source_target_pairs={{0,1},{1,0},{2,3},{3,2},{4,5},{5,4},{6,7},{7,6},{8,9},{9,8},{10,11... | collective-permute-start | bytes 1253384 | tf_op jit(solution)/shard_map/ppermute | solution.py:27
  116.3 1.6 %collective-permute-start.9 = (bf16[32,2176]{1,0:T(8,128)(2,1)S(1)}, bf16[32,2176]{1,0:T(8,128)(2,1)S(1)}, u32[]{:S(2)}, u32[]{:S(2)}) collective-permute-start(bf16[32,2176]{1,0:T(8,128)(2,1)S(1)} %get-tuple-element.51), channel_id=1, source_target_pairs={{0,1},{1,0},{2,3},{3,2},{4,5},{5,4},{6,7},{7,6},{8,9},{9,8},{10,11... | collective-permute-start | bytes 417800 | tf_op jit(solution)/shard_map/ppermute | solution.py:27
  118.1 4.9 %copy-start.12 = (s32[32]{0:T(128)S(1)}, s32[32]{0:T(128)}, u32[]{:S(2)}) copy-start(s32[32]{0:T(128)} %param.9) | copy-start | bytes 388
  118.1 9.8 %copy-start.4 = (bf16[32,2048]{1,0:T(8,128)(2,1)S(1)}, bf16[32,2048]{1,0:T(8,128)(2,1)}, u32[]{:S(2)}) copy-start(bf16[32,2048]{1,0:T(8,128)(2,1)} %noise_ref.1) | copy-start | bytes 393220
  118.2 6.5 %collective-permute-start.12 = (bf16[32,2176]{1,0:T(8,128)(2,1)S(1)}, bf16[32,2176]{1,0:T(8,128)(2,1)S(1)}, u32[]{:S(2)}, u32[]{:S(2)}) collective-permute-start(bf16[32,2176]{1,0:T(8,128)(2,1)S(1)} %shard_map.95), channel_id=1, source_target_pairs={{0,16},{1,17},{2,18},{3,19},{4,20},{5,21},{6,22},{7,23},{8,24},{9,... | collective-permute-start | bytes 417800 | tf_op jit(solution)/shard_map/ppermute | solution.py:27
  119.4 6.7 %collective-permute-start.11 = (bf16[32,2176]{1,0:T(8,128)(2,1)S(1)}, bf16[32,2176]{1,0:T(8,128)(2,1)S(1)}, u32[]{:S(2)}, u32[]{:S(2)}) collective-permute-start(bf16[32,2176]{1,0:T(8,128)(2,1)S(1)} %get-tuple-element.56), channel_id=1, source_target_pairs={{0,2},{1,3},{2,0},{3,1},{4,6},{5,7},{6,4},{7,5},{8,10},{9,11},{10,... | collective-permute-start | bytes 417800 | tf_op jit(solution)/shard_map/ppermute | solution.py:27
  120.1 7.9 %collective-permute-start.13 = (bf16[32,2176]{1,0:T(8,128)(2,1)S(1)}, bf16[32,2176]{1,0:T(8,128)(2,1)S(1)}, u32[]{:S(2)}, u32[]{:S(2)}) collective-permute-start(bf16[32,2176]{1,0:T(8,128)(2,1)S(1)} %get-tuple-element.58), channel_id=1, source_target_pairs={{0,18},{1,19},{2,16},{3,17},{4,22},{5,23},{6,20},{7,21},{8,26},{9,... | collective-permute-start | bytes 417800 | tf_op jit(solution)/shard_map/ppermute | solution.py:27
